TPU v7x, 32 devices: a whole 2x2x4 slice. The times are simulated.
32 devices in a mesh: slab: 16 (over z, x, core), dp: 2 (over y).
Axes of the slice: x: 2, y: 2, z: 4, core: 2. Of those that a mesh axis runs over, the one named last changes fastest.
Arguments:
- point_feats: float32 [2, 8192, 128], P('dp', 'slab'), may hold values from -6 to 6
- owner_slab: int32 [2, 8192, 1], P('dp', 'slab'), may hold values from 0 to 15; in each aligned block of 512 rows (0 to 511, 512 to 1023, ..., all dimensions but the last counted through in order) at most 64 rows name the same one
- block_slot: int32 [2, 8192], P('dp', 'slab'), may hold values from 0 to 1
- voxel_index: int32 [2, 8192], P('dp', 'slab'), may hold values from 0 to 511
- boundary: int32 [2, 16, 2, 1], P('dp', 'slab'), may hold values from 0 to 1, as said below
- neighbours: int32 [2, 32, 27], P('dp', 'slab'), may hold values from 0 to 4, as said below
- weight_taps: float32 [27, 128, 128], replicated, may hold values from -0.109375 to 0.109375
- cotangent: float32 [2, 16384, 128], P('dp', 'slab'), may hold values from -6 to 6
Outputs:
- activated: float32 [2, 16384, 128], P('dp', 'slab')
- point_grads: float32 [2, 8192, 128], P('dp', 'slab')
- weight_grads: float32 [3456, 128], P('slab')
Inputs may be any that keep to these rules, and one draw needn't show every extreme that they name: `owner_slab`: among the points of one device, no slab is named by more than 64 points, and exactly 64 in some device. `boundary`: each list of one slab holds 1 different block slots. `neighbours`: entry 13 of a block's row is the block's own slot. Entries 0 to 8 name a block of the slab (below 2), one of the 1 block from the slab before (2 to 2), or the zero block 4; entries 18 to 26 a block of the slab, one of the 1 block from the slab after, or the zero block; the others a block of the slab or the zero block.
All inputs are finite; a program needn't handle non-finite values.
Results may differ from a plain program's by a relative error of at most 0.0003.
Values sent between devices are 32-bit elements; how exact they have to be, the bound alone decides.
No kernel may reach another device: no remote copies, remote signals or barrier semaphores. Data moves between devices by JAX's collectives and lax.ppermute only.
A program may use at most 64 MiB of HBM per device.

v0:
```python
import functools
import math

import jax
import jax.numpy as jnp
from jax import lax
from jax.experimental import pallas as pl
from jax.experimental.pallas import tpu as pltpu
from jax.sharding import PartitionSpec as P

C = 128
E = 8
NB = 2
VOX = 512
FACE = E * E
PAD = E + 2
COLS = 9 * C

f32 = jnp.float32
bf16 = jnp.bfloat16
VMEM = pl.BlockSpec(memory_space=pltpu.VMEM)
SMEM = pl.BlockSpec(memory_space=pltpu.SMEM)


def params(mib):
    return pltpu.CompilerParams(vmem_limit_bytes=mib << 20)


def struct(*shape, dtype=f32):
    return jax.ShapeDtypeStruct(shape, dtype)


def mm(a, b, dims=((1,), (0,))):
    return lax.dot_general(a, b, (dims, ((), ())), preferred_element_type=f32)


def split(value):
    high = value.astype(bf16)
    return high, (value - high.astype(f32)).astype(bf16)


def split3(value):
    high = value.astype(bf16)
    rest = value - high.astype(f32)
    middle = rest.astype(bf16)
    return high, middle, (rest - middle.astype(f32)).astype(bf16)


def iota(shape, dim):
    return lax.broadcasted_iota(jnp.int32, shape, dim)


def pack_kernel(slabs, capacity, me_ref, feats, owner, slot, vox, out, dest_out):
    points = feats.shape[0]
    block = capacity + 8
    target = owner[...]
    onehot = iota((slabs, points), 0) == target
    marks = jnp.where(onehot, 1.0, 0.0).astype(bf16)
    earlier = jnp.where(iota((points, points), 0) < iota((points, points), 1), 1.0, 0.0).astype(bf16)
    counts = mm(marks, earlier)
    rank = jnp.sum(jnp.where(onehot, counts, 0.0), axis=0, keepdims=True).astype(jnp.int32)
    place = target * block + rank
    dest_out[...] = jnp.broadcast_to(target * capacity + rank, dest_out.shape)
    chosen = jnp.where(iota((slabs * block, points), 0) == place, 1.0, 0.0).astype(bf16)
    parts = jnp.concatenate(split3(feats[...]), axis=1)
    rows = mm(chosen, parts)
    rows = rows[:, :C] + rows[:, C : 2 * C] + rows[:, 2 * C :]
    out[...] = rows.reshape(slabs, block, C)
    code = slot[...] * VOX + vox[...] + 1
    upper = lax.shift_right_logical(code, 5)
    lower = jnp.bitwise_and(code, 31)
    lane = lax.rem(me_ref[0], C // capacity) * capacity + rank
    lanes = jnp.where(iota((C, points), 0) == lane, 1.0, 0.0).astype(bf16)
    nt = ((1,), (1,))
    high = mm(jnp.where(onehot, upper, 0).astype(f32).astype(bf16), lanes, nt)
    low = mm(jnp.where(onehot, lower, 0).astype(f32).astype(bf16), lanes, nt)
    ids = high * 32.0 + low
    out[:, capacity:, :] = jnp.broadcast_to(ids[:, None, :], (slabs, 8, C))


def weights_kernel(taps, forward, backward):
    for i in range(3):
        for jk in range(9):
            tap = taps[i * 9 + jk]
            high, low = split(tap)
            rows = slice(jk * C, (jk + 1) * C)
            for part in range(2):
                forward[i, part * COLS + jk * C : part * COLS + (jk + 1) * C, :C] = high
                forward[i, part * COLS + jk * C : part * COLS + (jk + 1) * C, C:] = low
            high, low = split(tap.T)
            backward[i * C : (i + 1) * C, rows] = high
            backward[(3 + i) * C : (4 + i) * C, rows] = high
            backward[(6 + i) * C : (7 + i) * C, rows] = low


def codes_of(ids, chunk, group):
    total = ids[chunk * group]
    for t in range(1, group):
        total = total + ids[chunk * group + t]
    return total


def voxel_kernel(capacity, lent, recv, blocks, to_left, to_right, codes_out, hot):
    slabs = recv.shape[0]
    group = C // capacity
    voxels = NB * VOX
    ids = recv[:, capacity:, :]
    rows = recv[:, :capacity, :].reshape(slabs * capacity, C)
    row_parts = jnp.concatenate(split(rows), axis=1)
    numbers = iota((voxels, C), 0).astype(f32) + 1.0
    for chunk in range(slabs // group):
        codes = codes_of(ids, chunk, group)
        codes_out[chunk * 8 : (chunk + 1) * 8, :] = codes
        match = numbers == codes[:1]
        hot[:, chunk * C : (chunk + 1) * C] = jnp.where(match, 1.0, 0.0).astype(bf16)
    sums = mm(hot[...], row_parts)
    blocks[...] = sums[:, :C] + sums[:, C:]
    left = pl.multiple_of(lent[0] * VOX, VOX)
    right = pl.multiple_of(lent[1] * VOX, VOX)
    to_left[...] = blocks[pl.ds(left, FACE), :]
    to_right[...] = blocks[pl.ds(right + VOX - FACE, FACE), :]


def sublane(shape):
    return iota(shape, len(shape) - 2)


def plane_versions(first, center, last):
    three = [jnp.concatenate([first[k], center[k], last[k]], axis=0).reshape(PAD, E, C) for k in range(3)]
    z = sublane((PAD, E, C))
    down = pltpu.roll(jnp.where(z == E - 1, three[0], three[1]), 1, 1)
    up = pltpu.roll(jnp.where(z == 0, three[2], three[1]), E - 1, 1)
    return [v.reshape(PAD * E, C) for v in (down, three[1], up)]


def put_columns(columns, b, p_rows, versions):
    for k in range(3):
        for j in range(3):
            high, low = split(versions[k][E * j : E * j + FACE])
            at = (3 * j + k) * C
            columns[b, p_rows, at : at + C] = high
            columns[b, p_rows, COLS + at : COLS + at + C] = low


def load(source, block, stride, offset, size):
    return source[pl.ds(pl.multiple_of(block * stride + offset, E), size), :]


def build_plane(names, b, i, source, stride, offset, limit):
    def piece(j, k, at, size):
        name = jnp.minimum(names[b, 9 * i + 3 * j + k], limit)
        return load(source, name, stride, offset + at, size)

    first = [piece(0, k, FACE - E, E) for k in range(3)]
    center = [piece(1, k, 0, FACE) for k in range(3)]
    last = [piece(2, k, 0, E) for k in range(3)]
    return plane_versions(first, center, last)


def spread_plane(names, b, i, sums, target, stride, offset, limit):
    z = sublane((PAD, E, C))
    three = [s.reshape(PAD, E, C) for s in sums]
    down = pltpu.roll(three[0], E - 1, 1)
    up = pltpu.roll(three[2], 1, 1)
    zero = jnp.zeros_like(down)
    own = three[1] + jnp.where(z < E - 1, down, zero) + jnp.where(z > 0, up, zero)
    values = [jnp.where(z == E - 1, down, zero), own, jnp.where(z == 0, up, zero)]
    for k in range(3):
        value = values[k].reshape(PAD * E, C)
        for j, at, size, start in ((0, FACE - E, E, 0), (1, 0, FACE, E), (2, 0, E, E + FACE)):
            name = jnp.minimum(names[b, 9 * i + 3 * j + k], limit)
            where = pl.ds(pl.multiple_of(name * stride + offset + at, E), size)
            target[where, :] = target[where, :] + value[start : start + size]


def column_sums(back):
    sums = []
    for k in range(3):
        total = None
        for j in range(3):
            around = [back(3 * j + k)]
            if j > 0:
                around.insert(0, jnp.zeros((E * j, C), f32))
            if j < 2:
                around.append(jnp.zeros((E * (2 - j), C), f32))
            value = jnp.concatenate(around, axis=0)
            total = value if total is None else total + value
        sums.append(total)
    return sums


def forward_kernel(
    names, blocks, from_left, from_right, forward, backward, cotangent,
    activated, grads, columns, edge_left, edge_right,
    visible, faces_low, faces_high, edge_back, low_grads, high_grads,
):
    visible[: NB * VOX] = blocks[...]
    visible[NB * VOX :] = jnp.zeros((VOX, C), f32)
    none = jnp.zeros((FACE, C), f32)
    for b in range(NB):
        faces_low[b * FACE : (b + 1) * FACE] = blocks[(b + 1) * VOX - FACE : (b + 1) * VOX]
        faces_high[b * FACE : (b + 1) * FACE] = blocks[b * VOX : b * VOX + FACE]
    faces_low[2 * FACE : 3 * FACE] = from_left[...]
    faces_low[3 * FACE : 4 * FACE] = none
    faces_low[4 * FACE :] = none
    faces_high[2 * FACE : 3 * FACE] = none
    faces_high[3 * FACE : 4 * FACE] = from_right[...]
    faces_high[4 * FACE :] = none
    low_grads[...] = jnp.zeros_like(low_grads)
    high_grads[...] = jnp.zeros_like(high_grads)
    grads[...] = jnp.zeros_like(grads)
    for b in range(NB):
        put_columns(columns, b, slice(0, FACE), build_plane(names, b, 0, faces_low, FACE, 0, 4))
        put_columns(
            columns, b, slice((PAD - 1) * FACE, PAD * FACE), build_plane(names, b, 2, faces_high, FACE, 0, 4)
        )

        @pl.loop(1, E + 1)
        def _(p):
            planes = build_plane(names, b, 1, visible, VOX, (p - 1) * FACE, 2)
            put_columns(columns, b, pl.ds(pl.multiple_of(p * FACE, FACE), FACE), planes)

        total = None
        for i in range(3):
            term = mm(columns[b, FACE * i : FACE * i + VOX, :], forward[i])
            total = term if total is None else total + term
        pre = total[:, :C] + total[:, C:]
        here = slice(b * VOX, (b + 1) * VOX)
        gate = jax.nn.sigmoid(pre)
        activated[here] = pre * gate
        grad = cotangent[here] * gate * (1.0 + pre * (1.0 - gate))
        high, low = split(grad)
        for i in range(3):
            at = slice(FACE * i, FACE * i + VOX)
            grads[b, at, i * C : (i + 1) * C] = high
            grads[b, at, (3 + i) * C : (4 + i) * C] = low
            grads[b, at, (6 + i) * C : (7 + i) * C] = high
    for i, p, target in ((0, 0, low_grads), (2, PAD - 1, high_grads)):
        here = slice(p * FACE, (p + 1) * FACE)
        for b in range(NB):
            edge_back[b * FACE : (b + 1) * FACE] = sum(
                mm(grads[b, here, part * C : (part + 1) * C], backward[part * C : (part + 1) * C, :])
                for part in (i, 3 + i, 6 + i)
            )
        for b in range(NB):
            sums = column_sums(lambda jk: edge_back[b * FACE : (b + 1) * FACE, jk * C : (jk + 1) * C])
            spread_plane(names, b, i, sums, target, FACE, 0, 4)
    edge_left[...] = low_grads[2 * FACE : 3 * FACE]
    edge_right[...] = high_grads[3 * FACE : 4 * FACE]


def weight_grad_kernel(places, columns, grads, out, total):
    for i in range(3):
        for b in range(NB):
            here = slice(FACE * i, FACE * i + VOX)
            pair = jnp.concatenate(
                [grads[b, here, i * C : (i + 1) * C], grads[b, here, (3 + i) * C : (4 + i) * C]], axis=1
            )
            term = mm(columns[b, here, :], pair, ((0,), (0,)))
            total[...] = term if b == 0 else total[...] + term
        value = total[:COLS, :C] + total[:COLS, C:] + total[COLS:, :C] + total[COLS:, C:]
        for start, stop, to in places:
            low, high = max(start, i * COLS), min(stop, (i + 1) * COLS)
            if low < high:
                out[to + low - start : to + high - start] = value[low - i * COLS : high - i * COLS]


def backward_kernel(names, lent, grads, backward, halo_left, halo_right, blocks_out, back, target):
    target[...] = jnp.zeros_like(target)
    for b in range(NB):
        back[...] = mm(grads[b], backward[...])

        def plane(i, p, offset):
            rows = pl.ds(pl.multiple_of(p * FACE, FACE), FACE)
            sums = column_sums(lambda jk: back[rows, jk * C : (jk + 1) * C])
            spread_plane(names, b, i, sums, target, VOX, offset, 2)

        plane(0, 0, VOX - FACE)
        plane(2, PAD - 1, 0)

        @pl.loop(1, E + 1)
        def _(p):
            plane(1, p, (p - 1) * FACE)

    left = pl.multiple_of(lent[0] * VOX, VOX)
    right = pl.multiple_of(lent[1] * VOX, VOX) + VOX - FACE
    target[pl.ds(left, FACE), :] = target[pl.ds(left, FACE), :] + halo_left[...]
    target[pl.ds(right, FACE), :] = target[pl.ds(right, FACE), :] + halo_right[...]
    blocks_out[...] = target[: NB * VOX]


def gather_kernel(grad_blocks, codes, out):
    parts = jnp.concatenate(split(grad_blocks[...]), axis=1)
    voxels = NB * VOX
    by_row = codes[...].T
    numbers = iota((C, voxels), 1).astype(f32) + 1.0
    for chunk in range(codes.shape[0] // 8):
        match = numbers == by_row[:, chunk * 8 : chunk * 8 + 1]
        rows = mm(jnp.where(match, 1.0, 0.0).astype(bf16), parts)
        out[chunk * C : (chunk + 1) * C] = rows[:, :C] + rows[:, C:]


def unpack_kernel(came_back, dest, out):
    places = dest[...].astype(f32).T[:, :1]
    points, slots = out.shape[0], came_back.shape[0]
    chosen = jnp.where(iota((points, slots), 1).astype(f32) == places, 1.0, 0.0).astype(bf16)
    rows = mm(chosen, jnp.concatenate(split3(came_back[...]), axis=1))
    out[...] = rows[:, :C] + rows[:, C : 2 * C] + rows[:, 2 * C :]


def bit_reversed(number, bits):
    return int(format(number, f"0{bits}b")[::-1], 2)


def per_device(
    point_feats, owner_slab, block_slot, voxel_index, boundary, neighbours, weight_taps, cotangent
):
    slabs = lax.axis_size("slab")
    windows = lax.axis_size("dp")
    points = point_feats.shape[1]
    capacity = 2 * points // slabs
    bits = slabs.bit_length() - 1
    me = lax.axis_index("slab")
    names = neighbours[0]
    lent = boundary.reshape(2)
    voxels = NB * VOX
    chunk = 27 * C // slabs

    send, dest = pl.pallas_call(
        functools.partial(pack_kernel, slabs, capacity),
        out_shape=(struct(slabs, capacity + 8, C), struct(8, points, dtype=jnp.int32)),
        in_specs=[SMEM] + [VMEM] * 4,
        out_specs=(VMEM, VMEM),
        compiler_params=params(32),
        name="pack",
    )(me.reshape(1), point_feats[0], owner_slab.reshape(1, points), block_slot, voxel_index)
    recv = lax.all_to_all(send, "slab", split_axis=0, concat_axis=0, tiled=True)
    forward, backward = pl.pallas_call(
        weights_kernel,
        out_shape=(struct(3, 2 * COLS, 2 * C, dtype=bf16), struct(9 * C, COLS, dtype=bf16)),
        in_specs=[VMEM],
        out_specs=(VMEM, VMEM),
        compiler_params=params(32),
        name="weights",
    )(weight_taps)
    blocks, to_left, to_right, codes = pl.pallas_call(
        functools.partial(voxel_kernel, capacity),
        out_shape=(
            struct(voxels, C), struct(FACE, C), struct(FACE, C), struct(slabs * capacity // C * 8, C)
        ),
        in_specs=[SMEM, VMEM],
        out_specs=(VMEM,) * 4,
        scratch_shapes=[pltpu.VMEM((voxels, slabs * capacity), bf16)],
        compiler_params=params(32),
        name="voxels",
    )(lent, recv)
    up = [(i, (i + 1) % slabs) for i in range(slabs)]
    down = [(j, i) for i, j in up]
    from_left = lax.ppermute(to_right, "slab", up)
    from_right = lax.ppermute(to_left, "slab", down)
    activated, grads, columns, edge_left, edge_right = pl.pallas_call(
        forward_kernel,
        out_shape=(
            struct(voxels, C),
            struct(NB, PAD * FACE, 9 * C, dtype=bf16),
            struct(NB, PAD * FACE, 2 * COLS, dtype=bf16),
            struct(FACE, C),
            struct(FACE, C),
        ),
        in_specs=[SMEM] + [VMEM] * 6,
        out_specs=(VMEM,) * 5,
        scratch_shapes=[
            pltpu.VMEM((3 * VOX, C), f32),
            pltpu.VMEM((5 * FACE, C), f32),
            pltpu.VMEM((5 * FACE, C), f32),
            pltpu.VMEM((NB * FACE, COLS), f32),
            pltpu.VMEM((5 * FACE, C), f32),
            pltpu.VMEM((5 * FACE, C), f32),
        ],
        compiler_params=params(40),
        name="forward",
    )(names, blocks, from_left, from_right, forward, backward, cotangent[0])
    halo_right = lax.ppermute(edge_left, "slab", down)
    halo_left = lax.ppermute(edge_right, "slab", up)

    aligned = chunk % 8 == 0
    places = tuple(
        (c * chunk, (c + 1) * chunk, (bit_reversed(c, bits) if aligned else c) * chunk) for c in range(slabs)
    )
    if not aligned:
        places = ((0, 27 * C, 0),)
    term = pl.pallas_call(
        functools.partial(weight_grad_kernel, places),
        out_shape=struct(27 * C, C),
        in_specs=[VMEM, VMEM],
        out_specs=VMEM,
        scratch_shapes=[pltpu.VMEM((2 * COLS, 2 * C), f32)],
        compiler_params=params(40),
        name="weight_grad",
    )(columns, grads)
    if not aligned:
        order = [bit_reversed(c, bits) for c in range(slabs)]
        term = term.reshape(slabs, chunk, C)[jnp.array(order)].reshape(27 * C, C)
    grad_blocks = pl.pallas_call(
        backward_kernel,
        out_shape=struct(voxels, C),
        in_specs=[SMEM, SMEM] + [VMEM] * 4,
        out_specs=VMEM,
        scratch_shapes=[pltpu.VMEM((PAD * FACE, COLS), f32), pltpu.VMEM((3 * VOX, C), f32)],
        compiler_params=params(40),
        name="backward",
    )(names, lent, grads, backward, halo_left, halo_right)
    back_points = pl.pallas_call(
        gather_kernel,
        out_shape=struct(slabs * capacity, C),
        in_specs=[VMEM, VMEM],
        out_specs=VMEM,
        compiler_params=params(32),
        name="gather",
    )(grad_blocks, codes)
    came_back = lax.all_to_all(
        back_points.reshape(slabs, capacity, C), "slab", split_axis=0, concat_axis=0, tiled=True
    )
    point_grads = pl.pallas_call(
        unpack_kernel,
        out_shape=struct(points, C),
        in_specs=[VMEM, VMEM],
        out_specs=VMEM,
        compiler_params=params(32),
        name="unpack",
    )(came_back.reshape(slabs * capacity, C), dest)

    share = term
    for bit in range(bits):
        side = lax.shift_right_logical(me, bit) & 1
        half = share.shape[0] // 2
        kept = lax.dynamic_slice_in_dim(share, side * half, half, 0)
        sent = lax.dynamic_slice_in_dim(share, (1 - side) * half, half, 0)
        share = kept + lax.ppermute(sent, "slab", [(i, i ^ (1 << bit)) for i in range(slabs)])
    step = 1
    while step < windows:
        share = share + lax.ppermute(share, "dp", [(i, i ^ step) for i in range(windows)])
        step *= 2
    scale = 1.0 / math.sqrt(windows * slabs * voxels)
    return (activated[None], point_grads[None], share * scale)


def solution(mesh):
    return jax.shard_map(
        per_device,
        mesh=mesh,
        in_specs=(
            P("dp", "slab", None),
            P("dp", "slab", None),
            P("dp", "slab"),
            P("dp", "slab"),
            P("dp", "slab", None, None),
            P("dp", "slab", None),
            P(),
            P("dp", "slab", None),
        ),
        out_specs=(P("dp", "slab", None), P("dp", "slab", None), P("slab", None)),
        check_vma=False,
    )
```

profile of v0, /device:TPU:0, one launch (start us, length us, event | category | flops | bytes accessed | tf_op | source)
XLA Modules:
  0.0 136.2 jit_solution(8694899977052756001)
XLA Ops:
  0.7 1.1 copy-done.11
  1.8 0.7 copy-done.16
  2.4 0.7 copy-done.17
  3.1 0.7 copy-done.18
  3.8 1.0 pack.1
  4.8 24.4 %all_to_all.10.recv = f32[16,72,128]{2,1,0:T(8,128)S(1)} all-to-all(f32[16,72,128]{2,1,0:T(8,128)S(1)} %get-tuple-element.16), channel_id=1, replica_groups=mesh['slab'=16,'dp'=2] {'slab'}, dimensions={0} | all-to-all | bytes 1179648 | tf_op jit(solution)/shard_map/all_to_all | solution.py:337
  29.2 0.7 copy-done.19
  29.9 1.5 %voxels.1 = (f32[1024,128]{1,0:T(8,128)S(1)}, f32[64,128]{1,0:T(8,128)S(1)}, f32[64,128]{1,0:T(8,128)S(1)}, f32[64,128]{1,0:T(8,128)S(1)}) custom-call(s32[2]{0:T(128)S(1)} %bitcast.16, f32[16,72,128]{2,1,0:T(8,128)S(1)} %all_to_all.10.recv), custom_call_target="tpu_custom_call" | custom-call | tf_op jit(solution)/shard_map/voxels/pallas_call | solution.py:346
  31.5 0.0 copy-start.9
  31.5 0.8 copy-done.9
  32.3 0.6 copy-done.12
  32.9 0.1 collective-permute-start
  33.0 4.3 %collective-permute-start.1 = (f32[64,128]{1,0:T(8,128)S(1)}, f32[64,128]{1,0:T(8,128)S(1)}, u32[]{:S(2)}, u32[]{:S(2)}) collective-permute-start(f32[64,128]{1,0:T(8,128)S(1)} %get-tuple-element.19), channel_id=1, source_target_pairs={{2,0},{4,2},{6,4},{8,6},{10,8},{12,10},{14,12},{16,14},{18,16},{20... | collective-permute-start | bytes 98312 | tf_op jit(solution)/shard_map/ppermute | solution.py:360
  37.3 0.8 weights.1
  38.1 1.5 %copy-done = bf16[1152,1152]{1,0:T(8,128)(2,1)} copy-done((bf16[1152,1152]{1,0:T(8,128)(2,1)}, bf16[1152,1152]{1,0:T(8,128)(2,1)S(1)}, u32[]{:S(2)}) %copy-start) | copy-done | bytes 2654232
  39.7 1.7 %copy-done.5 = bf16[3,2304,256]{2,1,0:T(8,128)(2,1)} copy-done((bf16[3,2304,256]{2,1,0:T(8,128)(2,1)}, bf16[3,2304,256]{2,1,0:T(8,128)(2,1)S(1)}, u32[]{:S(2)}) %copy-start.5) | copy-done | bytes 3538968
  41.4 1.7 %copy-done.1 = bf16[1152,1152]{1,0:T(8,128)(2,1)S(1)} copy-done((bf16[1152,1152]{1,0:T(8,128)(2,1)S(1)}, bf16[1152,1152]{1,0:T(8,128)(2,1)}, u32[]{:S(2)}) %copy-start.1) | copy-done | bytes 2654232
  43.2 2.0 %copy-done.6 = bf16[3,2304,256]{2,1,0:T(8,128)(2,1)S(1)} copy-done((bf16[3,2304,256]{2,1,0:T(8,128)(2,1)S(1)}, bf16[3,2304,256]{2,1,0:T(8,128)(2,1)}, u32[]{:S(2)}) %copy-start.6) | copy-done | bytes 3538968
  45.2 1.0 copy-done.10
  46.2 0.7 copy-done.14
  46.9 12.5 %forward.1 = (f32[1024,128]{1,0:T(8,128)}, bf16[2,640,1152]{2,1,0:T(8,128)(2,1)S(1)}, bf16[2,640,2304]{2,1,0:T(8,128)(2,1)}, f32[64,128]{1,0:T(8,128)S(1)}, f32[64,128]{1,0:T(8,128)S(1)}) custom-call(s32[2,27]{1,0:T(2,128)S(1)} %bitcast.13, f32[1024,128]{1,0:T(8,128)S(1)} %copy-done.10, f32[64,128]{1,0:T(8,128)S(1)} %collective-permute-done.from_left, ...), custom_call_target="tpu_custom_call" | custom-call | tf_op jit(solution)/shard_map/forward/pallas_call | solution.py:361
  59.4 0.6 copy-done.21
  60.0 0.6 copy-done.23
  60.6 2.7 %copy-done.4 = bf16[2,640,2304]{2,1,0:T(8,128)(2,1)S(1)} copy-done((bf16[2,640,2304]{2,1,0:T(8,128)(2,1)S(1)}, bf16[2,640,2304]{2,1,0:T(8,128)(2,1)}, u32[]{:S(2)}) %copy-start.4) | copy-done | bytes 5898264
  63.3 3.9 %weight_grad.1 = f32[3456,128]{1,0:T(8,128)S(1)} custom-call(bf16[2,640,2304]{2,1,0:T(8,128)(2,1)S(1)} %copy-done.4, bf16[2,640,1152]{2,1,0:T(8,128)(2,1)S(1)} %get-tuple-element.23.grads), custom_call_target="tpu_custom_call" | custom-call | tf_op jit(solution)/shard_map/weight_grad/pallas_call | solution.py:392
  67.2 1.2 copy-done.3
  68.4 1.0 constant_dynamic-slice_fusion.3
  69.4 0.0 copy-start.20
  69.4 2.7 %collective-permute-done.4 = f32[1728,128]{1,0:T(8,128)} collective-permute-done((f32[1728,128]{1,0:T(8,128)}, f32[1728,128]{1,0:T(8,128)}, u32[]{:S(2)}, u32[]{:S(2)}) %collective-permute-start.4) | collective-permute-done | bytes 884768 | tf_op jit(solution)/shard_map/ppermute | solution.py:439
  72.2 1.5 %dynamic-slice_add_fusion = f32[1728,128]{1,0:T(8,128)S(1)} fusion(f32[1728,128]{1,0:T(8,128)} %collective-permute-done.4, f32[3456,128]{1,0:T(8,128)} %copy-done.3, s32[]{:T(128)S(6)} %select_n.24), kind=kLoop, calls=%fused_computation | loop fusion | flops 221184 | bytes 2654212 | tf_op jit(solution)/shard_map/add | solution.py:439
  73.7 0.9 copy-done.25
  74.7 0.1 collective-permute-start.5
  74.8 12.3 %collective-permute-done.5 = f32[864,128]{1,0:T(8,128)} collective-permute-done((f32[864,128]{1,0:T(8,128)S(1)}, f32[864,128]{1,0:T(8,128)}, u32[]{:S(2)}, u32[]{:S(2)}) %collective-permute-start.5) | collective-permute-done | bytes 442400 | tf_op jit(solution)/shard_map/ppermute | solution.py:439
  87.1 1.2 dynamic-slice_add_fusion.1
  88.2 0.7 constant_dynamic-slice_fusion.1
  89.0 4.4 %collective-permute-start.3 = (f32[64,128]{1,0:T(8,128)S(1)}, f32[64,128]{1,0:T(8,128)S(1)}, u32[]{:S(2)}, u32[]{:S(2)}) collective-permute-start(f32[64,128]{1,0:T(8,128)S(1)} %copy-done.22), channel_id=1, source_target_pairs={{2,0},{4,2},{6,4},{8,6},{10,8},{12,10},{14,12},{16,14},{18,16},{20... | collective-permute-start | bytes 98312 | tf_op jit(solution)/shard_map/ppermute | solution.py:383
  93.4 2.6 %collective-permute-done.2.halo_left = f32[64,128]{1,0:T(8,128)S(1)} collective-permute-done((f32[64,128]{1,0:T(8,128)S(1)}, f32[64,128]{1,0:T(8,128)S(1)}, u32[]{:S(2)}, u32[]{:S(2)}) %collective-permute-start.2) | collective-permute-done | bytes 32800 | tf_op jit(solution)/shard_map/ppermute | solution.py:384
  96.1 1.7 %copy-done.2 = bf16[1152,1152]{1,0:T(8,128)(2,1)S(1)} copy-done((bf16[1152,1152]{1,0:T(8,128)(2,1)S(1)}, bf16[1152,1152]{1,0:T(8,128)(2,1)}, u32[]{:S(2)}) %copy-start.2) | copy-done | bytes 2654232
  97.8 6.5 %backward.1.grad_blocks = f32[1024,128]{1,0:T(8,128)S(1)} custom-call(s32[2,27]{1,0:T(2,128)S(1)} %bitcast.14, s32[2]{0:T(128)S(1)} %bitcast.17, bf16[2,640,1152]{2,1,0:T(8,128)(2,1)S(1)} %get-tuple-element.23.grads, bf16[1152,1152]{1,0:T(8,128)(2,1)S(1)} %copy-done.2, f32[64,128]{1,0:T(8,128)S(1)} %collective-permute-done.2.halo_left, ...), custom_call_target="tpu_custom_call" | custom-call | tf_op jit(solution)/shard_map/backward/pallas_call | solution.py:404
  104.3 1.7 %gather.1 = f32[1024,128]{1,0:T(8,128)} custom-call(f32[1024,128]{1,0:T(8,128)S(1)} %backward.1.grad_blocks, f32[64,128]{1,0:T(8,128)S(1)} %copy-done.13), custom_call_target="tpu_custom_call" | custom-call | tf_op jit(solution)/shard_map/gather/pallas_call | solution.py:413
  105.9 4.8 %all-to-all-start.1 = ((f32[16,64,128]{2,1,0:T(8,128)}), f32[16,64,128]{2,1,0:T(8,128)S(1)}, u32[]{:S(2)}, u32[]{:S(2)}) async-start(f32[16,64,128]{2,1,0:T(8,128)} %bitcast.7), calls=%async_computation.1 | async-start | bytes 1048576 | tf_op jit(solution)/shard_map/all_to_all | solution.py:421
  110.7 1.0 dynamic-slice_add_fusion.2
  111.7 2.9 %collective-permute-start.7 = (f32[216,128]{1,0:T(8,128)S(1)}, f32[216,128]{1,0:T(8,128)S(1)}, u32[]{:S(2)}, u32[]{:S(2)}) collective-permute-start(f32[216,128]{1,0:T(8,128)S(1)} %constant_dynamic-slice_fusion), channel_id=1, source_target_pairs={{0,16},{2,18},{4,20},{6,22},{8,24},{10,26},{12,28},{14,30},{16,0},... | collective-permute-start | bytes 331784 | tf_op jit(solution)/shard_map/ppermute | solution.py:439
  114.6 16.1 %collective-permute-done.7 = f32[216,128]{1,0:T(8,128)S(1)} collective-permute-done((f32[216,128]{1,0:T(8,128)S(1)}, f32[216,128]{1,0:T(8,128)S(1)}, u32[]{:S(2)}, u32[]{:S(2)}) %collective-permute-start.7) | collective-permute-done | bytes 110624 | tf_op jit(solution)/shard_map/ppermute | solution.py:439
  130.8 1.6 %collective-permute-start.8 = (f32[216,128]{1,0:T(8,128)S(1)}, f32[216,128]{1,0:T(8,128)S(1)}, u32[]{:S(2)}, u32[]{:S(2)}) collective-permute-start(f32[216,128]{1,0:T(8,128)S(1)} %dynamic-slice_add_fusion.3), channel_id=1, source_target_pairs={{0,1},{1,0},{2,3},{3,2},{4,5},{5,4},{6,7},{7,6},{8,9},{9,8},{10,11... | collective-permute-start | bytes 331784 | tf_op jit(solution)/shard_map/ppermute | solution.py:442
  132.3 1.7 %unpack.1 = f32[512,128]{1,0:T(8,128)} custom-call(f32[1024,128]{1,0:T(8,128)S(1)} %bitcast.10, s32[8,512]{1,0:T(8,128)S(1)} %get-tuple-element.27.dest), custom_call_target="tpu_custom_call" | custom-call | tf_op jit(solution)/shard_map/unpack/pallas_call | solution.py:424
  134.0 1.5 %collective-permute-done.8 = f32[216,128]{1,0:T(8,128)S(1)} collective-permute-done((f32[216,128]{1,0:T(8,128)S(1)}, f32[216,128]{1,0:T(8,128)S(1)}, u32[]{:S(2)}, u32[]{:S(2)}) %collective-permute-start.8) | collective-permute-done | bytes 110624 | tf_op jit(solution)/shard_map/ppermute | solution.py:442
  135.6 0.7 add_multiply_fusion
  (42 shorter events, 0.1 us)
Async XLA Ops:
  0.6 36.7 %copy-start.7 = (f32[27,128,128]{2,1,0:T(8,128)S(1)}, f32[27,128,128]{2,1,0:T(8,128)}, u32[]{:S(2)}) copy-start(f32[27,128,128]{2,1,0:T(8,128)} %taps.1) | copy-start | bytes 5308420
  0.6 40.8 %copy-start.8 = (f32[1,1024,128]{2,1,0:T(8,128)S(1)}, f32[1,1024,128]{2,1,0:T(8,128)}, u32[]{:S(2)}) copy-start(f32[1,1024,128]{2,1,0:T(8,128)} %param.15) | copy-start | bytes 1572868
  0.7 1.1 copy-start.11
  1.8 0.7 copy-start.16
  2.4 0.7 copy-start.17
  3.1 0.7 copy-start.18
  29.2 0.7 copy-start.19
  31.5 0.8 copy-start.9
  32.3 0.6 copy-start.12
  32.9 8.6 %collective-permute-start = (f32[64,128]{1,0:T(8,128)S(1)}, f32[64,128]{1,0:T(8,128)S(1)}, u32[]{:S(2)}, u32[]{:S(2)}) collective-permute-start(f32[64,128]{1,0:T(8,128)S(1)} %get-tuple-element.18), channel_id=1, source_target_pairs={{0,2},{2,4},{4,6},{6,8},{8,10},{10,12},{12,14},{14,16},{16,18},{18... | collective-permute-start | bytes 98312 | tf_op jit(solution)/shard_map/ppermute | solution.py:359
  33.0 8.4 %collective-permute-start.1 = (f32[64,128]{1,0:T(8,128)S(1)}, f32[64,128]{1,0:T(8,128)S(1)}, u32[]{:S(2)}, u32[]{:S(2)}) collective-permute-start(f32[64,128]{1,0:T(8,128)S(1)} %get-tuple-element.19), channel_id=1, source_target_pairs={{2,0},{4,2},{6,4},{8,6},{10,8},{12,10},{14,12},{16,14},{18,16},{20... | collective-permute-start | bytes 98312 | tf_op jit(solution)/shard_map/ppermute | solution.py:360
  38.1 1.6 %copy-start = (bf16[1152,1152]{1,0:T(8,128)(2,1)}, bf16[1152,1152]{1,0:T(8,128)(2,1)S(1)}, u32[]{:S(2)}) copy-start(bf16[1152,1152]{1,0:T(8,128)(2,1)S(1)} %get-tuple-element.21.backward) | copy-start | bytes 7962628
  39.7 1.7 %copy-start.5 = (bf16[3,2304,256]{2,1,0:T(8,128)(2,1)}, bf16[3,2304,256]{2,1,0:T(8,128)(2,1)S(1)}, u32[]{:S(2)}) copy-start(bf16[3,2304,256]{2,1,0:T(8,128)(2,1)S(1)} %get-tuple-element.20.forward) | copy-start | bytes 10616836
  41.4 1.8 %copy-start.1 = (bf16[1152,1152]{1,0:T(8,128)(2,1)S(1)}, bf16[1152,1152]{1,0:T(8,128)(2,1)}, u32[]{:S(2)}) copy-start(bf16[1152,1152]{1,0:T(8,128)(2,1)} %copy-done) | copy-start | bytes 7962628
  43.2 2.0 %copy-start.6 = (bf16[3,2304,256]{2,1,0:T(8,128)(2,1)S(1)}, bf16[3,2304,256]{2,1,0:T(8,128)(2,1)}, u32[]{:S(2)}) copy-start(bf16[3,2304,256]{2,1,0:T(8,128)(2,1)} %copy-done.5) | copy-start | bytes 10616836
  45.2 1.0 copy-start.10
  46.2 0.7 copy-start.14
  59.4 0.6 copy-start.21
  60.0 0.6 copy-start.23
  60.6 2.7 %copy-start.4 = (bf16[2,640,2304]{2,1,0:T(8,128)(2,1)S(1)}, bf16[2,640,2304]{2,1,0:T(8,128)(2,1)}, u32[]{:S(2)}) copy-start(bf16[2,640,2304]{2,1,0:T(8,128)(2,1)} %get-tuple-element.28.columns) | copy-start | bytes 17694724
  67.2 1.2 copy-start.3
  69.4 2.8 %collective-permute-start.4 = (f32[1728,128]{1,0:T(8,128)}, f32[1728,128]{1,0:T(8,128)}, u32[]{:S(2)}, u32[]{:S(2)}) collective-permute-start(f32[1728,128]{1,0:T(8,128)} %constant_dynamic-slice_fusion.3), channel_id=1, source_target_pairs={{0,2},{2,0},{4,6},{6,4},{8,10},{10,8},{12,14},{14,12},{16,18},{18,... | collective-permute-start | bytes 2654216 | tf_op jit(solution)/shard_map/ppermute | solution.py:439
  69.4 19.5 %copy-start.24 = (f32[64,128]{1,0:T(8,128)S(1)}, f32[64,128]{1,0:T(8,128)}, u32[]{:S(2)}) copy-start(f32[64,128]{1,0:T(8,128)} %copy-done.23) | copy-start | bytes 98308
  69.4 19.5 %copy-start.22 = (f32[64,128]{1,0:T(8,128)S(1)}, f32[64,128]{1,0:T(8,128)}, u32[]{:S(2)}) copy-start(f32[64,128]{1,0:T(8,128)} %copy-done.21) | copy-start | bytes 98308
  69.4 26.6 %copy-start.15 = (s32[1,2,27]{2,1,0:T(2,128)S(1)}, s32[1,2,27]{2,1,0:T(2,128)}, u32[]{:S(2)}) copy-start(s32[1,2,27]{2,1,0:T(2,128)} %param.13) | copy-start | bytes 652
  69.4 26.6 %copy-start.20 = (s32[1,1,2,1]{2,3,1,0:T(1,128)S(1)}, s32[1,1,2,1]{2,3,1,0:T(1,128)}, u32[]{:S(2)}) copy-start(s32[1,1,2,1]{2,3,1,0:T(1,128)} %param.12) | copy-start | bytes 28
  73.7 0.9 copy-start.25
  74.7 12.4 %collective-permute-start.5 = (f32[864,128]{1,0:T(8,128)S(1)}, f32[864,128]{1,0:T(8,128)}, u32[]{:S(2)}, u32[]{:S(2)}) collective-permute-start(f32[864,128]{1,0:T(8,128)S(1)} %constant_dynamic-slice_fusion.2), channel_id=1, source_target_pairs={{0,4},{2,6},{4,0},{6,2},{8,12},{10,14},{12,8},{14,10},{16,20},{18,... | collective-permute-start | bytes 1327112 | tf_op jit(solution)/shard_map/ppermute | solution.py:439
  89.0 21.8 %collective-permute-start.6 = (f32[432,128]{1,0:T(8,128)}, f32[432,128]{1,0:T(8,128)}, u32[]{:S(2)}, u32[]{:S(2)}) collective-permute-start(f32[432,128]{1,0:T(8,128)} %constant_dynamic-slice_fusion.1), channel_id=1, source_target_pairs={{0,8},{2,10},{4,12},{6,14},{8,0},{10,2},{12,4},{14,6},{16,24},{18,... | collective-permute-start | bytes 663560 | tf_op jit(solution)/shard_map/ppermute | solution.py:439
  89.0 7.1 %collective-permute-start.2 = (f32[64,128]{1,0:T(8,128)S(1)}, f32[64,128]{1,0:T(8,128)S(1)}, u32[]{:S(2)}, u32[]{:S(2)}) collective-permute-start(f32[64,128]{1,0:T(8,128)S(1)} %copy-done.24), channel_id=1, source_target_pairs={{0,2},{2,4},{4,6},{6,8},{8,10},{10,12},{12,14},{14,16},{16,18},{18... | collective-permute-start | bytes 98312 | tf_op jit(solution)/shard_map/ppermute | solution.py:384
  89.0 7.1 %collective-permute-start.3 = (f32[64,128]{1,0:T(8,128)S(1)}, f32[64,128]{1,0:T(8,128)S(1)}, u32[]{:S(2)}, u32[]{:S(2)}) collective-permute-start(f32[64,128]{1,0:T(8,128)S(1)} %copy-done.22), channel_id=1, source_target_pairs={{2,0},{4,2},{6,4},{8,6},{10,8},{12,10},{14,12},{16,14},{18,16},{20... | collective-permute-start | bytes 98312 | tf_op jit(solution)/shard_map/ppermute | solution.py:383
  96.0 1.8 %copy-start.2 = (bf16[1152,1152]{1,0:T(8,128)(2,1)S(1)}, bf16[1152,1152]{1,0:T(8,128)(2,1)}, u32[]{:S(2)}) copy-start(bf16[1152,1152]{1,0:T(8,128)(2,1)} %copy-done) | copy-start | bytes 7962628
  97.8 6.5 %copy-start.13 = (f32[64,128]{1,0:T(8,128)S(1)}, f32[64,128]{1,0:T(8,128)}, u32[]{:S(2)}) copy-start(f32[64,128]{1,0:T(8,128)} %copy-done.12) | copy-start | bytes 98308
  105.9 26.4 %all-to-all-start.1 = ((f32[16,64,128]{2,1,0:T(8,128)}), f32[16,64,128]{2,1,0:T(8,128)S(1)}, u32[]{:S(2)}, u32[]{:S(2)}) async-start(f32[16,64,128]{2,1,0:T(8,128)} %bitcast.7), calls=%async_computation.1 | async-start | bytes 1048576 | tf_op jit(solution)/shard_map/all_to_all | solution.py:421
  111.7 19.0 %collective-permute-start.7 = (f32[216,128]{1,0:T(8,128)S(1)}, f32[216,128]{1,0:T(8,128)S(1)}, u32[]{:S(2)}, u32[]{:S(2)}) collective-permute-start(f32[216,128]{1,0:T(8,128)S(1)} %constant_dynamic-slice_fusion), channel_id=1, source_target_pairs={{0,16},{2,18},{4,20},{6,22},{8,24},{10,26},{12,28},{14,30},{16,0},... | collective-permute-start | bytes 331784 | tf_op jit(solution)/shard_map/ppermute | solution.py:439
  130.8 4.8 %collective-permute-start.8 = (f32[216,128]{1,0:T(8,128)S(1)}, f32[216,128]{1,0:T(8,128)S(1)}, u32[]{:S(2)}, u32[]{:S(2)}) collective-permute-start(f32[216,128]{1,0:T(8,128)S(1)} %dynamic-slice_add_fusion.3), channel_id=1, source_target_pairs={{0,1},{1,0},{2,3},{3,2},{4,5},{5,4},{6,7},{7,6},{8,9},{9,8},{10,11... | collective-permute-start | bytes 331784 | tf_op jit(solution)/shard_map/ppermute | solution.py:442
where the time goes:
time: 137 us; the launch traced here: 136 us
  waiting for transfers between devices  35.3 us (26%)
  Pallas kernels  29.5 us (22%)
  blocking collectives  24.4 us (18%)
  local copies, waits for them, and re-layouts  23.5 us (17%)
  starting transfers between devices  18.2 us (13%)
  other arithmetic  4.36 us (3%)
    ppermute x4, waiting for transfers between devices, per_device(): lax.ppermute(sent, 'slab', [(i, i ^ 1 << bit) for i in range(slabs)])  31.2 us
    all_to_all x1, blocking collectives, per_device(): recv = lax.all_to_all(send, 'slab', split_axis=0, concat_axis=0, tiled=True)  24.4 us
    unnamed x52, local copies, waits for them, and re-layouts  21.7 us
    pallas_call x1, Pallas kernels, per_device(): pl.pallas_call(forward_kernel, out_shape=(struct(voxels, C), struct(NB, P...  12.5 us
    pallas_call x1, Pallas kernels, per_device(): pl.pallas_call(backward_kernel, out_shape=struct(voxels, C), in_specs=[SM...  6.45 us
    all_to_all x1, starting transfers between devices, per_device(): lax.all_to_all(back_points.reshape(slabs, capacity, C), 'slab', split_axi...  4.78 us
    ppermute x1, starting transfers between devices, per_device(): halo_right = lax.ppermute(edge_left, 'slab', down)  4.43 us
    ppermute x1, starting transfers between devices, per_device(): from_right = lax.ppermute(to_left, 'slab', down)  4.33 us
  transfers between devices with their start and end apart: 10, of which 5 were waited for; matrix products, arithmetic and copies ran while one was open for 1% of the time, Pallas kernels for 8%

commit v1 on v0

v1 whole, which is shorter than its diff:
```python
import functools
import math

import jax
import jax.numpy as jnp
from jax import lax
from jax.experimental import pallas as pl
from jax.experimental.pallas import tpu as pltpu
from jax.sharding import PartitionSpec as P

C = 128
E = 8
NB = 2
VOX = 512
FACE = E * E
PAD = E + 2
COLS = 9 * C

f32 = jnp.float32
bf16 = jnp.bfloat16
VMEM = pl.BlockSpec(memory_space=pltpu.VMEM)
SMEM = pl.BlockSpec(memory_space=pltpu.SMEM)
ANY = pl.BlockSpec(memory_space=pl.ANY)
HBM = pl.BlockSpec(memory_space=pltpu.HBM)


def params(mib):
    return pltpu.CompilerParams(vmem_limit_bytes=mib << 20)


def cost(microseconds):
    return pl.CostEstimate(flops=int(microseconds * 1e9), bytes_accessed=0, transcendentals=0)


def struct(*shape, dtype=f32):
    return jax.ShapeDtypeStruct(shape, dtype)


def mm(a, b, dims=((1,), (0,))):
    return lax.dot_general(a, b, (dims, ((), ())), preferred_element_type=f32)


def split(value):
    high = value.astype(bf16)
    return high, (value - high.astype(f32)).astype(bf16)


def split3(value):
    high = value.astype(bf16)
    rest = value - high.astype(f32)
    middle = rest.astype(bf16)
    return high, middle, (rest - middle.astype(f32)).astype(bf16)


def iota(shape, dim):
    return lax.broadcasted_iota(jnp.int32, shape, dim)


def pack_kernel(
    slabs, capacity, me_ref, feats_in, owner_in, slot_in, vox_in, out, dest_out, feats, owner, slot, vox, sems
):
    copies = [
        pltpu.make_async_copy(source, target, sems.at[n])
        for n, (source, target) in enumerate(
            ((owner_in, owner), (slot_in, slot), (vox_in, vox), (feats_in, feats))
        )
    ]
    for copy in copies:
        copy.start()
    points = feats.shape[0]
    block = capacity + 8
    for copy in copies[:3]:
        copy.wait()
    target = owner[...]
    onehot = iota((slabs, points), 0) == target
    marks = jnp.where(onehot, 1.0, 0.0).astype(bf16)
    earlier = jnp.where(iota((points, points), 0) < iota((points, points), 1), 1.0, 0.0).astype(bf16)
    counts = mm(marks, earlier)
    rank = jnp.sum(jnp.where(onehot, counts, 0.0), axis=0, keepdims=True).astype(jnp.int32)
    place = target * block + rank
    dest_out[...] = jnp.broadcast_to(target * capacity + rank, dest_out.shape)
    chosen = jnp.where(iota((slabs * block, points), 0) == place, 1.0, 0.0).astype(bf16)
    copies[3].wait()
    parts = jnp.concatenate(split3(feats[...]), axis=1)
    rows = mm(chosen, parts)
    rows = rows[:, :C] + rows[:, C : 2 * C] + rows[:, 2 * C :]
    out[...] = rows.reshape(slabs, block, C)
    code = slot[...] * VOX + vox[...] + 1
    upper = lax.shift_right_logical(code, 5)
    lower = jnp.bitwise_and(code, 31)
    lane = lax.rem(me_ref[0], C // capacity) * capacity + rank
    lanes = jnp.where(iota((C, points), 0) == lane, 1.0, 0.0).astype(bf16)
    nt = ((1,), (1,))
    high = mm(jnp.where(onehot, upper, 0).astype(f32).astype(bf16), lanes, nt)
    low = mm(jnp.where(onehot, lower, 0).astype(f32).astype(bf16), lanes, nt)
    ids = high * 32.0 + low
    out[:, capacity:, :] = jnp.broadcast_to(ids[:, None, :], (slabs, 8, C))


def weights_kernel(taps, backward):
    for i in range(3):
        for jk in range(9):
            high, low = split(taps[i * 9 + jk].T)
            columns = slice(jk * C, (jk + 1) * C)
            backward[i * C : (i + 1) * C, columns] = high
            backward[(3 + i) * C : (4 + i) * C, columns] = high
            backward[(6 + i) * C : (7 + i) * C, columns] = low


def split_taps(taps, forward):
    for i in range(3):
        for jk in range(9):
            high, low = split(taps[i * 9 + jk])
            for part in range(2):
                rows = slice(part * COLS + jk * C, part * COLS + (jk + 1) * C)
                forward[i, rows, :C] = high
                forward[i, rows, C:] = low


def codes_of(ids, chunk, group):
    total = ids[chunk * group]
    for t in range(1, group):
        total = total + ids[chunk * group + t]
    return total


def received(recv, capacity):
    slabs = recv.shape[0]
    rows = recv[:, :capacity, :].reshape(slabs * capacity, C)
    return recv[:, capacity:, :], jnp.concatenate(split(rows), axis=1)


def faces_kernel(capacity, lent, me, recv, to_core, to_far):
    group = C // capacity
    ids, row_parts = received(recv, capacity)
    row = iota((2 * FACE, C), 0)
    number = jnp.where(row < FACE, lent[0] * VOX + row, lent[1] * VOX + VOX - 2 * FACE + row)
    number = number.astype(f32) + 1.0
    hot = []
    for chunk in range(recv.shape[0] // group):
        match = number == codes_of(ids, chunk, group)[:1]
        hot.append(jnp.where(match, 1.0, 0.0).astype(bf16))
    sums = mm(jnp.concatenate(hot, axis=1), row_parts)
    sums = sums[:, :C] + sums[:, C:]
    even = jnp.bitwise_and(me[0], 1) == 0
    to_core[...] = jnp.where(even, sums[FACE:], sums[:FACE])
    to_far[...] = jnp.where(even, sums[:FACE], sums[FACE:])


def sublane(shape):
    return iota(shape, len(shape) - 2)


def plane_versions(first, center, last):
    three = [jnp.concatenate([first[k], center[k], last[k]], axis=0).reshape(PAD, E, C) for k in range(3)]
    z = sublane((PAD, E, C))
    down = pltpu.roll(jnp.where(z == E - 1, three[0], three[1]), 1, 1)
    up = pltpu.roll(jnp.where(z == 0, three[2], three[1]), E - 1, 1)
    return [v.reshape(PAD * E, C) for v in (down, three[1], up)]


def put_columns(columns, at_first, rows, versions):
    for k in range(3):
        for j in range(3):
            high, low = split(versions[k][E * j : E * j + FACE])
            at = (3 * j + k) * C
            columns[at_first, rows, at : at + C] = high
            columns[at_first, rows, COLS + at : COLS + at + C] = low


def load(source, block, stride, offset, size):
    return source[pl.ds(pl.multiple_of(block * stride + offset, E), size), :]


def build_plane(names, b, i, source, stride, offset, limit):
    def piece(j, k, at, size):
        name = jnp.minimum(names[b, 9 * i + 3 * j + k], limit)
        return load(source, name, stride, offset + at, size)

    first = [piece(0, k, FACE - E, E) for k in range(3)]
    center = [piece(1, k, 0, FACE) for k in range(3)]
    last = [piece(2, k, 0, E) for k in range(3)]
    return plane_versions(first, center, last)


def spread_plane(names, b, i, sums, target, stride, offset, limit):
    z = sublane((PAD, E, C))
    three = [s.reshape(PAD, E, C) for s in sums]
    down = pltpu.roll(three[0], E - 1, 1)
    up = pltpu.roll(three[2], 1, 1)
    zero = jnp.zeros_like(down)
    own = three[1] + jnp.where(z < E - 1, down, zero) + jnp.where(z > 0, up, zero)
    values = [jnp.where(z == E - 1, down, zero), own, jnp.where(z == 0, up, zero)]
    for k in range(3):
        value = values[k].reshape(PAD * E, C)
        for j, at, size, start in ((0, FACE - E, E, 0), (1, 0, FACE, E), (2, 0, E, E + FACE)):
            name = jnp.minimum(names[b, 9 * i + 3 * j + k], limit)
            where = pl.ds(pl.multiple_of(name * stride + offset + at, E), size)
            target[where, :] = target[where, :] + value[start : start + size]


def column_sums(back):
    sums = []
    for k in range(3):
        total = None
        for j in range(3):
            around = [back(3 * j + k)]
            if j > 0:
                around.insert(0, jnp.zeros((E * j, C), f32))
            if j < 2:
                around.append(jnp.zeros((E * (2 - j), C), f32))
            value = jnp.concatenate(around, axis=0)
            total = value if total is None else total + value
        sums.append(total)
    return sums


def interior_kernel(
    capacity, names_in, recv, taps_in,
    before, columns, faces, codes_out, forward,
    names, visible, hot, taps, sems,
):
    names_copy = pltpu.make_async_copy(names_in, names, sems.at[0])
    taps_copy = pltpu.make_async_copy(taps_in, taps, sems.at[1])
    names_copy.start()
    taps_copy.start()
    voxels = NB * VOX
    group = C // capacity
    ids, row_parts = received(recv, capacity)
    numbers = iota((voxels, C), 0).astype(f32) + 1.0
    for chunk in range(recv.shape[0] // group):
        codes = codes_of(ids, chunk, group)
        codes_out[chunk * 8 : (chunk + 1) * 8, :] = codes
        match = numbers == codes[:1]
        hot[:, chunk * C : (chunk + 1) * C] = jnp.where(match, 1.0, 0.0).astype(bf16)
    sums = mm(hot[...], row_parts)
    visible[:voxels] = sums[:, :C] + sums[:, C:]
    visible[voxels:] = jnp.zeros((VOX, C), f32)
    for b in range(NB):
        faces[b * FACE : (b + 1) * FACE] = visible[(b + 1) * VOX - FACE : (b + 1) * VOX]
        faces[(NB + b) * FACE : (NB + b + 1) * FACE] = visible[b * VOX : b * VOX + FACE]
    names_copy.wait()
    for b in range(NB):

        @pl.loop(1, E + 1)
        def _(p):
            planes = build_plane(names, b, 1, visible, VOX, (p - 1) * FACE, 2)
            put_columns(columns, b, pl.ds(pl.multiple_of((p - 1) * FACE, FACE), FACE), planes)

    taps_copy.wait()
    split_taps(taps, forward)
    for b in range(NB):
        start = b * VOX
        total = mm(columns[b], forward[1])
        before[start : start + VOX] = total[:, :C] + total[:, C:]
        total = mm(columns[b, : VOX - FACE, :], forward[0])
        here = slice(start + FACE, start + VOX)
        before[here] = before[here] + total[:, :C] + total[:, C:]
        total = mm(columns[b, FACE:, :], forward[2])
        here = slice(start, start + VOX - FACE)
        before[here] = before[here] + total[:, :C] + total[:, C:]


def finish_kernel(
    names_in, me, before, faces, from_core, from_far, forward, backward_in, cotangent_in,
    activated, grads, outer, to_core, to_far,
    names, faces_low, faces_high, pre, cotangent, backward, edge_back, low_grads, high_grads, sems,
):
    copies = [
        pltpu.make_async_copy(names_in, names, sems.at[0]),
        pltpu.make_async_copy(cotangent_in, cotangent, sems.at[1]),
    ]
    for n, i in enumerate((0, 2)):
        for part in (0, 3, 6):
            rows = pl.ds((i + part) * C, C)
            copies.append(
                pltpu.make_async_copy(
                    backward_in.at[rows], backward.at[pl.ds((3 * n + part // 3) * C, C)], sems.at[len(copies)]
                )
            )
    for copy in copies:
        copy.start()
    even = jnp.bitwise_and(me[0], 1) == 0
    none = jnp.zeros((FACE, C), f32)
    faces_low[: 2 * FACE] = faces[: 2 * FACE]
    faces_low[2 * FACE : 3 * FACE] = jnp.where(even, from_far[...], from_core[...])
    faces_low[3 * FACE : 4 * FACE] = none
    faces_low[4 * FACE :] = none
    faces_high[: 2 * FACE] = faces[2 * FACE :]
    faces_high[2 * FACE : 3 * FACE] = none
    faces_high[3 * FACE : 4 * FACE] = jnp.where(even, from_core[...], from_far[...])
    faces_high[4 * FACE :] = none
    low_grads[...] = jnp.zeros_like(low_grads)
    high_grads[...] = jnp.zeros_like(high_grads)
    pre[...] = before[...]
    copies[0].wait()
    for n, (i, x, source) in enumerate(((0, 0, faces_low), (2, E - 1, faces_high))):
        for b in range(NB):
            rows = slice(b * FACE, (b + 1) * FACE)
            put_columns(outer, n, rows, build_plane(names, b, i, source, FACE, 0, 4))
        total = mm(outer[n], forward[i])
        total = total[:, :C] + total[:, C:]
        for b in range(NB):
            here = slice(b * VOX + x * FACE, b * VOX + (x + 1) * FACE)
            pre[here] = pre[here] + total[b * FACE : (b + 1) * FACE]
    value = pre[...]
    gate = jax.nn.sigmoid(value)
    activated[...] = value * gate
    copies[1].wait()
    high, low = split(cotangent[...] * gate * (1.0 + value * (1.0 - gate)))
    grads[:, :C] = high
    grads[:, C:] = low
    for copy in copies[2:]:
        copy.wait()
    for n, (i, x, target) in enumerate(((0, 0, low_grads), (2, E - 1, high_grads))):
        both = jnp.concatenate([grads[b * VOX + x * FACE : b * VOX + (x + 1) * FACE, :] for b in range(NB)], axis=0)
        three = jnp.concatenate([both, both[:, :C]], axis=1)
        edge_back[...] = mm(three, backward[3 * n * C : 3 * (n + 1) * C, :])
        for b in range(NB):
            sums = column_sums(lambda jk: edge_back[b * FACE : (b + 1) * FACE, jk * C : (jk + 1) * C])
            spread_plane(names, b, i, sums, target, FACE, 0, 4)
    left = low_grads[2 * FACE : 3 * FACE]
    right = high_grads[3 * FACE : 4 * FACE]
    to_core[...] = jnp.where(even, right, left)
    to_far[...] = jnp.where(even, left, right)


def weight_grad_kernel(chunk, starts, me, columns, outer, grads, kept, sent, total, ordered):
    tn = ((0,), (0,))
    for i in range(3):
        low, high = max(i - 1, 0), E + min(i - 1, 0)
        for b in range(NB):
            x = b * E + 1 - i
            term = mm(columns[b, low * FACE : high * FACE, :], grads[(x + low) * FACE : (x + high) * FACE, :], tn)
            total[...] = term if b == 0 else total[...] + term
        if i != 1:
            x = 0 if i == 0 else E - 1
            faces = [grads[(b * E + x) * FACE : (b * E + x + 1) * FACE, :] for b in range(NB)]
            total[...] = total[...] + mm(outer[i // 2], jnp.concatenate(faces, axis=0), tn)
        value = total[:COLS, :C] + total[:COLS, C:] + total[COLS:, :C] + total[COLS:, C:]
        ordered[i * COLS : (i + 1) * COLS] = value
    first = jnp.bitwise_and(me[0], 1) == 0
    for n, to in enumerate(starts):
        even = ordered[2 * n * chunk : (2 * n + 1) * chunk]
        odd = ordered[(2 * n + 1) * chunk : (2 * n + 2) * chunk]
        kept[to : to + chunk] = jnp.where(first, even, odd)
        sent[to : to + chunk] = jnp.where(first, odd, even)


def halve(kept, arrived, side):
    half = kept.shape[0] // 2

    def part(which):
        return lax.dynamic_slice_in_dim(kept, which * half, half, 0) + lax.dynamic_slice_in_dim(
            arrived, which * half, half, 0
        )

    return part(side), part(1 - side)


def backward_kernel(names_in, grads, backward_in, blocks_out, names, backward, shifted, back, target, sems):
    copies = [
        pltpu.make_async_copy(names_in, names, sems.at[0]),
        pltpu.make_async_copy(backward_in, backward, sems.at[1]),
    ]
    for copy in copies:
        copy.start()
    target[...] = jnp.zeros_like(target)
    shifted[...] = jnp.zeros_like(shifted)
    copies[0].wait()
    for b in range(NB):
        rows = slice(b * VOX, (b + 1) * VOX)
        for i in range(3):
            at = slice(FACE * i, FACE * i + VOX)
            shifted[at, i * C : (i + 1) * C] = grads[rows, :C]
            shifted[at, (3 + i) * C : (4 + i) * C] = grads[rows, C:]
            shifted[at, (6 + i) * C : (7 + i) * C] = grads[rows, :C]
        if b == 0:
            copies[1].wait()
        back[...] = mm(shifted[...], backward[...])

        def plane(i, p, offset):
            rows = pl.ds(pl.multiple_of(p * FACE, FACE), FACE)
            sums = column_sums(lambda jk: back[rows, jk * C : (jk + 1) * C])
            spread_plane(names, b, i, sums, target, VOX, offset, 2)

        plane(0, 0, VOX - FACE)
        plane(2, PAD - 1, 0)

        @pl.loop(1, E + 1)
        def _(p):
            plane(1, p, (p - 1) * FACE)

    blocks_out[...] = target[: NB * VOX]


def gather_kernel(lent, me, grad_blocks, halo_core, halo_far, codes, out, target):
    voxels = NB * VOX
    even = jnp.bitwise_and(me[0], 1) == 0
    target[...] = grad_blocks[...]
    left = pl.ds(pl.multiple_of(lent[0] * VOX, VOX), FACE)
    right = pl.ds(pl.multiple_of(lent[1] * VOX, VOX) + VOX - FACE, FACE)
    target[left, :] = target[left, :] + jnp.where(even, halo_far[...], halo_core[...])
    target[right, :] = target[right, :] + jnp.where(even, halo_core[...], halo_far[...])
    parts = jnp.concatenate(split(target[...]), axis=1)
    by_row = codes[...].T
    numbers = iota((C, voxels), 1).astype(f32) + 1.0
    for chunk in range(codes.shape[0] // 8):
        match = numbers == by_row[:, chunk * 8 : chunk * 8 + 1]
        rows = mm(jnp.where(match, 1.0, 0.0).astype(bf16), parts)
        out[chunk * C : (chunk + 1) * C] = rows[:, :C] + rows[:, C:]


def unpack_kernel(came_back, dest, out):
    places = dest[...].astype(f32).T[:, :1]
    points, slots = out.shape[0], came_back.shape[0]
    chosen = jnp.where(iota((points, slots), 1).astype(f32) == places, 1.0, 0.0).astype(bf16)
    rows = mm(chosen, jnp.concatenate(split3(came_back[...]), axis=1))
    out[...] = rows[:, :C] + rows[:, C : 2 * C] + rows[:, 2 * C :]


def bit_reversed(number, bits):
    return int(format(number, f"0{bits}b")[::-1], 2)


def per_device(
    point_feats, owner_slab, block_slot, voxel_index, boundary, neighbours, weight_taps, cotangent
):
    slabs = lax.axis_size("slab")
    windows = lax.axis_size("dp")
    points = point_feats.shape[1]
    capacity = 2 * points // slabs
    bits = slabs.bit_length() - 1
    me = lax.axis_index("slab")
    names = neighbours[0]
    lent = boundary.reshape(2)
    voxels = NB * VOX
    chunk = 27 * C // slabs

    send, dest = pl.pallas_call(
        functools.partial(pack_kernel, slabs, capacity),
        out_shape=(struct(slabs, capacity + 8, C), struct(8, points, dtype=jnp.int32)),
        in_specs=[SMEM] + [HBM] * 4,
        out_specs=(VMEM, VMEM),
        scratch_shapes=[pltpu.VMEM((points, C), f32)]
        + [pltpu.VMEM((1, points), jnp.int32)] * 3
        + [pltpu.SemaphoreType.DMA((4,))],
        compiler_params=params(60),
        name="pack",
        cost_estimate=cost(2),
    )(me.reshape(1), point_feats[0], owner_slab.reshape(1, points), block_slot, voxel_index)
    send, weight_taps = lax.optimization_barrier((send, weight_taps))
    recv = lax.all_to_all(send, "slab", split_axis=0, concat_axis=0, tiled=True)
    backward = pl.pallas_call(
        weights_kernel,
        out_shape=struct(9 * C, COLS, dtype=bf16),
        in_specs=[VMEM],
        out_specs=VMEM,
        compiler_params=params(4),
        name="weights",
        cost_estimate=cost(0.6),
    )(weight_taps)
    recv, backward = lax.optimization_barrier((recv, backward))
    to_core, to_far = pl.pallas_call(
        functools.partial(faces_kernel, capacity),
        out_shape=(struct(FACE, C), struct(FACE, C)),
        in_specs=[SMEM, SMEM, VMEM],
        out_specs=(VMEM,) * 2,
        compiler_params=params(8),
        name="faces",
        cost_estimate=cost(0.8),
    )(lent, me.reshape(1), recv)
    core_pairs = [(i, i ^ 1) for i in range(slabs)]
    far_pairs = [(i, (i - 1 if i % 2 == 0 else i + 1) % slabs) for i in range(slabs)]
    from_core = lax.ppermute(to_core, "slab", core_pairs)
    from_far = lax.ppermute(to_far, "slab", far_pairs)
    before, columns, faces, codes, forward = pl.pallas_call(
        functools.partial(interior_kernel, capacity),
        out_shape=(
            struct(voxels, C),
            struct(NB, VOX, 2 * COLS, dtype=bf16),
            struct(2 * NB * FACE, C),
            struct(slabs * capacity // C * 8, C),
            struct(3, 2 * COLS, 2 * C, dtype=bf16),
        ),
        in_specs=[ANY, VMEM, ANY],
        out_specs=(VMEM,) * 5,
        scratch_shapes=[
            pltpu.SMEM((NB, 27), jnp.int32),
            pltpu.VMEM((3 * VOX, C), f32),
            pltpu.VMEM((voxels, slabs * capacity), bf16),
            pltpu.VMEM(weight_taps.shape, f32),
            pltpu.SemaphoreType.DMA((2,)),
        ],
        compiler_params=params(16),
        name="interior",
        cost_estimate=cost(6.5),
    )(names, recv, weight_taps)
    activated, grads, outer, edge_core, edge_far = pl.pallas_call(
        finish_kernel,
        out_shape=(
            struct(voxels, C),
            struct(voxels, 2 * C, dtype=bf16),
            struct(2, NB * FACE, 2 * COLS, dtype=bf16),
            struct(FACE, C),
            struct(FACE, C),
        ),
        in_specs=[ANY, SMEM] + [VMEM] * 5 + [ANY] * 2,
        out_specs=(VMEM,) * 5,
        scratch_shapes=[
            pltpu.SMEM((NB, 27), jnp.int32),
            pltpu.VMEM((5 * FACE, C), f32),
            pltpu.VMEM((5 * FACE, C), f32),
            pltpu.VMEM((voxels, C), f32),
            pltpu.VMEM((voxels, C), f32),
            pltpu.VMEM((6 * C, COLS), bf16),
            pltpu.VMEM((NB * FACE, COLS), f32),
            pltpu.VMEM((5 * FACE, C), f32),
            pltpu.VMEM((5 * FACE, C), f32),
            pltpu.SemaphoreType.DMA((8,)),
        ],
        compiler_params=params(14),
        name="finish",
        cost_estimate=cost(2.8),
    )(names, me.reshape(1), before, faces, from_core, from_far, forward, backward, cotangent[0])
    starts = tuple(bit_reversed(n, bits - 1) * chunk for n in range(slabs // 2))
    kept, sent = pl.pallas_call(
        functools.partial(weight_grad_kernel, chunk, starts),
        out_shape=(struct(27 * C // 2, C),) * 2,
        in_specs=[SMEM] + [VMEM] * 3,
        out_specs=(VMEM, VMEM),
        scratch_shapes=[pltpu.VMEM((2 * COLS, 2 * C), f32), pltpu.VMEM((27 * C, C), f32)],
        compiler_params=params(14),
        name="weight_grad",
        cost_estimate=cost(4),
    )(me.reshape(1), columns, outer, grads)
    def swapped(part, axis, bit):
        size = lax.axis_size(axis)
        return lax.ppermute(part, axis, [(i, i ^ (1 << bit)) for i in range(size)])

    def side(bit):
        return lax.shift_right_logical(me, bit) & 1

    halo_far = lax.ppermute(edge_far, "slab", far_pairs)
    halo_core = lax.ppermute(edge_core, "slab", core_pairs)
    sent, halo_far, halo_core = lax.optimization_barrier((sent, halo_far, halo_core))
    kept, sent = halve(kept, swapped(sent, "slab", 0), side(1))
    sent, grads = lax.optimization_barrier((sent, grads))
    arrived = swapped(sent, "slab", 1)
    grad_blocks = pl.pallas_call(
        backward_kernel,
        out_shape=struct(voxels, C),
        in_specs=[ANY, VMEM, ANY],
        out_specs=VMEM,
        scratch_shapes=[
            pltpu.SMEM((NB, 27), jnp.int32),
            pltpu.VMEM((9 * C, COLS), bf16),
            pltpu.VMEM((PAD * FACE, 9 * C), bf16),
            pltpu.VMEM((PAD * FACE, COLS), f32),
            pltpu.VMEM((3 * VOX, C), f32),
            pltpu.SemaphoreType.DMA((2,)),
        ],
        compiler_params=params(14),
        name="backward",
        cost_estimate=cost(6.5),
    )(names, grads, backward)
    arrived, grad_blocks = lax.optimization_barrier((arrived, grad_blocks))
    kept, sent = halve(kept, arrived, side(2))
    sent, grad_blocks = lax.optimization_barrier((sent, grad_blocks))
    arrived = swapped(sent, "slab", 2)
    back_points = pl.pallas_call(
        gather_kernel,
        out_shape=struct(slabs * capacity, C),
        in_specs=[SMEM] * 2 + [VMEM] * 4,
        out_specs=VMEM,
        scratch_shapes=[pltpu.VMEM((voxels, C), f32)],
        compiler_params=params(12),
        name="gather",
        cost_estimate=cost(2.2),
    )(lent, me.reshape(1), grad_blocks, halo_core, halo_far, codes)
    came_back = lax.all_to_all(
        back_points.reshape(slabs, capacity, C), "slab", split_axis=0, concat_axis=0, tiled=True
    )
    point_grads = pl.pallas_call(
        unpack_kernel,
        out_shape=struct(points, C),
        in_specs=[VMEM, VMEM],
        out_specs=VMEM,
        compiler_params=params(12),
        name="unpack",
        cost_estimate=cost(1.7),
    )(came_back.reshape(slabs * capacity, C), dest)

    for bit in range(2, bits):
        if bit > 2:
            kept, sent = halve(kept, arrived, side(bit))
            arrived = swapped(sent, "slab", bit)
        if bit == bits - 2:
            kept = kept + arrived
            step = 0
            while (1 << step) < windows:
                arrived = swapped(kept, "dp", step)
                step += 1
                if (1 << step) < windows:
                    kept = kept + arrived
    share = kept + arrived
    scale = 1.0 / math.sqrt(windows * slabs * voxels)
    return (activated[None], point_grads[None], share * scale)


def solution(mesh):
    return jax.shard_map(
        per_device,
        mesh=mesh,
        in_specs=(
            P("dp", "slab", None),
            P("dp", "slab", None),
            P("dp", "slab"),
            P("dp", "slab"),
            P("dp", "slab", None, None),
            P("dp", "slab", None),
            P(),
            P("dp", "slab", None),
        ),
        out_specs=(P("dp", "slab", None), P("dp", "slab", None), P("slab", None)),
        check_vma=False,
    )
```

time: 137 us -> 95.5 us (0.70)
  blocking collectives: 24.4 us -> 0 us
  local copies, waits for them, and re-layouts: 23.5 us -> 2.76 us
  starting transfers between devices: 18.2 us -> 22.1 us
  other arithmetic: 4.36 us -> 2.05 us
  waiting for transfers between devices: 35.3 us -> 37.4 us
    all_to_all x1 -> x0, blocking collectives: 24.4 us -> none  [per_device(): recv = lax.all_to_all(send, 'slab', split_axis=0, concat_axis=0, tiled=True)]
    unnamed x52 -> x32, local copies, waits for them, and re-layouts: 21.7 us -> 2.76 us
    all_to_all x0 -> x1, waiting for transfers between devices: none -> 13.5 us  [per_device(): recv = lax.all_to_all(send, 'slab', split_axis=0, concat_axis=0, tiled=True)]
    ppermute x9, waiting for transfers between devices: 35.3 us -> 23.9 us  [the longest x5 23.9 us: swapped(): return lax.ppermute(part, axis, [(i, i ^ 1 << bit) for i in range(size)])]
    all_to_all x0 -> x1, starting transfers between devices: none -> 7.37 us  [per_device(): recv = lax.all_to_all(send, 'slab', split_axis=0, concat_axis=0, tiled=True)]
    ppermute x9, starting transfers between devices: 13.4 us -> 9.7 us  [the longest x5 5.03 us: swapped(): return lax.ppermute(part, axis, [(i, i ^ 1 << bit) for i in range(size)])]
    add x4, other arithmetic: 3.7 us -> 1.38 us  [the longest x3 1.33 us: part(): lax.dynamic_slice_in_dim(kept, which * half, half, 0)]
    pallas_call x5 -> x6, Pallas kernels: 25.2 us -> 23.1 us  [the longest x1 6.72 us: per_device(): pl.pallas_call(functools.partial(interior_kernel, capacity), out_shape=(s...]
  transfers between devices with their start and end apart: 10 -> 11, of which waited for: 5 -> 5; matrix products, arithmetic and copies ran while one was open for 1% -> 1% of each run, Pallas kernels for 8% -> 23%
where the time goes in v1:
time: 95.5 us; the launch traced here: 95 us
  waiting for transfers between devices  37.4 us (39%)
  Pallas kernels  29.9 us (31%)
  starting transfers between devices  22.1 us (23%)
  local copies, waits for them, and re-layouts  2.76 us (3%)
  other arithmetic  2.05 us (2%)
    ppermute x5, waiting for transfers between devices, swapped(): return lax.ppermute(part, axis, [(i, i ^ 1 << bit) for i in range(size)])  23.9 us
    all_to_all x1, waiting for transfers between devices, per_device(): recv = lax.all_to_all(send, 'slab', split_axis=0, concat_axis=0, tiled=True)  13.5 us
    all_to_all x1, starting transfers between devices, per_device(): recv = lax.all_to_all(send, 'slab', split_axis=0, concat_axis=0, tiled=True)  7.37 us
    pallas_call x1, Pallas kernels, per_device(): pl.pallas_call(functools.partial(interior_kernel, capacity), out_shape=(s...  6.72 us
    pallas_call x1, Pallas kernels, per_device(): pl.pallas_call(backward_kernel, out_shape=struct(voxels, C), in_specs=[AN...  6.66 us
    pallas_call x1, Pallas kernels, per_device(): pl.pallas_call(functools.partial(weight_grad_kernel, chunk, starts), out_...  5.7 us
    ppermute x5, starting transfers between devices, swapped(): return lax.ppermute(part, axis, [(i, i ^ 1 << bit) for i in range(size)])  5.03 us
    all_to_all x1, starting transfers between devices, per_device(): lax.all_to_all(back_points.reshape(slabs, capacity, C), 'slab', split_axi...  4.98 us
  transfers between devices with their start and end apart: 11, of which 5 were waited for; matrix products, arithmetic and copies ran while one was open for 1% of the time, Pallas kernels for 23%

profile of v1, /device:TPU:0, one launch (start us, length us, event | category | flops | bytes accessed | tf_op | source)
XLA Modules:
  0.0 95.0 jit_solution(18073888890672901305)
XLA Ops:
  0.6 2.9 %pack.1 = (f32[16,72,128]{2,1,0:T(8,128)}, s32[8,512]{1,0:T(8,128)}) custom-call(s32[1]{0:T(128)} %bitcast.1.me_ref.me, f32[512,128]{1,0:T(8,128)} %bitcast.17, s32[1,512]{1,0:T(1,128)} %bitcast.18, s32[1,512]{1,0:T(1,128)} %slot_in.1, s32[1,512]{1,0:T(1,128)} %vox_in.1), custom_call_target="tpu_custom_call" | custom-call | flops 2000000000 | tf_op jit(solution)/shard_map/pack/pallas_call | solution.py:440
  3.5 0.0 copy-start.8
  3.6 7.4 %all-to-all-start = ((f32[16,72,128]{2,1,0:T(8,128)}), f32[16,72,128]{2,1,0:T(8,128)S(1)}, u32[]{:S(2)}, u32[]{:S(2)}) async-start(f32[16,72,128]{2,1,0:T(8,128)} %get-tuple-element.33), calls=%async_computation | async-start | bytes 1179648 | tf_op jit(solution)/shard_map/all_to_all | solution.py:453
  10.9 0.0 copy-start
  10.9 1.5 %copy-done = f32[27,128,128]{2,1,0:T(8,128)S(1)} copy-done((f32[27,128,128]{2,1,0:T(8,128)S(1)}, f32[27,128,128]{2,1,0:T(8,128)}, u32[]{:S(2)}) %copy-start) | copy-done | bytes 1769496
  12.4 0.5 weights.1.backward_in
  13.0 13.5 %all-to-all-done.recv = f32[16,72,128]{2,1,0:T(8,128)S(1)} async-done(((f32[16,72,128]{2,1,0:T(8,128)}), f32[16,72,128]{2,1,0:T(8,128)S(1)}, u32[]{:S(2)}, u32[]{:S(2)}) %all-to-all-start) | async-done | bytes 589856 | tf_op jit(solution)/shard_map/all_to_all | solution.py:453
  26.5 0.0 copy-done.8
  26.5 0.8 faces.1
  27.3 0.1 collective-permute-start
  27.4 3.1 %collective-permute-start.1 = (f32[64,128]{1,0:T(8,128)S(1)}, f32[64,128]{1,0:T(8,128)S(1)}, u32[]{:S(2)}, u32[]{:S(2)}) collective-permute-start(f32[64,128]{1,0:T(8,128)S(1)} %get-tuple-element.39), channel_id=1, source_target_pairs={{0,30},{2,4},{4,2},{6,8},{8,6},{10,12},{12,10},{14,16},{16,14},{18... | collective-permute-start | bytes 98312 | tf_op jit(solution)/shard_map/ppermute | solution.py:476
  30.5 0.0 copy-done.7
  30.5 0.0 copy-done.1
  30.5 6.7 %interior.1 = (f32[1024,128]{1,0:T(8,128)S(1)}, bf16[2,512,2304]{2,1,0:T(8,128)(2,1)S(1)}, f32[256,128]{1,0:T(8,128)S(1)}, f32[64,128]{1,0:T(8,128)S(1)}, bf16[3,2304,256]{2,1,0:T(8,128)(2,1)S(1)}) custom-call(s32[2,27]{1,0:T(2,128)S(1)} %bitcast.12, f32[16,72,128]{2,1,0:T(8,128)S(1)} %all-to-all-done.recv, f32[27,128,128]{2,1,0:T(8,128)S(1)} %copy-done.1), custom_call_target="tpu_custom_call" | custom-call | flops 6499999744 | tf_op jit(solution)/shard_map/interior/pallas_call | solution.py:477
  37.2 0.0 collective-permute-done.from_core
  37.2 0.0 collective-permute-done.1.from_far
  37.3 0.0 copy-done.2
  37.3 2.7 %finish.1 = (f32[1024,128]{1,0:T(8,128)}, bf16[1024,256]{1,0:T(8,128)(2,1)S(1)}, bf16[2,128,2304]{2,1,0:T(8,128)(2,1)S(1)}, f32[64,128]{1,0:T(8,128)S(1)}, f32[64,128]{1,0:T(8,128)S(1)}) custom-call(s32[2,27]{1,0:T(2,128)S(1)} %bitcast.13, s32[1]{0:T(128)} %bitcast.1.me_ref.me, f32[1024,128]{1,0:T(8,128)S(1)} %get-tuple-element.36.before, ...), custom_call_target="tpu_custom_call" | custom-call | flops 2800000000 | tf_op jit(solution)/shard_map/finish/pallas_call | solution.py:499
  40.0 1.4 %collective-permute-start.2 = (f32[64,128]{1,0:T(8,128)S(1)}, f32[64,128]{1,0:T(8,128)S(1)}, u32[]{:S(2)}, u32[]{:S(2)}) collective-permute-start(f32[64,128]{1,0:T(8,128)S(1)} %get-tuple-element.48), channel_id=1, source_target_pairs={{0,30},{2,4},{4,2},{6,8},{8,6},{10,12},{12,10},{14,16},{16,14},{18... | collective-permute-start | bytes 98312 | tf_op jit(solution)/shard_map/ppermute | solution.py:544
  41.4 0.0 collective-permute-start.3
  41.4 5.7 %weight_grad.1 = (f32[1728,128]{1,0:T(8,128)S(1)}, f32[1728,128]{1,0:T(8,128)}) custom-call(s32[1]{0:T(128)} %bitcast.1.me_ref.me, bf16[2,512,2304]{2,1,0:T(8,128)(2,1)S(1)} %get-tuple-element.43.columns, bf16[2,128,2304]{2,1,0:T(8,128)(2,1)S(1)} %get-tuple-element.44.outer, bf16[1024,256]{1,0:T(8,128)(2,1)S(1)} %get-tuple-element.52.grads), custom_call_target="tpu_custom_call" | custom-call | flops 4000000000 | tf_op jit(solution)/shard_map/weight_grad/pallas_call | solution.py:527
  47.1 0.0 copy-done.9
  47.1 0.0 collective-permute-done.2.halo_far
  47.1 0.6 copy-done.3
  47.8 0.0 collective-permute-done.3.halo_core
  47.8 0.6 copy-done.5
  48.4 0.5 collective-permute-start.4
  48.9 2.4 %collective-permute-done.4 = f32[1728,128]{1,0:T(8,128)} collective-permute-done((f32[1728,128]{1,0:T(8,128)}, f32[1728,128]{1,0:T(8,128)}, u32[]{:S(2)}, u32[]{:S(2)}) %collective-permute-start.4) | collective-permute-done | bytes 884768 | tf_op jit(solution)/shard_map/ppermute | solution.py:539
  51.3 1.3 %dynamic-slice_add_fusion.1 = (f32[864,128]{1,0:T(8,128)S(1)}, f32[864,128]{1,0:T(8,128)S(1)}) fusion(f32[1728,128]{1,0:T(8,128)} %collective-permute-done.4, s32[]{:T(128)S(6)} %select_n.24, f32[1728,128]{1,0:T(8,128)S(1)} %get-tuple-element.46, s32[]{:T(128)S(6)} %select_n.26), kind=kLoop, calls=%fused_computation.1 | loop fusion | flops 221184 | bytes 2654216 | tf_op jit(solution)/shard_map/add | solution.py:354
  52.6 0.0 copy-start.4
  52.6 0.0 copy-start.6
  52.6 0.0 copy-start.12
  52.6 0.1 collective-permute-start.5
  52.7 6.7 %backward.1.grad_blocks = f32[1024,128]{1,0:T(8,128)S(1)} custom-call(s32[2,27]{1,0:T(2,128)S(1)} %bitcast.14, bf16[1024,256]{1,0:T(8,128)(2,1)S(1)} %copy-done.10, bf16[1152,1152]{1,0:T(8,128)(2,1)S(1)} %weights.1.backward_in), custom_call_target="tpu_custom_call" | custom-call | flops 6499999744 | tf_op jit(solution)/shard_map/backward/pallas_call | solution.py:550
  59.4 5.8 %collective-permute-done.5 = f32[864,128]{1,0:T(8,128)S(1)} collective-permute-done((f32[864,128]{1,0:T(8,128)S(1)}, f32[864,128]{1,0:T(8,128)S(1)}, u32[]{:S(2)}, u32[]{:S(2)}) %collective-permute-start.5) | collective-permute-done | bytes 442400 | tf_op jit(solution)/shard_map/ppermute | solution.py:539
  65.2 0.2 collective-permute-start.6
  65.4 0.0 copy-done.12
  65.4 2.2 %gather.1 = f32[1024,128]{1,0:T(8,128)} custom-call(s32[2]{0:T(128)S(1)} %bitcast.16, s32[1]{0:T(128)} %bitcast.1.me_ref.me, f32[1024,128]{1,0:T(8,128)S(1)} %backward.1.grad_blocks, f32[64,128]{1,0:T(8,128)S(1)} %copy-done.6, f32[64,128]{1,0:T(8,128)S(1)} %copy-done.4, f32[64,128]{1,0:T(8,128)S(1)} %copy-done.12), custom_call_target="tpu_custom_call" | custom-call | flops 2200000000 | tf_op jit(solution)/shard_map/gather/pallas_call | solution.py:571
  67.6 5.0 %all-to-all-start.1 = ((f32[16,64,128]{2,1,0:T(8,128)}), f32[16,64,128]{2,1,0:T(8,128)S(1)}, u32[]{:S(2)}, u32[]{:S(2)}) async-start(f32[16,64,128]{2,1,0:T(8,128)} %bitcast.7), calls=%async_computation.1 | async-start | bytes 1048576 | tf_op jit(solution)/shard_map/all_to_all | solution.py:581
  72.6 0.0 collective-permute-done.6
  72.7 0.1 add_add_fusion
  72.7 1.6 %collective-permute-start.7 = (f32[432,128]{1,0:T(8,128)S(1)}, f32[432,128]{1,0:T(8,128)S(1)}, u32[]{:S(2)}, u32[]{:S(2)}) collective-permute-start(f32[432,128]{1,0:T(8,128)S(1)} %add_add_fusion), channel_id=1, source_target_pairs={{0,1},{1,0},{2,3},{3,2},{4,5},{5,4},{6,7},{7,6},{8,9},{9,8},{10,11... | collective-permute-start | bytes 663560 | tf_op jit(solution)/shard_map/ppermute | solution.py:539
  74.3 6.2 %collective-permute-done.7 = f32[432,128]{1,0:T(8,128)S(1)} collective-permute-done((f32[432,128]{1,0:T(8,128)S(1)}, f32[432,128]{1,0:T(8,128)S(1)}, u32[]{:S(2)}, u32[]{:S(2)}) %collective-permute-start.7) | collective-permute-done | bytes 221216 | tf_op jit(solution)/shard_map/ppermute | solution.py:539
  80.6 2.6 %collective-permute-start.8 = (f32[216,128]{1,0:T(8,128)S(1)}, f32[216,128]{1,0:T(8,128)S(1)}, u32[]{:S(2)}, u32[]{:S(2)}) collective-permute-start(f32[216,128]{1,0:T(8,128)S(1)} %dynamic-slice_add_fusion.3), channel_id=1, source_target_pairs={{0,16},{2,18},{4,20},{6,22},{8,24},{10,26},{12,28},{14,30},{16,0},... | collective-permute-start | bytes 331784 | tf_op jit(solution)/shard_map/ppermute | solution.py:539
  83.2 9.5 %collective-permute-done.8 = f32[216,128]{1,0:T(8,128)S(1)} collective-permute-done((f32[216,128]{1,0:T(8,128)S(1)}, f32[216,128]{1,0:T(8,128)S(1)}, u32[]{:S(2)}, u32[]{:S(2)}) %collective-permute-start.8) | collective-permute-done | bytes 110624 | tf_op jit(solution)/shard_map/ppermute | solution.py:539
  92.7 0.7 add_multiply_fusion
  93.3 0.0 all-to-all-done.1
  93.3 1.7 %unpack.1 = f32[512,128]{1,0:T(8,128)} custom-call(f32[1024,128]{1,0:T(8,128)S(1)} %bitcast.10, s32[8,512]{1,0:T(8,128)S(1)} %copy-done.13), custom_call_target="tpu_custom_call" | custom-call | flops 1700000000 | tf_op jit(solution)/shard_map/unpack/pallas_call | solution.py:584
  (20 shorter events, 0.1 us)
Async XLA Ops:
  3.5 22.9 %copy-start.8 = (s32[1,1,2,1]{2,3,1,0:T(1,128)S(1)}, s32[1,1,2,1]{2,3,1,0:T(1,128)}, u32[]{:S(2)}) copy-start(s32[1,1,2,1]{2,3,1,0:T(1,128)} %param.12) | copy-start | bytes 28
  3.6 22.9 %all-to-all-start = ((f32[16,72,128]{2,1,0:T(8,128)}), f32[16,72,128]{2,1,0:T(8,128)S(1)}, u32[]{:S(2)}, u32[]{:S(2)}) async-start(f32[16,72,128]{2,1,0:T(8,128)} %get-tuple-element.33), calls=%async_computation | async-start | bytes 1179648 | tf_op jit(solution)/shard_map/all_to_all | solution.py:453
  10.9 1.5 %copy-start = (f32[27,128,128]{2,1,0:T(8,128)S(1)}, f32[27,128,128]{2,1,0:T(8,128)}, u32[]{:S(2)}) copy-start(f32[27,128,128]{2,1,0:T(8,128)} %taps_in) | copy-start | bytes 5308420
  12.4 18.1 %copy-start.7 = (s32[1,2,27]{2,1,0:T(2,128)S(1)}, s32[1,2,27]{2,1,0:T(2,128)}, u32[]{:S(2)}) copy-start(s32[1,2,27]{2,1,0:T(2,128)} %param.13) | copy-start | bytes 652
  26.5 4.0 %copy-start.1 = (f32[27,128,128]{2,1,0:T(8,128)S(1)}, f32[27,128,128]{2,1,0:T(8,128)}, u32[]{:S(2)}) copy-start(f32[27,128,128]{2,1,0:T(8,128)} %taps_in) | copy-start | bytes 5308420
  27.3 10.0 %collective-permute-start = (f32[64,128]{1,0:T(8,128)S(1)}, f32[64,128]{1,0:T(8,128)S(1)}, u32[]{:S(2)}, u32[]{:S(2)}) collective-permute-start(f32[64,128]{1,0:T(8,128)S(1)} %get-tuple-element.38), channel_id=1, source_target_pairs={{0,2},{2,0},{4,6},{6,4},{8,10},{10,8},{12,14},{14,12},{16,18},{18,... | collective-permute-start | bytes 98312 | tf_op jit(solution)/shard_map/ppermute | solution.py:475
  27.4 9.9 %collective-permute-start.1 = (f32[64,128]{1,0:T(8,128)S(1)}, f32[64,128]{1,0:T(8,128)S(1)}, u32[]{:S(2)}, u32[]{:S(2)}) collective-permute-start(f32[64,128]{1,0:T(8,128)S(1)} %get-tuple-element.39), channel_id=1, source_target_pairs={{0,30},{2,4},{4,2},{6,8},{8,6},{10,12},{12,10},{14,16},{16,14},{18... | collective-permute-start | bytes 98312 | tf_op jit(solution)/shard_map/ppermute | solution.py:476
  30.5 6.8 %copy-start.2 = (f32[1,1024,128]{2,1,0:T(8,128)S(1)}, f32[1,1024,128]{2,1,0:T(8,128)}, u32[]{:S(2)}) copy-start(f32[1,1024,128]{2,1,0:T(8,128)} %param.15) | copy-start | bytes 1572868
  37.2 2.7 %copy-start.11 = (f32[64,128]{1,0:T(8,128)}, f32[64,128]{1,0:T(8,128)S(1)}, u32[]{:S(2)}) copy-start(f32[64,128]{1,0:T(8,128)S(1)} %get-tuple-element.58.codes) | copy-start | bytes 98308
  40.0 7.2 %copy-start.9 = (bf16[1024,256]{1,0:T(8,128)(2,1)}, bf16[1024,256]{1,0:T(8,128)(2,1)S(1)}, u32[]{:S(2)}) copy-start(bf16[1024,256]{1,0:T(8,128)(2,1)S(1)} %get-tuple-element.52.grads) | copy-start | bytes 1572868
  40.0 7.2 %collective-permute-start.2 = (f32[64,128]{1,0:T(8,128)S(1)}, f32[64,128]{1,0:T(8,128)S(1)}, u32[]{:S(2)}, u32[]{:S(2)}) collective-permute-start(f32[64,128]{1,0:T(8,128)S(1)} %get-tuple-element.48), channel_id=1, source_target_pairs={{0,30},{2,4},{4,2},{6,8},{8,6},{10,12},{12,10},{14,16},{16,14},{18... | collective-permute-start | bytes 98312 | tf_op jit(solution)/shard_map/ppermute | solution.py:544
  41.4 6.3 %collective-permute-start.3 = (f32[64,128]{1,0:T(8,128)S(1)}, f32[64,128]{1,0:T(8,128)S(1)}, u32[]{:S(2)}, u32[]{:S(2)}) collective-permute-start(f32[64,128]{1,0:T(8,128)S(1)} %get-tuple-element.49), channel_id=1, source_target_pairs={{0,2},{2,0},{4,6},{6,4},{8,10},{10,8},{12,14},{14,12},{16,18},{18,... | collective-permute-start | bytes 98312 | tf_op jit(solution)/shard_map/ppermute | solution.py:545
  47.1 0.6 copy-start.3
  47.8 0.6 copy-start.5
  48.4 2.9 %collective-permute-start.4 = (f32[1728,128]{1,0:T(8,128)}, f32[1728,128]{1,0:T(8,128)}, u32[]{:S(2)}, u32[]{:S(2)}) collective-permute-start(f32[1728,128]{1,0:T(8,128)} %get-tuple-element.50), channel_id=1, source_target_pairs={{0,2},{2,0},{4,6},{6,4},{8,10},{10,8},{12,14},{14,12},{16,18},{18,... | collective-permute-start | bytes 2654216 | tf_op jit(solution)/shard_map/ppermute | solution.py:539
  48.9 3.8 %copy-start.10 = (bf16[1024,256]{1,0:T(8,128)(2,1)S(1)}, bf16[1024,256]{1,0:T(8,128)(2,1)}, u32[]{:S(2)}) copy-start(bf16[1024,256]{1,0:T(8,128)(2,1)} %copy-done.9) | copy-start | bytes 1572868
  52.6 12.6 %copy-start.14 = (f32[864,128]{1,0:T(8,128)}, f32[864,128]{1,0:T(8,128)S(1)}, u32[]{:S(2)}) copy-start(f32[864,128]{1,0:T(8,128)S(1)} %get-tuple-element.61) | copy-start | bytes 1327108
  52.6 12.8 %copy-start.4 = (f32[64,128]{1,0:T(8,128)S(1)}, f32[64,128]{1,0:T(8,128)}, u32[]{:S(2)}) copy-start(f32[64,128]{1,0:T(8,128)} %copy-done.3) | copy-start | bytes 98308
  52.6 12.8 %copy-start.6 = (f32[64,128]{1,0:T(8,128)S(1)}, f32[64,128]{1,0:T(8,128)}, u32[]{:S(2)}) copy-start(f32[64,128]{1,0:T(8,128)} %copy-done.5) | copy-start | bytes 98308
  52.6 12.8 %copy-start.12 = (f32[64,128]{1,0:T(8,128)S(1)}, f32[64,128]{1,0:T(8,128)}, u32[]{:S(2)}) copy-start(f32[64,128]{1,0:T(8,128)} %copy-done.11) | copy-start | bytes 98308
  52.6 12.5 %collective-permute-start.5 = (f32[864,128]{1,0:T(8,128)S(1)}, f32[864,128]{1,0:T(8,128)S(1)}, u32[]{:S(2)}, u32[]{:S(2)}) collective-permute-start(f32[864,128]{1,0:T(8,128)S(1)} %get-tuple-element.51), channel_id=1, source_target_pairs={{0,4},{2,6},{4,0},{6,2},{8,12},{10,14},{12,8},{14,10},{16,20},{18,... | collective-permute-start | bytes 1327112 | tf_op jit(solution)/shard_map/ppermute | solution.py:539
  65.2 7.5 %collective-permute-start.6 = (f32[432,128]{1,0:T(8,128)S(1)}, f32[432,128]{1,0:T(8,128)S(1)}, u32[]{:S(2)}, u32[]{:S(2)}) collective-permute-start(f32[432,128]{1,0:T(8,128)S(1)} %dynamic-slice_add_fusion.2), channel_id=1, source_target_pairs={{0,8},{2,10},{4,12},{6,14},{8,0},{10,2},{12,4},{14,6},{16,24},{18,... | collective-permute-start | bytes 663560 | tf_op jit(solution)/shard_map/ppermute | solution.py:539
  65.4 7.2 %copy-start.15 = (f32[864,128]{1,0:T(8,128)S(1)}, f32[864,128]{1,0:T(8,128)}, u32[]{:S(2)}) copy-start(f32[864,128]{1,0:T(8,128)} %copy-done.14) | copy-start | bytes 1327108
  67.6 25.7 %copy-start.13 = (s32[8,512]{1,0:T(8,128)S(1)}, s32[8,512]{1,0:T(8,128)}, u32[]{:S(2)}) copy-start(s32[8,512]{1,0:T(8,128)} %get-tuple-element.59.dest) | copy-start | bytes 49156
  67.6 25.7 %all-to-all-start.1 = ((f32[16,64,128]{2,1,0:T(8,128)}), f32[16,64,128]{2,1,0:T(8,128)S(1)}, u32[]{:S(2)}, u32[]{:S(2)}) async-start(f32[16,64,128]{2,1,0:T(8,128)} %bitcast.7), calls=%async_computation.1 | async-start | bytes 1048576 | tf_op jit(solution)/shard_map/all_to_all | solution.py:581
  72.7 7.8 %collective-permute-start.7 = (f32[432,128]{1,0:T(8,128)S(1)}, f32[432,128]{1,0:T(8,128)S(1)}, u32[]{:S(2)}, u32[]{:S(2)}) collective-permute-start(f32[432,128]{1,0:T(8,128)S(1)} %add_add_fusion), channel_id=1, source_target_pairs={{0,1},{1,0},{2,3},{3,2},{4,5},{5,4},{6,7},{7,6},{8,9},{9,8},{10,11... | collective-permute-start | bytes 663560 | tf_op jit(solution)/shard_map/ppermute | solution.py:539
  80.6 12.1 %collective-permute-start.8 = (f32[216,128]{1,0:T(8,128)S(1)}, f32[216,128]{1,0:T(8,128)S(1)}, u32[]{:S(2)}, u32[]{:S(2)}) collective-permute-start(f32[216,128]{1,0:T(8,128)S(1)} %dynamic-slice_add_fusion.3), channel_id=1, source_target_pairs={{0,16},{2,18},{4,20},{6,22},{8,24},{10,26},{12,28},{14,30},{16,0},... | collective-permute-start | bytes 331784 | tf_op jit(solution)/shard_map/ppermute | solution.py:539

commit v2 on v1

--- a/solution.py
+++ b/solution.py
@@ -159,13 +159,13 @@
     return [v.reshape(PAD * E, C) for v in (down, three[1], up)]
 
 
-def put_columns(columns, at_first, rows, versions):
+def put_columns(columns, rows, versions):
     for k in range(3):
         for j in range(3):
             high, low = split(versions[k][E * j : E * j + FACE])
             at = (3 * j + k) * C
-            columns[at_first, rows, at : at + C] = high
-            columns[at_first, rows, COLS + at : COLS + at + C] = low
+            columns[rows, at : at + C] = high
+            columns[rows, COLS + at : COLS + at + C] = low
 
 
 def load(source, block, stride, offset, size):
@@ -218,7 +218,7 @@
 def interior_kernel(
     capacity, names_in, recv, taps_in,
     before, columns, faces, codes_out, forward,
-    names, visible, hot, taps, sems,
+    names, visible, taps, sems,
 ):
     names_copy = pltpu.make_async_copy(names_in, names, sems.at[0])
     taps_copy = pltpu.make_async_copy(taps_in, taps, sems.at[1])
@@ -227,38 +227,35 @@
     voxels = NB * VOX
     group = C // capacity
     ids, row_parts = received(recv, capacity)
-    numbers = iota((voxels, C), 0).astype(f32) + 1.0
+    tiles = []
     for chunk in range(recv.shape[0] // group):
         codes = codes_of(ids, chunk, group)
         codes_out[chunk * 8 : (chunk + 1) * 8, :] = codes
-        match = numbers == codes[:1]
-        hot[:, chunk * C : (chunk + 1) * C] = jnp.where(match, 1.0, 0.0).astype(bf16)
-    sums = mm(hot[...], row_parts)
-    visible[:voxels] = sums[:, :C] + sums[:, C:]
+        tiles.append(codes[:1])
+    for start in range(0, voxels, C):
+        number = iota((C, C), 0).astype(f32) + (start + 1.0)
+        hot = [jnp.where(number == tile, 1.0, 0.0).astype(bf16) for tile in tiles]
+        sums = mm(jnp.concatenate(hot, axis=1), row_parts)
+        visible[start : start + C] = sums[:, :C] + sums[:, C:]
     visible[voxels:] = jnp.zeros((VOX, C), f32)
     for b in range(NB):
         faces[b * FACE : (b + 1) * FACE] = visible[(b + 1) * VOX - FACE : (b + 1) * VOX]
         faces[(NB + b) * FACE : (NB + b + 1) * FACE] = visible[b * VOX : b * VOX + FACE]
     names_copy.wait()
     for b in range(NB):
-
-        @pl.loop(1, E + 1)
-        def _(p):
-            planes = build_plane(names, b, 1, visible, VOX, (p - 1) * FACE, 2)
-            put_columns(columns, b, pl.ds(pl.multiple_of((p - 1) * FACE, FACE), FACE), planes)
-
-    taps_copy.wait()
-    split_taps(taps, forward)
-    for b in range(NB):
-        start = b * VOX
-        total = mm(columns[b], forward[1])
-        before[start : start + VOX] = total[:, :C] + total[:, C:]
-        total = mm(columns[b, : VOX - FACE, :], forward[0])
-        here = slice(start + FACE, start + VOX)
-        before[here] = before[here] + total[:, :C] + total[:, C:]
-        total = mm(columns[b, FACE:, :], forward[2])
-        here = slice(start, start + VOX - FACE)
-        before[here] = before[here] + total[:, :C] + total[:, C:]
+        for x in range(E):
+            rows = slice(b * VOX + x * FACE, b * VOX + (x + 1) * FACE)
+            put_columns(columns, rows, build_plane(names, b, 1, visible, VOX, x * FACE, 2))
+        if b == 0:
+            taps_copy.wait()
+            split_taps(taps, forward)
+        low, high = b * VOX, (b + 1) * VOX
+        total = mm(columns[low:high, :], forward[1])
+        before[low:high] = total[:, :C] + total[:, C:]
+        total = mm(columns[low : high - FACE, :], forward[0])
+        before[low + FACE : high] = before[low + FACE : high] + total[:, :C] + total[:, C:]
+        total = mm(columns[low + FACE : high, :], forward[2])
+        before[low : high - FACE] = before[low : high - FACE] + total[:, :C] + total[:, C:]
 
 
 def finish_kernel(
@@ -297,7 +294,7 @@
     for n, (i, x, source) in enumerate(((0, 0, faces_low), (2, E - 1, faces_high))):
         for b in range(NB):
             rows = slice(b * FACE, (b + 1) * FACE)
-            put_columns(outer, n, rows, build_plane(names, b, i, source, FACE, 0, 4))
+            put_columns(outer.at[n], rows, build_plane(names, b, i, source, FACE, 0, 4))
         total = mm(outer[n], forward[i])
         total = total[:, :C] + total[:, C:]
         for b in range(NB):
@@ -325,40 +322,90 @@
     to_far[...] = jnp.where(even, left, right)
 
 
-def weight_grad_kernel(chunk, starts, me, columns, outer, grads, kept, sent, total, ordered):
+def face_grads(grads, i):
+    x = 0 if i == 0 else E - 1
+    return jnp.concatenate([grads[(b * E + x) * FACE : (b * E + x + 1) * FACE, :] for b in range(NB)], axis=0)
+
+
+def shifted_grads(grads, i):
+    none = jnp.zeros((FACE, grads.shape[1]), bf16)
+    rows = []
+    for b in range(NB):
+        block = grads[b * VOX : (b + 1) * VOX, :]
+        rows += [[block[FACE:], none], [block], [none, block[: VOX - FACE]]][i]
+    return jnp.concatenate(rows, axis=0)
+
+
+def weight_grad_kernel(chunk, pieces, me, columns, outer, grads, kept, sent, ordered):
     tn = ((0,), (0,))
-    for i in range(3):
-        low, high = max(i - 1, 0), E + min(i - 1, 0)
-        for b in range(NB):
-            x = b * E + 1 - i
-            term = mm(columns[b, low * FACE : high * FACE, :], grads[(x + low) * FACE : (x + high) * FACE, :], tn)
-            total[...] = term if b == 0 else total[...] + term
-        if i != 1:
-            x = 0 if i == 0 else E - 1
-            faces = [grads[(b * E + x) * FACE : (b * E + x + 1) * FACE, :] for b in range(NB)]
-            total[...] = total[...] + mm(outer[i // 2], jnp.concatenate(faces, axis=0), tn)
-        value = total[:COLS, :C] + total[:COLS, C:] + total[COLS:, :C] + total[COLS:, C:]
-        ordered[i * COLS : (i + 1) * COLS] = value
+    shifted = [shifted_grads(grads, i) for i in range(3)]
+    wide = jnp.concatenate(shifted, axis=1)
+    narrow = jnp.concatenate([value[:, :C] for value in shifted], axis=1)
+    faces = [face_grads(grads, i) for i in range(3)]
+    for start in range(0, COLS, 3 * C):
+        high = slice(start, start + 3 * C)
+        low = slice(COLS + start, COLS + start + 3 * C)
+        term = mm(columns[:, high], wide, tn)
+        rest = mm(columns[:, low], narrow, tn)
+        for i in range(3):
+            value = term[:, 2 * i * C : (2 * i + 1) * C] + term[:, (2 * i + 1) * C : (2 * i + 2) * C]
+            value = value + rest[:, i * C : (i + 1) * C]
+            if i != 1:
+                face = mm(outer[i // 2, :, high], faces[i], tn)
+                value = value + face[:, :C] + face[:, C:]
+                value = value + mm(outer[i // 2, :, low], faces[i][:, :C], tn)
+            ordered[i * COLS + start : i * COLS + start + 3 * C] = value
     first = jnp.bitwise_and(me[0], 1) == 0
-    for n, to in enumerate(starts):
-        even = ordered[2 * n * chunk : (2 * n + 1) * chunk]
-        odd = ordered[(2 * n + 1) * chunk : (2 * n + 2) * chunk]
-        kept[to : to + chunk] = jnp.where(first, even, odd)
-        sent[to : to + chunk] = jnp.where(first, odd, even)
-
-
-def halve(kept, arrived, side):
-    half = kept.shape[0] // 2
-
-    def part(which):
-        return lax.dynamic_slice_in_dim(kept, which * half, half, 0) + lax.dynamic_slice_in_dim(
-            arrived, which * half, half, 0
+    for n, runs in enumerate(pieces):
+        for start, size, to in runs:
+            start = 2 * n * chunk + start
+            even = ordered[start : start + size]
+            odd = ordered[start + chunk : start + chunk + size]
+            kept[to : to + size] = jnp.where(first, even, odd)
+            sent[to : to + size] = jnp.where(first, odd, even)
+
+
+def halve_kernel(split_at, side, kept, arrived, kept_out, sent_out):
+    total, half = kept.shape[0], kept_out.shape[0]
+    for start, stop in ((0, split_at), (split_at, total)):
+        size = (stop - start) // 2
+        to = slice(start // 2, start // 2 + size)
+        mine = pl.ds(pl.multiple_of(start + side[0] * size, 8), size)
+        other = pl.ds(pl.multiple_of(start + (1 - side[0]) * size, 8), size)
+        kept_out[to] = kept[mine, :] + arrived[mine, :]
+        sent_out[to] = kept[other, :] + arrived[other, :]
+
+
+def part_of(kept, arrived, start, size):
+    return lax.dynamic_slice_in_dim(kept, start, size, 0) + lax.dynamic_slice_in_dim(arrived, start, size, 0)
+
+
+def halve(kept, arrived, split_at, side):
+    total = kept.shape[0]
+    if split_at % 16 == 0 and total % 16 == 0:
+        return pl.pallas_call(
+            functools.partial(halve_kernel, split_at),
+            out_shape=(struct(total // 2, C),) * 2,
+            in_specs=[SMEM, VMEM, VMEM],
+            out_specs=(VMEM, VMEM),
+            compiler_params=params(4),
+            name="halve",
+            cost_estimate=cost(5),
+        )(side.reshape(1), kept, arrived)
+    one, two = split_at // 2, (total - split_at) // 2
+
+    def take(which):
+        return jnp.concatenate(
+            [part_of(kept, arrived, which * one, one), part_of(kept, arrived, split_at + which * two, two)], axis=0
         )
 
-    return part(side), part(1 - side)
-
-
-def backward_kernel(names_in, grads, backward_in, blocks_out, names, backward, shifted, back, target, sems):
+    return take(side), take(1 - side)
+
+
+def backward_kernel(
+    names_in, lent, me, grads, backward_in, halo_core, halo_far, blocks_out,
+    names, backward, shifted, back, target, sems,
+):
     copies = [
         pltpu.make_async_copy(names_in, names, sems.at[0]),
         pltpu.make_async_copy(backward_in, backward, sems.at[1]),
@@ -377,32 +424,25 @@
             shifted[at, (6 + i) * C : (7 + i) * C] = grads[rows, :C]
         if b == 0:
             copies[1].wait()
-        back[...] = mm(shifted[...], backward[...])
-
-        def plane(i, p, offset):
-            rows = pl.ds(pl.multiple_of(p * FACE, FACE), FACE)
-            sums = column_sums(lambda jk: back[rows, jk * C : (jk + 1) * C])
+        back[b] = mm(shifted[...], backward[...])
+    for b in range(NB):
+        for p in range(PAD):
+            i = 0 if p == 0 else 2 if p == PAD - 1 else 1
+            offset = (VOX - FACE, (p - 1) * FACE, 0)[i]
+            rows = slice(p * FACE, (p + 1) * FACE)
+            sums = column_sums(lambda jk: back[b, rows, jk * C : (jk + 1) * C])
             spread_plane(names, b, i, sums, target, VOX, offset, 2)
-
-        plane(0, 0, VOX - FACE)
-        plane(2, PAD - 1, 0)
-
-        @pl.loop(1, E + 1)
-        def _(p):
-            plane(1, p, (p - 1) * FACE)
-
-    blocks_out[...] = target[: NB * VOX]
-
-
-def gather_kernel(lent, me, grad_blocks, halo_core, halo_far, codes, out, target):
-    voxels = NB * VOX
     even = jnp.bitwise_and(me[0], 1) == 0
-    target[...] = grad_blocks[...]
     left = pl.ds(pl.multiple_of(lent[0] * VOX, VOX), FACE)
     right = pl.ds(pl.multiple_of(lent[1] * VOX, VOX) + VOX - FACE, FACE)
     target[left, :] = target[left, :] + jnp.where(even, halo_far[...], halo_core[...])
     target[right, :] = target[right, :] + jnp.where(even, halo_core[...], halo_far[...])
-    parts = jnp.concatenate(split(target[...]), axis=1)
+    blocks_out[...] = target[: NB * VOX]
+
+
+def gather_kernel(grad_blocks, codes, out):
+    voxels = NB * VOX
+    parts = jnp.concatenate(split(grad_blocks[...]), axis=1)
     by_row = codes[...].T
     numbers = iota((C, voxels), 1).astype(f32) + 1.0
     for chunk in range(codes.shape[0] // 8):
@@ -411,6 +451,10 @@
         out[chunk * C : (chunk + 1) * C] = rows[:, :C] + rows[:, C:]
 
 
+def pass_kernel(rows, one, two, out):
+    del rows, one, two, out
+
+
 def unpack_kernel(came_back, dest, out):
     places = dest[...].astype(f32).T[:, :1]
     points, slots = out.shape[0], came_back.shape[0]
@@ -419,8 +463,11 @@
     out[...] = rows[:, :C] + rows[:, C : 2 * C] + rows[:, 2 * C :]
 
 
-def bit_reversed(number, bits):
-    return int(format(number, f"0{bits}b")[::-1], 2)
+def place(slab, order):
+    number = 0
+    for bit in order:
+        number = 2 * number + (slab >> bit & 1)
+    return number
 
 
 def per_device(
@@ -478,7 +525,7 @@
         functools.partial(interior_kernel, capacity),
         out_shape=(
             struct(voxels, C),
-            struct(NB, VOX, 2 * COLS, dtype=bf16),
+            struct(voxels, 2 * COLS, dtype=bf16),
             struct(2 * NB * FACE, C),
             struct(slabs * capacity // C * 8, C),
             struct(3, 2 * COLS, 2 * C, dtype=bf16),
@@ -488,13 +535,12 @@
         scratch_shapes=[
             pltpu.SMEM((NB, 27), jnp.int32),
             pltpu.VMEM((3 * VOX, C), f32),
-            pltpu.VMEM((voxels, slabs * capacity), bf16),
             pltpu.VMEM(weight_taps.shape, f32),
             pltpu.SemaphoreType.DMA((2,)),
         ],
         compiler_params=params(16),
         name="interior",
-        cost_estimate=cost(6.5),
+        cost_estimate=cost(5),
     )(names, recv, weight_taps)
     activated, grads, outer, edge_core, edge_far = pl.pallas_call(
         finish_kernel,
@@ -523,13 +569,22 @@
         name="finish",
         cost_estimate=cost(2.8),
     )(names, me.reshape(1), before, faces, from_core, from_far, forward, backward, cotangent[0])
-    starts = tuple(bit_reversed(n, bits - 1) * chunk for n in range(slabs // 2))
+    cut = -(-chunk // 16) * 8
+    rest = list(range(3, bits))
+    orders = ([1, 2] + rest, [2, 1] + rest)
+    pieces = tuple(
+        (
+            (0, cut, place(2 * n, orders[0]) * cut),
+            (cut, chunk - cut, slabs // 2 * cut + place(2 * n, orders[1]) * (chunk - cut)),
+        )
+        for n in range(slabs // 2)
+    )
     kept, sent = pl.pallas_call(
-        functools.partial(weight_grad_kernel, chunk, starts),
+        functools.partial(weight_grad_kernel, chunk, pieces),
         out_shape=(struct(27 * C // 2, C),) * 2,
         in_specs=[SMEM] + [VMEM] * 3,
         out_specs=(VMEM, VMEM),
-        scratch_shapes=[pltpu.VMEM((2 * COLS, 2 * C), f32), pltpu.VMEM((27 * C, C), f32)],
+        scratch_shapes=[pltpu.VMEM((27 * C, C), f32)],
         compiler_params=params(14),
         name="weight_grad",
         cost_estimate=cost(4),
@@ -543,41 +598,55 @@
 
     halo_far = lax.ppermute(edge_far, "slab", far_pairs)
     halo_core = lax.ppermute(edge_core, "slab", core_pairs)
-    sent, halo_far, halo_core = lax.optimization_barrier((sent, halo_far, halo_core))
-    kept, sent = halve(kept, swapped(sent, "slab", 0), side(1))
-    sent, grads = lax.optimization_barrier((sent, grads))
-    arrived = swapped(sent, "slab", 1)
+    arrived = swapped(sent, "slab", 0)
+    mids, sides = slabs // 2 * cut, (side(1), side(2))
+    halves = (mids // 2, (kept.shape[0] - mids) // 2)
+    sent = [part_of(kept, arrived, (0, mids)[q] + (1 - sides[q]) * halves[q], halves[q]) for q in range(2)]
+    sent[0], sent[1], grads, halo_far, halo_core = lax.optimization_barrier(
+        (sent[0], sent[1], grads, halo_far, halo_core)
+    )
+    kept = [part_of(kept, arrived, (0, mids)[q] + sides[q] * halves[q], halves[q]) for q in range(2)]
+    arrived = [swapped(sent[q], "slab", (1, 2)[q]) for q in range(2)]
     grad_blocks = pl.pallas_call(
         backward_kernel,
         out_shape=struct(voxels, C),
-        in_specs=[ANY, VMEM, ANY],
+        in_specs=[ANY, SMEM, SMEM, VMEM, ANY, VMEM, VMEM],
         out_specs=VMEM,
         scratch_shapes=[
             pltpu.SMEM((NB, 27), jnp.int32),
             pltpu.VMEM((9 * C, COLS), bf16),
             pltpu.VMEM((PAD * FACE, 9 * C), bf16),
-            pltpu.VMEM((PAD * FACE, COLS), f32),
+            pltpu.VMEM((NB, PAD * FACE, COLS), f32),
             pltpu.VMEM((3 * VOX, C), f32),
             pltpu.SemaphoreType.DMA((2,)),
         ],
         compiler_params=params(14),
         name="backward",
         cost_estimate=cost(6.5),
-    )(names, grads, backward)
-    arrived, grad_blocks = lax.optimization_barrier((arrived, grad_blocks))
-    kept, sent = halve(kept, arrived, side(2))
-    sent, grad_blocks = lax.optimization_barrier((sent, grad_blocks))
-    arrived = swapped(sent, "slab", 2)
+    )(names, lent, me.reshape(1), grads, backward, halo_core, halo_far)
     back_points = pl.pallas_call(
         gather_kernel,
         out_shape=struct(slabs * capacity, C),
-        in_specs=[SMEM] * 2 + [VMEM] * 4,
+        in_specs=[VMEM, VMEM],
         out_specs=VMEM,
-        scratch_shapes=[pltpu.VMEM((voxels, C), f32)],
         compiler_params=params(12),
         name="gather",
         cost_estimate=cost(2.2),
-    )(lent, me.reshape(1), grad_blocks, halo_core, halo_far, codes)
+    )(grad_blocks, codes)
+    arrived[0], arrived[1], back_points = lax.optimization_barrier((arrived[0], arrived[1], back_points))
+    sides, halves = (side(2), side(1)), [half // 2 for half in halves]
+    sent = [part_of(kept[q], arrived[q], (1 - sides[q]) * halves[q], halves[q]) for q in range(2)]
+    kept = [part_of(kept[q], arrived[q], sides[q] * halves[q], halves[q]) for q in range(2)]
+    back_points = pl.pallas_call(
+        pass_kernel,
+        out_shape=struct(slabs * capacity, C),
+        in_specs=[ANY] * 3,
+        out_specs=ANY,
+        input_output_aliases={0: 0},
+        name="pass",
+        cost_estimate=cost(2.2),
+    )(back_points, *sent)
+    arrived = [swapped(sent[q], "slab", (2, 1)[q]) for q in range(2)]
     came_back = lax.all_to_all(
         back_points.reshape(slabs, capacity, C), "slab", split_axis=0, concat_axis=0, tiled=True
     )
@@ -591,18 +660,18 @@
         cost_estimate=cost(1.7),
     )(came_back.reshape(slabs * capacity, C), dest)
 
-    for bit in range(2, bits):
-        if bit > 2:
-            kept, sent = halve(kept, arrived, side(bit))
-            arrived = swapped(sent, "slab", bit)
-        if bit == bits - 2:
+    kept = jnp.concatenate([kept[q] + arrived[q] for q in range(2)], axis=0)
+    split_at, step = halves[0], 0
+    while (1 << step) < windows:
+        arrived = swapped(kept, "dp", step)
+        step += 1
+        if (1 << step) < windows:
             kept = kept + arrived
-            step = 0
-            while (1 << step) < windows:
-                arrived = swapped(kept, "dp", step)
-                step += 1
-                if (1 << step) < windows:
-                    kept = kept + arrived
+    for bit in rest:
+        kept, sent = halve(kept, arrived, split_at, side(bit))
+        arrived = swapped(sent, "slab", bit)
+        split_at //= 2
+    arrived, point_grads = lax.optimization_barrier((arrived, point_grads))
     share = kept + arrived
     scale = 1.0 / math.sqrt(windows * slabs * voxels)
     return (activated[None], point_grads[None], share * scale)

time: 95.5 us -> 86.6 us (0.907)
  waiting for transfers between devices: 37.4 us -> 29.9 us
  Pallas kernels: 29.9 us -> 25.5 us
  starting transfers between devices: 22.1 us -> 24 us
  other arithmetic: 2.05 us -> 3.1 us
    ppermute x5 -> x7, waiting for transfers between devices: 23.9 us -> 10.8 us  [swapped(): return lax.ppermute(part, axis, [(i, i ^ 1 << bit) for i in range(size)])]
    all_to_all x1, waiting for transfers between devices: 0.01 us -> 4.36 us  [per_device(): lax.all_to_all(back_points.reshape(slabs, capacity, C), 'slab', split_axi...]
    ppermute x5 -> x7, starting transfers between devices: 5.03 us -> 8.43 us  [swapped(): return lax.ppermute(part, axis, [(i, i ^ 1 << bit) for i in range(size)])]
    pallas_call x1, Pallas kernels: 6.72 us -> 5.2 us  [per_device(): pl.pallas_call(functools.partial(interior_kernel, capacity), out_shape=(s...]
    all_to_all x1, starting transfers between devices: 4.98 us -> 3.58 us  [per_device(): lax.all_to_all(back_points.reshape(slabs, capacity, C), 'slab', split_axi...]
    pallas_call x1, Pallas kernels: 2.21 us -> 0.86 us  [per_device(): pl.pallas_call(gather_kernel, out_shape=struct(slabs * capacity, C), in_s...]
    ppermute x1, waiting for transfers between devices: 0.01 us -> 1.2 us  [per_device(): halo_far = lax.ppermute(edge_far, 'slab', far_pairs)]
    add x4 -> x6, other arithmetic: 1.38 us -> 2.42 us  [the longest x4 2.35 us: part_of(): lax.dynamic_slice_in_dim(kept, start, size, 0)]
  transfers between devices with their start and end apart: 11 -> 13, of which waited for: 5 -> 6; matrix products, arithmetic and copies ran while one was open for 1% -> 3% of each run, Pallas kernels for 23% -> 17%
where the time goes in v2:
time: 86.6 us; the launch traced here: 86.2 us
  waiting for transfers between devices  29.9 us (35%)
  Pallas kernels  25.5 us (29%)
  starting transfers between devices  24 us (28%)
  other arithmetic  3.1 us (4%)
  local copies, waits for them, and re-layouts  2.75 us (3%)
  between operations  0.94 us (1%)
    all_to_all x1, waiting for transfers between devices, per_device(): recv = lax.all_to_all(send, 'slab', split_axis=0, concat_axis=0, tiled=True)  13.5 us
    ppermute x7, waiting for transfers between devices, swapped(): return lax.ppermute(part, axis, [(i, i ^ 1 << bit) for i in range(size)])  10.8 us
    ppermute x7, starting transfers between devices, swapped(): return lax.ppermute(part, axis, [(i, i ^ 1 << bit) for i in range(size)])  8.43 us
    all_to_all x1, starting transfers between devices, per_device(): recv = lax.all_to_all(send, 'slab', split_axis=0, concat_axis=0, tiled=True)  7.37 us
    pallas_call x1, Pallas kernels, per_device(): pl.pallas_call(backward_kernel, out_shape=struct(voxels, C), in_specs=[AN...  6.02 us
    pallas_call x1, Pallas kernels, per_device(): pl.pallas_call(functools.partial(interior_kernel, capacity), out_shape=(s...  5.2 us
    pallas_call x1, Pallas kernels, per_device(): pl.pallas_call(functools.partial(weight_grad_kernel, chunk, pieces), out_...  4.74 us
    all_to_all x1, waiting for transfers between devices, per_device(): lax.all_to_all(back_points.reshape(slabs, capacity, C), 'slab', split_axi...  4.36 us
  transfers between devices with their start and end apart: 13, of which 6 were waited for; matrix products, arithmetic and copies ran while one was open for 3% of the time, Pallas kernels for 17%

profile of v2, /device:TPU:0, one launch (start us, length us, event | category | flops | bytes accessed | tf_op | source)
XLA Modules:
  0.0 86.2 jit_solution(15833539448575478949)
XLA Ops:
  0.6 2.9 %pack.1 = (f32[16,72,128]{2,1,0:T(8,128)}, s32[8,512]{1,0:T(8,128)}) custom-call(s32[1]{0:T(128)} %bitcast.1.me_ref.me, f32[512,128]{1,0:T(8,128)} %bitcast.19, s32[1,512]{1,0:T(1,128)} %bitcast.20, s32[1,512]{1,0:T(1,128)} %slot_in.1, s32[1,512]{1,0:T(1,128)} %vox_in.1), custom_call_target="tpu_custom_call" | custom-call | flops 2000000000 | tf_op jit(solution)/shard_map/pack/pallas_call | solution.py:487
  3.5 0.0 copy-start.7
  3.6 7.4 %all-to-all-start = ((f32[16,72,128]{2,1,0:T(8,128)}), f32[16,72,128]{2,1,0:T(8,128)S(1)}, u32[]{:S(2)}, u32[]{:S(2)}) async-start(f32[16,72,128]{2,1,0:T(8,128)} %get-tuple-element.36), calls=%async_computation | async-start | bytes 1179648 | tf_op jit(solution)/shard_map/all_to_all | solution.py:500
  10.9 0.0 copy-start
  10.9 1.5 %copy-done = f32[27,128,128]{2,1,0:T(8,128)S(1)} copy-done((f32[27,128,128]{2,1,0:T(8,128)S(1)}, f32[27,128,128]{2,1,0:T(8,128)}, u32[]{:S(2)}) %copy-start) | copy-done | bytes 1769496
  12.4 0.5 weights.1.backward_in
  13.0 13.5 %all-to-all-done.recv = f32[16,72,128]{2,1,0:T(8,128)S(1)} async-done(((f32[16,72,128]{2,1,0:T(8,128)}), f32[16,72,128]{2,1,0:T(8,128)S(1)}, u32[]{:S(2)}, u32[]{:S(2)}) %all-to-all-start) | async-done | bytes 589856 | tf_op jit(solution)/shard_map/all_to_all | solution.py:500
  26.5 0.8 faces.1
  27.3 0.1 collective-permute-start
  27.4 3.1 %collective-permute-start.1 = (f32[64,128]{1,0:T(8,128)S(1)}, f32[64,128]{1,0:T(8,128)S(1)}, u32[]{:S(2)}, u32[]{:S(2)}) collective-permute-start(f32[64,128]{1,0:T(8,128)S(1)} %get-tuple-element.42), channel_id=1, source_target_pairs={{0,30},{2,4},{4,2},{6,8},{8,6},{10,12},{12,10},{14,16},{16,14},{18... | collective-permute-start | bytes 98312 | tf_op jit(solution)/shard_map/ppermute | solution.py:523
  30.5 0.0 copy-done.1
  30.5 5.2 %interior.1 = (f32[1024,128]{1,0:T(8,128)S(1)}, bf16[1024,2304]{1,0:T(8,128)(2,1)S(1)}, f32[256,128]{1,0:T(8,128)S(1)}, f32[64,128]{1,0:T(8,128)S(1)}, bf16[3,2304,256]{2,1,0:T(8,128)(2,1)S(1)}) custom-call(s32[2,27]{1,0:T(2,128)S(1)} %bitcast.14, f32[16,72,128]{2,1,0:T(8,128)S(1)} %all-to-all-done.recv, f32[27,128,128]{2,1,0:T(8,128)S(1)} %copy-done.1), custom_call_target="tpu_custom_call" | custom-call | flops 5000000000 | tf_op jit(solution)/shard_map/interior/pallas_call | solution.py:524
  35.7 0.0 collective-permute-done.from_core
  35.7 0.0 collective-permute-done.1.from_far
  35.8 2.7 %finish.1 = (f32[1024,128]{1,0:T(8,128)}, bf16[1024,256]{1,0:T(8,128)(2,1)S(1)}, bf16[2,128,2304]{2,1,0:T(8,128)(2,1)S(1)}, f32[64,128]{1,0:T(8,128)S(1)}, f32[64,128]{1,0:T(8,128)S(1)}) custom-call(s32[2,27]{1,0:T(2,128)S(1)} %bitcast.15, s32[1]{0:T(128)} %bitcast.1.me_ref.me, f32[1024,128]{1,0:T(8,128)S(1)} %get-tuple-element.39.before, ...), custom_call_target="tpu_custom_call" | custom-call | flops 2800000000 | tf_op jit(solution)/shard_map/finish/pallas_call | solution.py:545
  38.5 0.0 copy-start.4
  38.5 0.6 copy-done.4
  39.1 0.6 copy-done.5
  39.7 4.7 %weight_grad.1 = (f32[1728,128]{1,0:T(8,128)S(1)}, f32[1728,128]{1,0:T(8,128)}) custom-call(s32[1]{0:T(128)} %bitcast.1.me_ref.me, bf16[1024,2304]{1,0:T(8,128)(2,1)S(1)} %get-tuple-element.46.columns, bf16[2,128,2304]{2,1,0:T(8,128)(2,1)S(1)} %get-tuple-element.47.outer, bf16[1024,256]{1,0:T(8,128)(2,1)S(1)} %get-tuple-element.55.grads), custom_call_target="tpu_custom_call" | custom-call | flops 4000000000 | tf_op jit(solution)/shard_map/weight_grad/pallas_call | solution.py:582
  44.4 0.0 collective-permute-start.2
  44.4 1.4 %collective-permute-start.3 = (f32[64,128]{1,0:T(8,128)}, f32[64,128]{1,0:T(8,128)S(1)}, u32[]{:S(2)}, u32[]{:S(2)}) collective-permute-start(f32[64,128]{1,0:T(8,128)} %copy-done.5), channel_id=1, source_target_pairs={{0,30},{2,4},{4,2},{6,8},{8,6},{10,12},{12,10},{14,16},{16,14},{18... | collective-permute-start | bytes 98312 | tf_op jit(solution)/shard_map/ppermute | solution.py:599
  45.9 0.0 collective-permute-start.4
  45.9 1.3 %collective-permute-done.2 = f32[1728,128]{1,0:T(8,128)} collective-permute-done((f32[1728,128]{1,0:T(8,128)}, f32[1728,128]{1,0:T(8,128)}, u32[]{:S(2)}, u32[]{:S(2)}) %collective-permute-start.2) | collective-permute-done | bytes 884768 | tf_op jit(solution)/shard_map/ppermute | solution.py:594
  47.2 1.1 %dynamic-slice_add_fusion.1 = (f32[448,128]{1,0:T(8,128)S(1)}, f32[448,128]{1,0:T(8,128)S(1)}) fusion(f32[1728,128]{1,0:T(8,128)} %collective-permute-done.2, s32[]{:T(128)S(6)} %select_n.32, f32[1728,128]{1,0:T(8,128)S(1)} %get-tuple-element.49, s32[]{:T(128)S(6)} %select_n.34), kind=kLoop, calls=%fused_computation.1 | loop fusion | flops 114688 | bytes 1376264 | tf_op jit(solution)/shard_map/add | solution.py:380
  48.3 0.0 copy-start.13
  48.3 1.2 %dynamic-slice_add_fusion.2 = (f32[416,128]{1,0:T(8,128)S(1)}, f32[416,128]{1,0:T(8,128)S(1)}) fusion(f32[1728,128]{1,0:T(8,128)} %collective-permute-done.2, s32[]{:T(128)S(6)} %select_n.37, f32[1728,128]{1,0:T(8,128)S(1)} %get-tuple-element.49, s32[]{:T(128)S(6)} %select_n.35), kind=kLoop, calls=%fused_computation.3 | loop fusion | flops 106496 | bytes 1277960 | tf_op jit(solution)/shard_map/add | solution.py:380
  49.5 1.2 %collective-permute-done.3.halo_far = f32[64,128]{1,0:T(8,128)S(1)} collective-permute-done((f32[64,128]{1,0:T(8,128)}, f32[64,128]{1,0:T(8,128)S(1)}, u32[]{:S(2)}, u32[]{:S(2)}) %collective-permute-start.3) | collective-permute-done | bytes 32800 | tf_op jit(solution)/shard_map/ppermute | solution.py:599
  50.7 0.0 collective-permute-done.4.halo_core
  50.7 0.0 collective-permute-start.5
  50.7 0.2 collective-permute-start.6
  50.9 6.0 %backward.1.grad_blocks = f32[1024,128]{1,0:T(8,128)S(1)} custom-call(s32[2,27]{1,0:T(2,128)S(1)} %bitcast.16, s32[2]{0:T(128)S(1)} %bitcast.18, s32[1]{0:T(128)} %bitcast.1.me_ref.me, bf16[1024,256]{1,0:T(8,128)(2,1)S(1)} %copy-done.9, bf16[1152,1152]{1,0:T(8,128)(2,1)S(1)} %weights.1.backward_in, f32[64,128]{1,0:T(8,128)S(1)} %collective-permute-done.4.halo_core, ...), custom_call_target="tpu_custom_call" | custom-call | flops 6499999744 | tf_op jit(solution)/shard_map/backward/pallas_call | solution.py:610
  57.0 0.9 gather.1.rows
  57.8 0.0 collective-permute-done.6
  57.8 0.0 collective-permute-done.5
  57.9 1.9 %collective-permute-start.7 = (f32[224,128]{1,0:T(8,128)S(1)}, f32[224,128]{1,0:T(8,128)S(1)}, u32[]{:S(2)}, u32[]{:S(2)}) collective-permute-start(f32[224,128]{1,0:T(8,128)S(1)} %dynamic-slice_add_fusion.4.one), channel_id=1, source_target_pairs={{0,8},{2,10},{4,12},{6,14},{8,0},{10,2},{12,4},{14,6},{16,24},{18,... | collective-permute-start | bytes 344072 | tf_op jit(solution)/shard_map/ppermute | solution.py:594
  59.9 0.0 copy-start.18
  59.9 0.0 copy-start.14
  59.9 2.1 %collective-permute-start.8 = (f32[208,128]{1,0:T(8,128)S(1)}, f32[208,128]{1,0:T(8,128)S(1)}, u32[]{:S(2)}, u32[]{:S(2)}) collective-permute-start(f32[208,128]{1,0:T(8,128)S(1)} %dynamic-slice_add_fusion.5.two), channel_id=1, source_target_pairs={{0,4},{2,6},{4,0},{6,2},{8,12},{10,14},{12,8},{14,10},{16,20},{18,... | collective-permute-start | bytes 319496 | tf_op jit(solution)/shard_map/ppermute | solution.py:594
  62.0 3.6 %all-to-all-start.1 = ((f32[16,64,128]{2,1,0:T(8,128)}), f32[16,64,128]{2,1,0:T(8,128)S(1)}, u32[]{:S(2)}, u32[]{:S(2)}) async-start(f32[16,64,128]{2,1,0:T(8,128)} %bitcast.12), calls=%async_computation.1 | async-start | bytes 1048576 | tf_op jit(solution)/shard_map/all_to_all | solution.py:650
  65.6 0.0 collective-permute-done.8
  65.6 0.0 collective-permute-done.7
  65.7 1.6 %collective-permute-start.9 = (f32[432,128]{1,0:T(8,128)S(1)}, f32[432,128]{1,0:T(8,128)S(1)}, u32[]{:S(2)}, u32[]{:S(2)}) collective-permute-start(f32[432,128]{1,0:T(8,128)S(1)} %pad_maximum_fusion.kept), channel_id=1, source_target_pairs={{0,1},{1,0},{2,3},{3,2},{4,5},{5,4},{6,7},{7,6},{8,9},{9,8},{10,11... | collective-permute-start | bytes 663560 | tf_op jit(solution)/shard_map/ppermute | solution.py:594
  67.3 6.1 %collective-permute-done.9.arrived = f32[432,128]{1,0:T(8,128)S(1)} collective-permute-done((f32[432,128]{1,0:T(8,128)S(1)}, f32[432,128]{1,0:T(8,128)S(1)}, u32[]{:S(2)}, u32[]{:S(2)}) %collective-permute-start.9) | collective-permute-done | bytes 221216 | tf_op jit(solution)/shard_map/ppermute | solution.py:594
  73.4 2.7 %collective-permute-start.10 = (f32[216,128]{1,0:T(8,128)S(1)}, f32[216,128]{1,0:T(8,128)S(1)}, u32[]{:S(2)}, u32[]{:S(2)}) collective-permute-start(f32[216,128]{1,0:T(8,128)S(1)} %get-tuple-element.61), channel_id=1, source_target_pairs={{0,16},{2,18},{4,20},{6,22},{8,24},{10,26},{12,28},{14,30},{16,0},... | collective-permute-start | bytes 331784 | tf_op jit(solution)/shard_map/ppermute | solution.py:594
  76.1 4.4 %all-to-all-done.1 = f32[16,64,128]{2,1,0:T(8,128)S(1)} async-done(((f32[16,64,128]{2,1,0:T(8,128)}), f32[16,64,128]{2,1,0:T(8,128)S(1)}, u32[]{:S(2)}, u32[]{:S(2)}) %all-to-all-start.1) | async-done | bytes 524320 | tf_op jit(solution)/shard_map/all_to_all | solution.py:650
  80.5 1.7 %unpack.1 = f32[512,128]{1,0:T(8,128)} custom-call(f32[1024,128]{1,0:T(8,128)S(1)} %bitcast.11, s32[8,512]{1,0:T(8,128)S(1)} %copy-done.12), custom_call_target="tpu_custom_call" | custom-call | flops 1700000000 | tf_op jit(solution)/shard_map/unpack/pallas_call | solution.py:653
  82.2 3.3 %collective-permute-done.10 = f32[216,128]{1,0:T(8,128)S(1)} collective-permute-done((f32[216,128]{1,0:T(8,128)S(1)}, f32[216,128]{1,0:T(8,128)S(1)}, u32[]{:S(2)}, u32[]{:S(2)}) %collective-permute-start.10) | collective-permute-done | bytes 110624 | tf_op jit(solution)/shard_map/ppermute | solution.py:594
  85.5 0.7 add_multiply_fusion
  (35 shorter events, 0.2 us)
Async XLA Ops:
  3.5 22.9 %copy-start.7 = (s32[1,1,2,1]{2,3,1,0:T(1,128)S(1)}, s32[1,1,2,1]{2,3,1,0:T(1,128)}, u32[]{:S(2)}) copy-start(s32[1,1,2,1]{2,3,1,0:T(1,128)} %param.12) | copy-start | bytes 28
  3.6 22.9 %all-to-all-start = ((f32[16,72,128]{2,1,0:T(8,128)}), f32[16,72,128]{2,1,0:T(8,128)S(1)}, u32[]{:S(2)}, u32[]{:S(2)}) async-start(f32[16,72,128]{2,1,0:T(8,128)} %get-tuple-element.36), calls=%async_computation | async-start | bytes 1179648 | tf_op jit(solution)/shard_map/all_to_all | solution.py:500
  10.9 1.5 %copy-start = (f32[27,128,128]{2,1,0:T(8,128)S(1)}, f32[27,128,128]{2,1,0:T(8,128)}, u32[]{:S(2)}) copy-start(f32[27,128,128]{2,1,0:T(8,128)} %taps_in) | copy-start | bytes 5308420
  12.4 18.1 %copy-start.6 = (s32[1,2,27]{2,1,0:T(2,128)S(1)}, s32[1,2,27]{2,1,0:T(2,128)}, u32[]{:S(2)}) copy-start(s32[1,2,27]{2,1,0:T(2,128)} %param.13) | copy-start | bytes 652
  26.5 4.0 %copy-start.1 = (f32[27,128,128]{2,1,0:T(8,128)S(1)}, f32[27,128,128]{2,1,0:T(8,128)}, u32[]{:S(2)}) copy-start(f32[27,128,128]{2,1,0:T(8,128)} %taps_in) | copy-start | bytes 5308420
  27.3 8.5 %collective-permute-start = (f32[64,128]{1,0:T(8,128)S(1)}, f32[64,128]{1,0:T(8,128)S(1)}, u32[]{:S(2)}, u32[]{:S(2)}) collective-permute-start(f32[64,128]{1,0:T(8,128)S(1)} %get-tuple-element.41), channel_id=1, source_target_pairs={{0,2},{2,0},{4,6},{6,4},{8,10},{10,8},{12,14},{14,12},{16,18},{18,... | collective-permute-start | bytes 98312 | tf_op jit(solution)/shard_map/ppermute | solution.py:522
  27.4 8.4 %collective-permute-start.1 = (f32[64,128]{1,0:T(8,128)S(1)}, f32[64,128]{1,0:T(8,128)S(1)}, u32[]{:S(2)}, u32[]{:S(2)}) collective-permute-start(f32[64,128]{1,0:T(8,128)S(1)} %get-tuple-element.42), channel_id=1, source_target_pairs={{0,30},{2,4},{4,2},{6,8},{8,6},{10,12},{12,10},{14,16},{16,14},{18... | collective-permute-start | bytes 98312 | tf_op jit(solution)/shard_map/ppermute | solution.py:523
  30.5 5.2 %copy-start.3 = (f32[1,1024,128]{2,1,0:T(8,128)S(1)}, f32[1,1024,128]{2,1,0:T(8,128)}, u32[]{:S(2)}) copy-start(f32[1,1024,128]{2,1,0:T(8,128)} %param.15) | copy-start | bytes 1572868
  35.7 2.7 %copy-start.10 = (f32[64,128]{1,0:T(8,128)}, f32[64,128]{1,0:T(8,128)S(1)}, u32[]{:S(2)}) copy-start(f32[64,128]{1,0:T(8,128)S(1)} %get-tuple-element.58.codes) | copy-start | bytes 98308
  38.5 0.6 copy-start.4
  39.1 0.6 copy-start.5
  39.7 4.7 %copy-start.8 = (bf16[1024,256]{1,0:T(8,128)(2,1)}, bf16[1024,256]{1,0:T(8,128)(2,1)S(1)}, u32[]{:S(2)}) copy-start(bf16[1024,256]{1,0:T(8,128)(2,1)S(1)} %get-tuple-element.55.grads) | copy-start | bytes 1572868
  44.4 2.8 %collective-permute-start.2 = (f32[1728,128]{1,0:T(8,128)}, f32[1728,128]{1,0:T(8,128)}, u32[]{:S(2)}, u32[]{:S(2)}) collective-permute-start(f32[1728,128]{1,0:T(8,128)} %get-tuple-element.50), channel_id=1, source_target_pairs={{0,2},{2,0},{4,6},{6,4},{8,10},{10,8},{12,14},{14,12},{16,18},{18,... | collective-permute-start | bytes 2654216 | tf_op jit(solution)/shard_map/ppermute | solution.py:594
  44.4 6.5 %copy-start.9 = (bf16[1024,256]{1,0:T(8,128)(2,1)S(1)}, bf16[1024,256]{1,0:T(8,128)(2,1)}, u32[]{:S(2)}) copy-start(bf16[1024,256]{1,0:T(8,128)(2,1)} %copy-done.8) | copy-start | bytes 1572868
  44.4 6.3 %collective-permute-start.3 = (f32[64,128]{1,0:T(8,128)}, f32[64,128]{1,0:T(8,128)S(1)}, u32[]{:S(2)}, u32[]{:S(2)}) collective-permute-start(f32[64,128]{1,0:T(8,128)} %copy-done.5), channel_id=1, source_target_pairs={{0,30},{2,4},{4,2},{6,8},{8,6},{10,12},{12,10},{14,16},{16,14},{18... | collective-permute-start | bytes 98312 | tf_op jit(solution)/shard_map/ppermute | solution.py:599
  45.9 4.9 %collective-permute-start.4 = (f32[64,128]{1,0:T(8,128)}, f32[64,128]{1,0:T(8,128)S(1)}, u32[]{:S(2)}, u32[]{:S(2)}) collective-permute-start(f32[64,128]{1,0:T(8,128)} %copy-done.4), channel_id=1, source_target_pairs={{0,2},{2,0},{4,6},{6,4},{8,10},{10,8},{12,14},{14,12},{16,18},{18,... | collective-permute-start | bytes 98312 | tf_op jit(solution)/shard_map/ppermute | solution.py:600
  48.3 9.5 %copy-start.13 = (f32[448,128]{1,0:T(8,128)}, f32[448,128]{1,0:T(8,128)S(1)}, u32[]{:S(2)}) copy-start(f32[448,128]{1,0:T(8,128)S(1)} %get-tuple-element.67) | copy-start | bytes 688132
  49.5 10.3 %copy-start.15 = (f32[416,128]{1,0:T(8,128)}, f32[416,128]{1,0:T(8,128)S(1)}, u32[]{:S(2)}) copy-start(f32[416,128]{1,0:T(8,128)S(1)} %get-tuple-element.69) | copy-start | bytes 638980
  50.7 6.2 %copy-start.11 = (f32[64,128]{1,0:T(8,128)S(1)}, f32[64,128]{1,0:T(8,128)}, u32[]{:S(2)}) copy-start(f32[64,128]{1,0:T(8,128)} %copy-done.10) | copy-start | bytes 98308
  50.7 7.1 %collective-permute-start.5 = (f32[448,128]{1,0:T(8,128)S(1)}, f32[448,128]{1,0:T(8,128)S(1)}, u32[]{:S(2)}, u32[]{:S(2)}) collective-permute-start(f32[448,128]{1,0:T(8,128)S(1)} %get-tuple-element.53), channel_id=1, source_target_pairs={{0,4},{2,6},{4,0},{6,2},{8,12},{10,14},{12,8},{14,10},{16,20},{18,... | collective-permute-start | bytes 688136 | tf_op jit(solution)/shard_map/ppermute | solution.py:594
  50.7 7.1 %collective-permute-start.6 = (f32[416,128]{1,0:T(8,128)S(1)}, f32[416,128]{1,0:T(8,128)S(1)}, u32[]{:S(2)}, u32[]{:S(2)}) collective-permute-start(f32[416,128]{1,0:T(8,128)S(1)} %get-tuple-element.54), channel_id=1, source_target_pairs={{0,8},{2,10},{4,12},{6,14},{8,0},{10,2},{12,4},{14,6},{16,24},{18,... | collective-permute-start | bytes 638984 | tf_op jit(solution)/shard_map/ppermute | solution.py:594
  57.8 4.2 %copy-start.2 = (f32[1024,128]{1,0:T(8,128)}, f32[1024,128]{1,0:T(8,128)S(1)}, u32[]{:S(2)}) copy-start(f32[1024,128]{1,0:T(8,128)S(1)} %gather.1.rows) | copy-start | bytes 1572868
  57.9 4.1 %copy-start.17 = (f32[224,128]{1,0:T(8,128)}, f32[224,128]{1,0:T(8,128)S(1)}, u32[]{:S(2)}) copy-start(f32[224,128]{1,0:T(8,128)S(1)} %dynamic-slice_add_fusion.4.one) | copy-start | bytes 344068
  57.9 7.7 %collective-permute-start.7 = (f32[224,128]{1,0:T(8,128)S(1)}, f32[224,128]{1,0:T(8,128)S(1)}, u32[]{:S(2)}, u32[]{:S(2)}) collective-permute-start(f32[224,128]{1,0:T(8,128)S(1)} %dynamic-slice_add_fusion.4.one), channel_id=1, source_target_pairs={{0,8},{2,10},{4,12},{6,14},{8,0},{10,2},{12,4},{14,6},{16,24},{18,... | collective-permute-start | bytes 344072 | tf_op jit(solution)/shard_map/ppermute | solution.py:594
  59.9 2.1 %copy-start.18 = (f32[208,128]{1,0:T(8,128)}, f32[208,128]{1,0:T(8,128)S(1)}, u32[]{:S(2)}) copy-start(f32[208,128]{1,0:T(8,128)S(1)} %dynamic-slice_add_fusion.5.two) | copy-start | bytes 319492
  59.9 5.7 %copy-start.16 = (f32[416,128]{1,0:T(8,128)S(1)}, f32[416,128]{1,0:T(8,128)}, u32[]{:S(2)}) copy-start(f32[416,128]{1,0:T(8,128)} %copy-done.15) | copy-start | bytes 638980
  59.9 5.8 %copy-start.14 = (f32[448,128]{1,0:T(8,128)S(1)}, f32[448,128]{1,0:T(8,128)}, u32[]{:S(2)}) copy-start(f32[448,128]{1,0:T(8,128)} %copy-done.13) | copy-start | bytes 688132
  59.9 5.7 %collective-permute-start.8 = (f32[208,128]{1,0:T(8,128)S(1)}, f32[208,128]{1,0:T(8,128)S(1)}, u32[]{:S(2)}, u32[]{:S(2)}) collective-permute-start(f32[208,128]{1,0:T(8,128)S(1)} %dynamic-slice_add_fusion.5.two), channel_id=1, source_target_pairs={{0,4},{2,6},{4,0},{6,2},{8,12},{10,14},{12,8},{14,10},{16,20},{18,... | collective-permute-start | bytes 319496 | tf_op jit(solution)/shard_map/ppermute | solution.py:594
  62.0 18.5 %all-to-all-start.1 = ((f32[16,64,128]{2,1,0:T(8,128)}), f32[16,64,128]{2,1,0:T(8,128)S(1)}, u32[]{:S(2)}, u32[]{:S(2)}) async-start(f32[16,64,128]{2,1,0:T(8,128)} %bitcast.12), calls=%async_computation.1 | async-start | bytes 1048576 | tf_op jit(solution)/shard_map/all_to_all | solution.py:650
  65.7 7.7 %collective-permute-start.9 = (f32[432,128]{1,0:T(8,128)S(1)}, f32[432,128]{1,0:T(8,128)S(1)}, u32[]{:S(2)}, u32[]{:S(2)}) collective-permute-start(f32[432,128]{1,0:T(8,128)S(1)} %pad_maximum_fusion.kept), channel_id=1, source_target_pairs={{0,1},{1,0},{2,3},{3,2},{4,5},{5,4},{6,7},{7,6},{8,9},{9,8},{10,11... | collective-permute-start | bytes 663560 | tf_op jit(solution)/shard_map/ppermute | solution.py:594
  73.4 7.1 %copy-start.12 = (s32[8,512]{1,0:T(8,128)S(1)}, s32[8,512]{1,0:T(8,128)}, u32[]{:S(2)}) copy-start(s32[8,512]{1,0:T(8,128)} %get-tuple-element.63.dest) | copy-start | bytes 49156
  73.4 12.1 %collective-permute-start.10 = (f32[216,128]{1,0:T(8,128)S(1)}, f32[216,128]{1,0:T(8,128)S(1)}, u32[]{:S(2)}, u32[]{:S(2)}) collective-permute-start(f32[216,128]{1,0:T(8,128)S(1)} %get-tuple-element.61), channel_id=1, source_target_pairs={{0,16},{2,18},{4,20},{6,22},{8,24},{10,26},{12,28},{14,30},{16,0},... | collective-permute-start | bytes 331784 | tf_op jit(solution)/shard_map/ppermute | solution.py:594

commit v3 on v2

--- a/solution.py
+++ b/solution.py
@@ -259,22 +259,14 @@
 
 
 def finish_kernel(
-    names_in, me, before, faces, from_core, from_far, forward, backward_in, cotangent_in,
-    activated, grads, outer, to_core, to_far,
-    names, faces_low, faces_high, pre, cotangent, backward, edge_back, low_grads, high_grads, sems,
+    names_in, me, before, faces, from_core, from_far, forward, backward, cotangent_in,
+    activated_out, grads, outer, to_core, to_far,
+    names, faces_low, faces_high, pre, cotangent, activated, edge_back, low_grads, high_grads, sems,
 ):
     copies = [
         pltpu.make_async_copy(names_in, names, sems.at[0]),
         pltpu.make_async_copy(cotangent_in, cotangent, sems.at[1]),
     ]
-    for n, i in enumerate((0, 2)):
-        for part in (0, 3, 6):
-            rows = pl.ds((i + part) * C, C)
-            copies.append(
-                pltpu.make_async_copy(
-                    backward_in.at[rows], backward.at[pl.ds((3 * n + part // 3) * C, C)], sems.at[len(copies)]
-                )
-            )
     for copy in copies:
         copy.start()
     even = jnp.bitwise_and(me[0], 1) == 0
@@ -303,16 +295,17 @@
     value = pre[...]
     gate = jax.nn.sigmoid(value)
     activated[...] = value * gate
+    copies.append(pltpu.make_async_copy(activated, activated_out, sems.at[2]))
+    copies[2].start()
     copies[1].wait()
     high, low = split(cotangent[...] * gate * (1.0 + value * (1.0 - gate)))
     grads[:, :C] = high
     grads[:, C:] = low
-    for copy in copies[2:]:
-        copy.wait()
     for n, (i, x, target) in enumerate(((0, 0, low_grads), (2, E - 1, high_grads))):
         both = jnp.concatenate([grads[b * VOX + x * FACE : b * VOX + (x + 1) * FACE, :] for b in range(NB)], axis=0)
         three = jnp.concatenate([both, both[:, :C]], axis=1)
-        edge_back[...] = mm(three, backward[3 * n * C : 3 * (n + 1) * C, :])
+        matching = jnp.concatenate([backward[(i + part) * C : (i + part + 1) * C, :] for part in (0, 3, 6)], axis=0)
+        edge_back[...] = mm(three, matching)
         for b in range(NB):
             sums = column_sums(lambda jk: edge_back[b * FACE : (b + 1) * FACE, jk * C : (jk + 1) * C])
             spread_plane(names, b, i, sums, target, FACE, 0, 4)
@@ -320,6 +313,7 @@
     right = high_grads[3 * FACE : 4 * FACE]
     to_core[...] = jnp.where(even, right, left)
     to_far[...] = jnp.where(even, left, right)
+    copies[2].wait()
 
 
 def face_grads(grads, i):
@@ -336,7 +330,7 @@
     return jnp.concatenate(rows, axis=0)
 
 
-def weight_grad_kernel(chunk, pieces, me, columns, outer, grads, kept, sent, ordered):
+def weight_grad_kernel(chunk, pieces, me, columns, outer, grads, kept_a, sent_a, kept_b, sent_b, ordered):
     tn = ((0,), (0,))
     shifted = [shifted_grads(grads, i) for i in range(3)]
     wide = jnp.concatenate(shifted, axis=1)
@@ -357,7 +351,7 @@
             ordered[i * COLS + start : i * COLS + start + 3 * C] = value
     first = jnp.bitwise_and(me[0], 1) == 0
     for n, runs in enumerate(pieces):
-        for start, size, to in runs:
+        for (start, size, to), kept, sent in zip(runs, (kept_a, kept_b), (sent_a, sent_b)):
             start = 2 * n * chunk + start
             even = ordered[start : start + size]
             odd = ordered[start + chunk : start + chunk + size]
@@ -551,19 +545,19 @@
             struct(FACE, C),
             struct(FACE, C),
         ),
-        in_specs=[ANY, SMEM] + [VMEM] * 5 + [ANY] * 2,
-        out_specs=(VMEM,) * 5,
+        in_specs=[ANY, SMEM] + [VMEM] * 6 + [ANY],
+        out_specs=(ANY,) + (VMEM,) * 4,
         scratch_shapes=[
             pltpu.SMEM((NB, 27), jnp.int32),
             pltpu.VMEM((5 * FACE, C), f32),
             pltpu.VMEM((5 * FACE, C), f32),
             pltpu.VMEM((voxels, C), f32),
             pltpu.VMEM((voxels, C), f32),
-            pltpu.VMEM((6 * C, COLS), bf16),
+            pltpu.VMEM((voxels, C), f32),
             pltpu.VMEM((NB * FACE, COLS), f32),
             pltpu.VMEM((5 * FACE, C), f32),
             pltpu.VMEM((5 * FACE, C), f32),
-            pltpu.SemaphoreType.DMA((8,)),
+            pltpu.SemaphoreType.DMA((3,)),
         ],
         compiler_params=params(14),
         name="finish",
@@ -575,17 +569,18 @@
     pieces = tuple(
         (
             (0, cut, place(2 * n, orders[0]) * cut),
-            (cut, chunk - cut, slabs // 2 * cut + place(2 * n, orders[1]) * (chunk - cut)),
+            (cut, chunk - cut, place(2 * n, orders[1]) * (chunk - cut)),
         )
         for n in range(slabs // 2)
     )
-    kept, sent = pl.pallas_call(
+    sizes = (slabs // 2 * cut, slabs // 2 * (chunk - cut))
+    kept_a, sent_a, kept_b, sent_b = pl.pallas_call(
         functools.partial(weight_grad_kernel, chunk, pieces),
-        out_shape=(struct(27 * C // 2, C),) * 2,
+        out_shape=(struct(sizes[0], C),) * 2 + (struct(sizes[1], C),) * 2,
         in_specs=[SMEM] + [VMEM] * 3,
-        out_specs=(VMEM, VMEM),
+        out_specs=(VMEM,) * 4,
         scratch_shapes=[pltpu.VMEM((27 * C, C), f32)],
-        compiler_params=params(14),
+        compiler_params=params(9),
         name="weight_grad",
         cost_estimate=cost(4),
     )(me.reshape(1), columns, outer, grads)
@@ -598,14 +593,11 @@
 
     halo_far = lax.ppermute(edge_far, "slab", far_pairs)
     halo_core = lax.ppermute(edge_core, "slab", core_pairs)
-    arrived = swapped(sent, "slab", 0)
-    mids, sides = slabs // 2 * cut, (side(1), side(2))
-    halves = (mids // 2, (kept.shape[0] - mids) // 2)
-    sent = [part_of(kept, arrived, (0, mids)[q] + (1 - sides[q]) * halves[q], halves[q]) for q in range(2)]
-    sent[0], sent[1], grads, halo_far, halo_core = lax.optimization_barrier(
-        (sent[0], sent[1], grads, halo_far, halo_core)
-    )
-    kept = [part_of(kept, arrived, (0, mids)[q] + sides[q] * halves[q], halves[q]) for q in range(2)]
+    kept, arrived = (kept_a, kept_b), (swapped(sent_a, "slab", 0), swapped(sent_b, "slab", 0))
+    sides, halves = (side(1), side(2)), [size // 2 for size in sizes]
+    sent = [part_of(kept[q], arrived[q], (1 - sides[q]) * halves[q], halves[q]) for q in range(2)]
+    sent[0], sent[1], grads = lax.optimization_barrier((sent[0], sent[1], grads))
+    kept = [part_of(kept[q], arrived[q], sides[q] * halves[q], halves[q]) for q in range(2)]
     arrived = [swapped(sent[q], "slab", (1, 2)[q]) for q in range(2)]
     grad_blocks = pl.pallas_call(
         backward_kernel,
@@ -643,6 +635,7 @@
         in_specs=[ANY] * 3,
         out_specs=ANY,
         input_output_aliases={0: 0},
+        compiler_params=params(1),
         name="pass",
         cost_estimate=cost(2.2),
     )(back_points, *sent)

time: 86.6 us -> 83.7 us (0.967)
  waiting for transfers between devices: 29.9 us -> 28.6 us
    ppermute x7 -> x8, waiting for transfers between devices: 10.8 us -> 9.65 us  [swapped(): return lax.ppermute(part, axis, [(i, i ^ 1 << bit) for i in range(size)])]
    unnamed x38 -> x36, local copies, waits for them, and re-layouts: 2.75 us -> 1.89 us
    ppermute x7 -> x8, starting transfers between devices: 8.43 us -> 7.72 us  [swapped(): return lax.ppermute(part, axis, [(i, i ^ 1 << bit) for i in range(size)])]
  transfers between devices with their start and end apart: 13 -> 14, of which waited for: 6 -> 6; matrix products, arithmetic and copies ran while one was open for 3% -> 3% of each run, Pallas kernels for 17% -> 18%
where the time goes in v3:
time: 83.7 us; the launch traced here: 83.2 us
  waiting for transfers between devices  28.6 us (34%)
  Pallas kernels  25.5 us (30%)
  starting transfers between devices  23.3 us (28%)
  other arithmetic  3.08 us (4%)
  local copies, waits for them, and re-layouts  1.89 us (2%)
  between operations  0.92 us (1%)
    all_to_all x1, waiting for transfers between devices, per_device(): recv = lax.all_to_all(send, 'slab', split_axis=0, concat_axis=0, tiled=True)  13.5 us
    ppermute x8, waiting for transfers between devices, swapped(): return lax.ppermute(part, axis, [(i, i ^ 1 << bit) for i in range(size)])  9.65 us
    ppermute x8, starting transfers between devices, swapped(): return lax.ppermute(part, axis, [(i, i ^ 1 << bit) for i in range(size)])  7.72 us
    all_to_all x1, starting transfers between devices, per_device(): recv = lax.all_to_all(send, 'slab', split_axis=0, concat_axis=0, tiled=True)  7.37 us
    pallas_call x1, Pallas kernels, per_device(): pl.pallas_call(backward_kernel, out_shape=struct(voxels, C), in_specs=[AN...  5.97 us
    pallas_call x1, Pallas kernels, per_device(): pl.pallas_call(functools.partial(interior_kernel, capacity), out_shape=(s...  5.2 us
    pallas_call x1, Pallas kernels, per_device(): pl.pallas_call(functools.partial(weight_grad_kernel, chunk, pieces), out_...  4.71 us
    all_to_all x1, waiting for transfers between devices, per_device(): lax.all_to_all(back_points.reshape(slabs, capacity, C), 'slab', split_axi...  4.35 us
  transfers between devices with their start and end apart: 14, of which 6 were waited for; matrix products, arithmetic and copies ran while one was open for 3% of the time, Pallas kernels for 18%

profile of v3, /device:TPU:0, one launch (start us, length us, event | category | flops | bytes accessed | tf_op | source)
XLA Modules:
  0.0 83.2 jit_solution(2256796045604967645)
XLA Ops:
  0.6 2.9 %pack.1 = (f32[16,72,128]{2,1,0:T(8,128)}, s32[8,512]{1,0:T(8,128)}) custom-call(s32[1]{0:T(128)} %bitcast.1.me_ref.me, f32[512,128]{1,0:T(8,128)} %bitcast.18, s32[1,512]{1,0:T(1,128)} %bitcast.19, s32[1,512]{1,0:T(1,128)} %slot_in.1, s32[1,512]{1,0:T(1,128)} %vox_in.1), custom_call_target="tpu_custom_call" | custom-call | flops 2000000000 | tf_op jit(solution)/shard_map/pack/pallas_call | solution.py:481
  3.5 0.0 copy-start.6
  3.6 7.4 %all-to-all-start = ((f32[16,72,128]{2,1,0:T(8,128)}), f32[16,72,128]{2,1,0:T(8,128)S(1)}, u32[]{:S(2)}, u32[]{:S(2)}) async-start(f32[16,72,128]{2,1,0:T(8,128)} %get-tuple-element.36), calls=%async_computation | async-start | bytes 1179648 | tf_op jit(solution)/shard_map/all_to_all | solution.py:494
  10.9 0.0 copy-start
  10.9 1.5 %copy-done = f32[27,128,128]{2,1,0:T(8,128)S(1)} copy-done((f32[27,128,128]{2,1,0:T(8,128)S(1)}, f32[27,128,128]{2,1,0:T(8,128)}, u32[]{:S(2)}) %copy-start) | copy-done | bytes 1769496
  12.4 0.5 weights.1.backward.backward_in
  13.0 13.5 %all-to-all-done.recv = f32[16,72,128]{2,1,0:T(8,128)S(1)} async-done(((f32[16,72,128]{2,1,0:T(8,128)}), f32[16,72,128]{2,1,0:T(8,128)S(1)}, u32[]{:S(2)}, u32[]{:S(2)}) %all-to-all-start) | async-done | bytes 589856 | tf_op jit(solution)/shard_map/all_to_all | solution.py:494
  26.5 0.8 faces.1
  27.3 0.1 collective-permute-start
  27.4 3.1 %collective-permute-start.1 = (f32[64,128]{1,0:T(8,128)S(1)}, f32[64,128]{1,0:T(8,128)S(1)}, u32[]{:S(2)}, u32[]{:S(2)}) collective-permute-start(f32[64,128]{1,0:T(8,128)S(1)} %get-tuple-element.42), channel_id=1, source_target_pairs={{0,30},{2,4},{4,2},{6,8},{8,6},{10,12},{12,10},{14,16},{16,14},{18... | collective-permute-start | bytes 98312 | tf_op jit(solution)/shard_map/ppermute | solution.py:517
  30.5 5.2 %interior.1 = (f32[1024,128]{1,0:T(8,128)S(1)}, bf16[1024,2304]{1,0:T(8,128)(2,1)S(1)}, f32[256,128]{1,0:T(8,128)S(1)}, f32[64,128]{1,0:T(8,128)S(1)}, bf16[3,2304,256]{2,1,0:T(8,128)(2,1)S(1)}) custom-call(s32[2,27]{1,0:T(2,128)S(1)} %bitcast.13, f32[16,72,128]{2,1,0:T(8,128)S(1)} %all-to-all-done.recv, f32[27,128,128]{2,1,0:T(8,128)S(1)} %copy-done.1), custom_call_target="tpu_custom_call" | custom-call | flops 5000000000 | tf_op jit(solution)/shard_map/interior/pallas_call | solution.py:518
  35.7 0.0 collective-permute-done.from_core
  35.7 0.0 collective-permute-done.1.from_far
  35.8 2.0 %finish.1 = (f32[1024,128]{1,0:T(8,128)}, bf16[1024,256]{1,0:T(8,128)(2,1)S(1)}, bf16[2,128,2304]{2,1,0:T(8,128)(2,1)S(1)}, f32[64,128]{1,0:T(8,128)S(1)}, f32[64,128]{1,0:T(8,128)S(1)}) custom-call(s32[2,27]{1,0:T(2,128)S(1)} %bitcast.14, s32[1]{0:T(128)} %bitcast.1.me_ref.me, f32[1024,128]{1,0:T(8,128)S(1)} %get-tuple-element.39.before, ...), custom_call_target="tpu_custom_call" | custom-call | flops 2800000000 | tf_op jit(solution)/shard_map/finish/pallas_call | solution.py:539
  37.8 0.0 copy-start.3
  37.8 0.0 copy-start.4
  37.8 4.7 %weight_grad.1 = (f32[896,128]{1,0:T(8,128)S(1)}, f32[896,128]{1,0:T(8,128)}, f32[832,128]{1,0:T(8,128)S(1)}, f32[832,128]{1,0:T(8,128)}) custom-call(s32[1]{0:T(128)} %bitcast.1.me_ref.me, bf16[1024,2304]{1,0:T(8,128)(2,1)S(1)} %get-tuple-element.46.columns, bf16[2,128,2304]{2,1,0:T(8,128)(2,1)S(1)} %get-tuple-element.47.outer, ...), custom_call_target="tpu_custom_call" | custom-call | flops 4000000000 | tf_op jit(solution)/shard_map/weight_grad/pallas_call | solution.py:577
  42.5 0.1 collective-permute-start.3
  42.6 0.5 collective-permute-start.2
  43.1 0.1 collective-permute-start.6
  43.2 1.4 %collective-permute-start.7 = (f32[64,128]{1,0:T(8,128)}, f32[64,128]{1,0:T(8,128)S(1)}, u32[]{:S(2)}, u32[]{:S(2)}) collective-permute-start(f32[64,128]{1,0:T(8,128)} %copy-done.3), channel_id=1, source_target_pairs={{0,30},{2,4},{4,2},{6,8},{8,6},{10,12},{12,10},{14,16},{16,14},{18... | collective-permute-start | bytes 98312 | tf_op jit(solution)/shard_map/ppermute | solution.py:594
  44.5 0.2 collective-permute-done.3
  44.7 1.1 %dynamic-slice_add_fusion.2 = (f32[416,128]{1,0:T(8,128)S(1)}, f32[416,128]{1,0:T(8,128)S(1)}) fusion(f32[832,128]{1,0:T(8,128)} %collective-permute-done.3, s32[]{:T(128)S(6)} %select_n.37, f32[832,128]{1,0:T(8,128)S(1)} %get-tuple-element.51, s32[]{:T(128)S(6)} %select_n.35), kind=kLoop, calls=%fused_computation.3 | loop fusion | flops 106496 | bytes 1277960 | tf_op jit(solution)/shard_map/add | solution.py:374
  45.8 0.0 collective-permute-done.2
  45.8 1.2 %dynamic-slice_add_fusion.1 = (f32[448,128]{1,0:T(8,128)S(1)}, f32[448,128]{1,0:T(8,128)S(1)}) fusion(f32[896,128]{1,0:T(8,128)} %collective-permute-done.2, s32[]{:T(128)S(6)} %select_n.32, f32[896,128]{1,0:T(8,128)S(1)} %get-tuple-element.49, s32[]{:T(128)S(6)} %select_n.34), kind=kLoop, calls=%fused_computation.1 | loop fusion | flops 114688 | bytes 1376264 | tf_op jit(solution)/shard_map/add | solution.py:374
  47.0 0.6 collective-permute-start.4
  47.6 0.7 collective-permute-start.5
  48.4 0.0 collective-permute-done.6.halo_core
  48.4 1.0 %collective-permute-done.7.halo_far = f32[64,128]{1,0:T(8,128)S(1)} collective-permute-done((f32[64,128]{1,0:T(8,128)}, f32[64,128]{1,0:T(8,128)S(1)}, u32[]{:S(2)}, u32[]{:S(2)}) %collective-permute-start.7) | collective-permute-done | bytes 32800 | tf_op jit(solution)/shard_map/ppermute | solution.py:594
  49.4 6.0 %backward.1.grad_blocks = f32[1024,128]{1,0:T(8,128)S(1)} custom-call(s32[2,27]{1,0:T(2,128)S(1)} %bitcast.15, s32[2]{0:T(128)S(1)} %bitcast.17, s32[1]{0:T(128)} %bitcast.1.me_ref.me, bf16[1024,256]{1,0:T(8,128)(2,1)S(1)} %copy-done.8, bf16[1152,1152]{1,0:T(8,128)(2,1)S(1)} %weights.1.backward.backward_in, f32[64,128]{1,0:T(8,128)S(1)} %collective-permute-done.6.halo_core, ...), custom_call_target="tpu_custom_call" | custom-call | flops 6499999744 | tf_op jit(solution)/shard_map/backward/pallas_call | solution.py:602
  55.4 1.6 %gather.1.rows = f32[1024,128]{1,0:T(8,128)} custom-call(f32[1024,128]{1,0:T(8,128)S(1)} %backward.1.grad_blocks, f32[64,128]{1,0:T(8,128)S(1)} %copy-done.10), custom_call_target="tpu_custom_call" | custom-call | flops 2200000000 | tf_op jit(solution)/shard_map/gather/pallas_call | solution.py:619
  57.1 0.0 collective-permute-done.5
  57.1 0.0 collective-permute-done.4
  57.1 0.0 copy-start.14
  57.1 0.4 collective-permute-start.8
  57.5 0.3 copy-done.14
  57.8 0.0 copy-done.16
  57.9 0.0 copy-start.15
  57.9 1.2 %collective-permute-start.9 = (f32[208,128]{1,0:T(8,128)S(1)}, f32[208,128]{1,0:T(8,128)S(1)}, u32[]{:S(2)}, u32[]{:S(2)}) collective-permute-start(f32[208,128]{1,0:T(8,128)S(1)} %dynamic-slice_add_fusion.5.two), channel_id=1, source_target_pairs={{0,4},{2,6},{4,0},{6,2},{8,12},{10,14},{12,8},{14,10},{16,20},{18,... | collective-permute-start | bytes 319496 | tf_op jit(solution)/shard_map/ppermute | solution.py:589
  59.1 3.6 %all-to-all-start.1 = ((f32[16,64,128]{2,1,0:T(8,128)}), f32[16,64,128]{2,1,0:T(8,128)S(1)}, u32[]{:S(2)}, u32[]{:S(2)}) async-start(f32[16,64,128]{2,1,0:T(8,128)} %bitcast.8), calls=%async_computation.1 | async-start | bytes 1048576 | tf_op jit(solution)/shard_map/all_to_all | solution.py:643
  62.6 0.0 collective-permute-done.9
  62.8 1.6 %collective-permute-start.10 = (f32[432,128]{1,0:T(8,128)S(1)}, f32[432,128]{1,0:T(8,128)S(1)}, u32[]{:S(2)}, u32[]{:S(2)}) collective-permute-start(f32[432,128]{1,0:T(8,128)S(1)} %pad_maximum_fusion.kept), channel_id=1, source_target_pairs={{0,1},{1,0},{2,3},{3,2},{4,5},{5,4},{6,7},{7,6},{8,9},{9,8},{10,11... | collective-permute-start | bytes 663560 | tf_op jit(solution)/shard_map/ppermute | solution.py:589
  64.3 6.1 %collective-permute-done.10.arrived = f32[432,128]{1,0:T(8,128)S(1)} collective-permute-done((f32[432,128]{1,0:T(8,128)S(1)}, f32[432,128]{1,0:T(8,128)S(1)}, u32[]{:S(2)}, u32[]{:S(2)}) %collective-permute-start.10) | collective-permute-done | bytes 221216 | tf_op jit(solution)/shard_map/ppermute | solution.py:589
  70.5 2.7 %collective-permute-start.11 = (f32[216,128]{1,0:T(8,128)S(1)}, f32[216,128]{1,0:T(8,128)S(1)}, u32[]{:S(2)}, u32[]{:S(2)}) collective-permute-start(f32[216,128]{1,0:T(8,128)S(1)} %get-tuple-element.61), channel_id=1, source_target_pairs={{0,16},{2,18},{4,20},{6,22},{8,24},{10,26},{12,28},{14,30},{16,0},... | collective-permute-start | bytes 331784 | tf_op jit(solution)/shard_map/ppermute | solution.py:589
  73.2 4.4 %all-to-all-done.1 = f32[16,64,128]{2,1,0:T(8,128)S(1)} async-done(((f32[16,64,128]{2,1,0:T(8,128)}), f32[16,64,128]{2,1,0:T(8,128)S(1)}, u32[]{:S(2)}, u32[]{:S(2)}) %all-to-all-start.1) | async-done | bytes 524320 | tf_op jit(solution)/shard_map/all_to_all | solution.py:643
  77.5 1.7 %unpack.1 = f32[512,128]{1,0:T(8,128)} custom-call(f32[1024,128]{1,0:T(8,128)S(1)} %bitcast.11, s32[8,512]{1,0:T(8,128)S(1)} %copy-done.11), custom_call_target="tpu_custom_call" | custom-call | flops 1700000000 | tf_op jit(solution)/shard_map/unpack/pallas_call | solution.py:646
  79.2 3.3 %collective-permute-done.11 = f32[216,128]{1,0:T(8,128)S(1)} collective-permute-done((f32[216,128]{1,0:T(8,128)S(1)}, f32[216,128]{1,0:T(8,128)S(1)}, u32[]{:S(2)}, u32[]{:S(2)}) %collective-permute-start.11) | collective-permute-done | bytes 110624 | tf_op jit(solution)/shard_map/ppermute | solution.py:589
  82.6 0.7 add_multiply_fusion
  (35 shorter events, 0.2 us)
Async XLA Ops:
  3.5 22.9 %copy-start.6 = (s32[1,1,2,1]{2,3,1,0:T(1,128)S(1)}, s32[1,1,2,1]{2,3,1,0:T(1,128)}, u32[]{:S(2)}) copy-start(s32[1,1,2,1]{2,3,1,0:T(1,128)} %param.12) | copy-start | bytes 28
  3.6 22.9 %all-to-all-start = ((f32[16,72,128]{2,1,0:T(8,128)}), f32[16,72,128]{2,1,0:T(8,128)S(1)}, u32[]{:S(2)}, u32[]{:S(2)}) async-start(f32[16,72,128]{2,1,0:T(8,128)} %get-tuple-element.36), calls=%async_computation | async-start | bytes 1179648 | tf_op jit(solution)/shard_map/all_to_all | solution.py:494
  10.9 1.5 %copy-start = (f32[27,128,128]{2,1,0:T(8,128)S(1)}, f32[27,128,128]{2,1,0:T(8,128)}, u32[]{:S(2)}) copy-start(f32[27,128,128]{2,1,0:T(8,128)} %taps_in) | copy-start | bytes 5308420
  12.4 18.1 %copy-start.5 = (s32[1,2,27]{2,1,0:T(2,128)S(1)}, s32[1,2,27]{2,1,0:T(2,128)}, u32[]{:S(2)}) copy-start(s32[1,2,27]{2,1,0:T(2,128)} %param.13) | copy-start | bytes 652
  26.5 4.0 %copy-start.1 = (f32[27,128,128]{2,1,0:T(8,128)S(1)}, f32[27,128,128]{2,1,0:T(8,128)}, u32[]{:S(2)}) copy-start(f32[27,128,128]{2,1,0:T(8,128)} %taps_in) | copy-start | bytes 5308420
  27.3 8.5 %collective-permute-start = (f32[64,128]{1,0:T(8,128)S(1)}, f32[64,128]{1,0:T(8,128)S(1)}, u32[]{:S(2)}, u32[]{:S(2)}) collective-permute-start(f32[64,128]{1,0:T(8,128)S(1)} %get-tuple-element.41), channel_id=1, source_target_pairs={{0,2},{2,0},{4,6},{6,4},{8,10},{10,8},{12,14},{14,12},{16,18},{18,... | collective-permute-start | bytes 98312 | tf_op jit(solution)/shard_map/ppermute | solution.py:516
  27.4 8.4 %collective-permute-start.1 = (f32[64,128]{1,0:T(8,128)S(1)}, f32[64,128]{1,0:T(8,128)S(1)}, u32[]{:S(2)}, u32[]{:S(2)}) collective-permute-start(f32[64,128]{1,0:T(8,128)S(1)} %get-tuple-element.42), channel_id=1, source_target_pairs={{0,30},{2,4},{4,2},{6,8},{8,6},{10,12},{12,10},{14,16},{16,14},{18... | collective-permute-start | bytes 98312 | tf_op jit(solution)/shard_map/ppermute | solution.py:517
  30.5 5.2 %copy-start.2 = (f32[1,1024,128]{2,1,0:T(8,128)S(1)}, f32[1,1024,128]{2,1,0:T(8,128)}, u32[]{:S(2)}) copy-start(f32[1,1024,128]{2,1,0:T(8,128)} %param.15) | copy-start | bytes 1572868
  35.7 2.0 %copy-start.9 = (f32[64,128]{1,0:T(8,128)}, f32[64,128]{1,0:T(8,128)S(1)}, u32[]{:S(2)}) copy-start(f32[64,128]{1,0:T(8,128)S(1)} %get-tuple-element.58.codes) | copy-start | bytes 98308
  37.8 4.7 %copy-start.3 = (f32[64,128]{1,0:T(8,128)}, f32[64,128]{1,0:T(8,128)S(1)}, u32[]{:S(2)}) copy-start(f32[64,128]{1,0:T(8,128)S(1)} %get-tuple-element.57) | copy-start | bytes 98308
  37.8 4.7 %copy-start.4 = (f32[64,128]{1,0:T(8,128)}, f32[64,128]{1,0:T(8,128)S(1)}, u32[]{:S(2)}) copy-start(f32[64,128]{1,0:T(8,128)S(1)} %get-tuple-element.56) | copy-start | bytes 98308
  37.8 4.7 %copy-start.7 = (bf16[1024,256]{1,0:T(8,128)(2,1)}, bf16[1024,256]{1,0:T(8,128)(2,1)S(1)}, u32[]{:S(2)}) copy-start(bf16[1024,256]{1,0:T(8,128)(2,1)S(1)} %get-tuple-element.55.grads) | copy-start | bytes 1572868
  42.5 2.2 %collective-permute-start.3 = (f32[832,128]{1,0:T(8,128)}, f32[832,128]{1,0:T(8,128)}, u32[]{:S(2)}, u32[]{:S(2)}) collective-permute-start(f32[832,128]{1,0:T(8,128)} %get-tuple-element.52), channel_id=1, source_target_pairs={{0,2},{2,0},{4,6},{6,4},{8,10},{10,8},{12,14},{14,12},{16,18},{18,... | collective-permute-start | bytes 1277960 | tf_op jit(solution)/shard_map/ppermute | solution.py:589
  42.6 3.2 %collective-permute-start.2 = (f32[896,128]{1,0:T(8,128)}, f32[896,128]{1,0:T(8,128)}, u32[]{:S(2)}, u32[]{:S(2)}) collective-permute-start(f32[896,128]{1,0:T(8,128)} %get-tuple-element.50), channel_id=1, source_target_pairs={{0,2},{2,0},{4,6},{6,4},{8,10},{10,8},{12,14},{14,12},{16,18},{18,... | collective-permute-start | bytes 1376264 | tf_op jit(solution)/shard_map/ppermute | solution.py:589
  43.1 6.3 %copy-start.8 = (bf16[1024,256]{1,0:T(8,128)(2,1)S(1)}, bf16[1024,256]{1,0:T(8,128)(2,1)}, u32[]{:S(2)}) copy-start(bf16[1024,256]{1,0:T(8,128)(2,1)} %copy-done.7) | copy-start | bytes 1572868
  43.1 5.3 %collective-permute-start.6 = (f32[64,128]{1,0:T(8,128)}, f32[64,128]{1,0:T(8,128)S(1)}, u32[]{:S(2)}, u32[]{:S(2)}) collective-permute-start(f32[64,128]{1,0:T(8,128)} %copy-done.4), channel_id=1, source_target_pairs={{0,2},{2,0},{4,6},{6,4},{8,10},{10,8},{12,14},{14,12},{16,18},{18,... | collective-permute-start | bytes 98312 | tf_op jit(solution)/shard_map/ppermute | solution.py:595
  43.2 6.2 %collective-permute-start.7 = (f32[64,128]{1,0:T(8,128)}, f32[64,128]{1,0:T(8,128)S(1)}, u32[]{:S(2)}, u32[]{:S(2)}) collective-permute-start(f32[64,128]{1,0:T(8,128)} %copy-done.3), channel_id=1, source_target_pairs={{0,30},{2,4},{4,2},{6,8},{8,6},{10,12},{12,10},{14,16},{16,14},{18... | collective-permute-start | bytes 98312 | tf_op jit(solution)/shard_map/ppermute | solution.py:594
  45.8 12.0 %copy-start.12 = (f32[416,128]{1,0:T(8,128)}, f32[416,128]{1,0:T(8,128)S(1)}, u32[]{:S(2)}) copy-start(f32[416,128]{1,0:T(8,128)S(1)} %get-tuple-element.69) | copy-start | bytes 638980
  47.0 8.4 %copy-start.10 = (f32[64,128]{1,0:T(8,128)S(1)}, f32[64,128]{1,0:T(8,128)}, u32[]{:S(2)}) copy-start(f32[64,128]{1,0:T(8,128)} %copy-done.9) | copy-start | bytes 98308
  47.0 10.0 %collective-permute-start.4 = (f32[448,128]{1,0:T(8,128)S(1)}, f32[448,128]{1,0:T(8,128)S(1)}, u32[]{:S(2)}, u32[]{:S(2)}) collective-permute-start(f32[448,128]{1,0:T(8,128)S(1)} %get-tuple-element.53), channel_id=1, source_target_pairs={{0,4},{2,6},{4,0},{6,2},{8,12},{10,14},{12,8},{14,10},{16,20},{18,... | collective-permute-start | bytes 688136 | tf_op jit(solution)/shard_map/ppermute | solution.py:589
  47.6 9.4 %collective-permute-start.5 = (f32[416,128]{1,0:T(8,128)S(1)}, f32[416,128]{1,0:T(8,128)S(1)}, u32[]{:S(2)}, u32[]{:S(2)}) collective-permute-start(f32[416,128]{1,0:T(8,128)S(1)} %get-tuple-element.54), channel_id=1, source_target_pairs={{0,8},{2,10},{4,12},{6,14},{8,0},{10,2},{12,4},{14,6},{16,24},{18,... | collective-permute-start | bytes 638984 | tf_op jit(solution)/shard_map/ppermute | solution.py:589
  57.1 0.8 copy-start.16
  57.1 0.7 copy-start.14
  57.1 5.6 %collective-permute-start.8 = (f32[224,128]{1,0:T(8,128)S(1)}, f32[224,128]{1,0:T(8,128)S(1)}, u32[]{:S(2)}, u32[]{:S(2)}) collective-permute-start(f32[224,128]{1,0:T(8,128)S(1)} %dynamic-slice_add_fusion.4.one), channel_id=1, source_target_pairs={{0,8},{2,10},{4,12},{6,14},{8,0},{10,2},{12,4},{14,6},{16,24},{18,... | collective-permute-start | bytes 344072 | tf_op jit(solution)/shard_map/ppermute | solution.py:589
  57.9 4.8 %copy-start.13 = (f32[416,128]{1,0:T(8,128)S(1)}, f32[416,128]{1,0:T(8,128)}, u32[]{:S(2)}) copy-start(f32[416,128]{1,0:T(8,128)} %copy-done.12) | copy-start | bytes 638980
  57.9 4.8 %copy-start.17 = (f32[416,128]{1,0:T(8,128)S(1)}, f32[416,128]{1,0:T(8,128)}, u32[]{:S(2)}) copy-start(f32[416,128]{1,0:T(8,128)} %copy-done.16) | copy-start | bytes 638980
  57.9 4.8 %copy-start.15 = (f32[448,128]{1,0:T(8,128)S(1)}, f32[448,128]{1,0:T(8,128)}, u32[]{:S(2)}) copy-start(f32[448,128]{1,0:T(8,128)} %copy-done.14) | copy-start | bytes 688132
  57.9 4.8 %collective-permute-start.9 = (f32[208,128]{1,0:T(8,128)S(1)}, f32[208,128]{1,0:T(8,128)S(1)}, u32[]{:S(2)}, u32[]{:S(2)}) collective-permute-start(f32[208,128]{1,0:T(8,128)S(1)} %dynamic-slice_add_fusion.5.two), channel_id=1, source_target_pairs={{0,4},{2,6},{4,0},{6,2},{8,12},{10,14},{12,8},{14,10},{16,20},{18,... | collective-permute-start | bytes 319496 | tf_op jit(solution)/shard_map/ppermute | solution.py:589
  59.1 18.5 %all-to-all-start.1 = ((f32[16,64,128]{2,1,0:T(8,128)}), f32[16,64,128]{2,1,0:T(8,128)S(1)}, u32[]{:S(2)}, u32[]{:S(2)}) async-start(f32[16,64,128]{2,1,0:T(8,128)} %bitcast.8), calls=%async_computation.1 | async-start | bytes 1048576 | tf_op jit(solution)/shard_map/all_to_all | solution.py:643
  62.8 7.7 %collective-permute-start.10 = (f32[432,128]{1,0:T(8,128)S(1)}, f32[432,128]{1,0:T(8,128)S(1)}, u32[]{:S(2)}, u32[]{:S(2)}) collective-permute-start(f32[432,128]{1,0:T(8,128)S(1)} %pad_maximum_fusion.kept), channel_id=1, source_target_pairs={{0,1},{1,0},{2,3},{3,2},{4,5},{5,4},{6,7},{7,6},{8,9},{9,8},{10,11... | collective-permute-start | bytes 663560 | tf_op jit(solution)/shard_map/ppermute | solution.py:589
  70.5 7.1 %copy-start.11 = (s32[8,512]{1,0:T(8,128)S(1)}, s32[8,512]{1,0:T(8,128)}, u32[]{:S(2)}) copy-start(s32[8,512]{1,0:T(8,128)} %get-tuple-element.63.dest) | copy-start | bytes 49156
  70.5 12.1 %collective-permute-start.11 = (f32[216,128]{1,0:T(8,128)S(1)}, f32[216,128]{1,0:T(8,128)S(1)}, u32[]{:S(2)}, u32[]{:S(2)}) collective-permute-start(f32[216,128]{1,0:T(8,128)S(1)} %get-tuple-element.61), channel_id=1, source_target_pairs={{0,16},{2,18},{4,20},{6,22},{8,24},{10,26},{12,28},{14,30},{16,0},... | collective-permute-start | bytes 331784 | tf_op jit(solution)/shard_map/ppermute | solution.py:589

commit v4 on v3

--- a/solution.py
+++ b/solution.py
@@ -397,18 +397,13 @@
 
 
 def backward_kernel(
-    names_in, lent, me, grads, backward_in, halo_core, halo_far, blocks_out,
-    names, backward, shifted, back, target, sems,
+    names_in, lent, me, grads, backward, halo_core, halo_far, blocks_out,
+    names, shifted, back, target, sem,
 ):
-    copies = [
-        pltpu.make_async_copy(names_in, names, sems.at[0]),
-        pltpu.make_async_copy(backward_in, backward, sems.at[1]),
-    ]
-    for copy in copies:
-        copy.start()
+    names_copy = pltpu.make_async_copy(names_in, names, sem)
+    names_copy.start()
     target[...] = jnp.zeros_like(target)
     shifted[...] = jnp.zeros_like(shifted)
-    copies[0].wait()
     for b in range(NB):
         rows = slice(b * VOX, (b + 1) * VOX)
         for i in range(3):
@@ -416,9 +411,8 @@
             shifted[at, i * C : (i + 1) * C] = grads[rows, :C]
             shifted[at, (3 + i) * C : (4 + i) * C] = grads[rows, C:]
             shifted[at, (6 + i) * C : (7 + i) * C] = grads[rows, :C]
-        if b == 0:
-            copies[1].wait()
         back[b] = mm(shifted[...], backward[...])
+    names_copy.wait()
     for b in range(NB):
         for p in range(PAD):
             i = 0 if p == 0 else 2 if p == PAD - 1 else 1
@@ -602,15 +596,14 @@
     grad_blocks = pl.pallas_call(
         backward_kernel,
         out_shape=struct(voxels, C),
-        in_specs=[ANY, SMEM, SMEM, VMEM, ANY, VMEM, VMEM],
+        in_specs=[ANY, SMEM, SMEM] + [VMEM] * 4,
         out_specs=VMEM,
         scratch_shapes=[
             pltpu.SMEM((NB, 27), jnp.int32),
-            pltpu.VMEM((9 * C, COLS), bf16),
             pltpu.VMEM((PAD * FACE, 9 * C), bf16),
             pltpu.VMEM((NB, PAD * FACE, COLS), f32),
             pltpu.VMEM((3 * VOX, C), f32),
-            pltpu.SemaphoreType.DMA((2,)),
+            pltpu.SemaphoreType.DMA,
         ],
         compiler_params=params(14),
         name="backward",
@@ -635,7 +628,6 @@
         in_specs=[ANY] * 3,
         out_specs=ANY,
         input_output_aliases={0: 0},
-        compiler_params=params(1),
         name="pass",
         cost_estimate=cost(2.2),
     )(back_points, *sent)

time: 83.7 us -> 83.2 us (level)
    unnamed x36 -> x38, local copies, waits for them, and re-layouts: 1.89 us -> 1.84 us
where the time goes in v4:
time: 83.2 us; the launch traced here: 82.8 us
  waiting for transfers between devices  28.5 us (34%)
  Pallas kernels  24.9 us (30%)
  starting transfers between devices  23.5 us (28%)
  other arithmetic  3.08 us (4%)
  local copies, waits for them, and re-layouts  1.84 us (2%)
  between operations  0.96 us (1%)
    all_to_all x1, waiting for transfers between devices, per_device(): recv = lax.all_to_all(send, 'slab', split_axis=0, concat_axis=0, tiled=True)  13.5 us
    ppermute x8, waiting for transfers between devices, swapped(): return lax.ppermute(part, axis, [(i, i ^ 1 << bit) for i in range(size)])  9.61 us
    ppermute x8, starting transfers between devices, swapped(): return lax.ppermute(part, axis, [(i, i ^ 1 << bit) for i in range(size)])  7.77 us
    all_to_all x1, starting transfers between devices, per_device(): recv = lax.all_to_all(send, 'slab', split_axis=0, concat_axis=0, tiled=True)  7.37 us
    pallas_call x1, Pallas kernels, per_device(): pl.pallas_call(backward_kernel, out_shape=struct(voxels, C), in_specs=[AN...  6.15 us
    pallas_call x1, Pallas kernels, per_device(): pl.pallas_call(functools.partial(interior_kernel, capacity), out_shape=(s...  5.21 us
    pallas_call x1, Pallas kernels, per_device(): pl.pallas_call(functools.partial(weight_grad_kernel, chunk, pieces), out_...  4.72 us
    all_to_all x1, waiting for transfers between devices, per_device(): lax.all_to_all(back_points.reshape(slabs, capacity, C), 'slab', split_axi...  4.36 us
  transfers between devices with their start and end apart: 14, of which 6 were waited for; matrix products, arithmetic and copies ran while one was open for 3% of the time, Pallas kernels for 18%

profile of v4, /device:TPU:0, one launch (start us, length us, event | category | flops | bytes accessed | tf_op | source)
XLA Modules:
  0.0 82.8 jit_solution(4168159565286069894)
XLA Ops:
  0.6 2.9 %pack.1 = (f32[16,72,128]{2,1,0:T(8,128)}, s32[8,512]{1,0:T(8,128)}) custom-call(s32[1]{0:T(128)} %bitcast.1.me_ref.me, f32[512,128]{1,0:T(8,128)} %bitcast.19, s32[1,512]{1,0:T(1,128)} %bitcast.20, s32[1,512]{1,0:T(1,128)} %slot_in.1, s32[1,512]{1,0:T(1,128)} %vox_in.1), custom_call_target="tpu_custom_call" | custom-call | flops 2000000000 | tf_op jit(solution)/shard_map/pack/pallas_call | solution.py:475
  3.6 0.0 copy-start.7
  3.6 7.4 %all-to-all-start = ((f32[16,72,128]{2,1,0:T(8,128)}), f32[16,72,128]{2,1,0:T(8,128)S(1)}, u32[]{:S(2)}, u32[]{:S(2)}) async-start(f32[16,72,128]{2,1,0:T(8,128)} %get-tuple-element.36), calls=%async_computation | async-start | bytes 1179648 | tf_op jit(solution)/shard_map/all_to_all | solution.py:488
  10.9 0.0 copy-start
  11.0 1.5 %copy-done = f32[27,128,128]{2,1,0:T(8,128)S(1)} copy-done((f32[27,128,128]{2,1,0:T(8,128)S(1)}, f32[27,128,128]{2,1,0:T(8,128)}, u32[]{:S(2)}) %copy-start) | copy-done | bytes 1769496
  12.4 0.5 weights.1.backward
  13.0 13.5 %all-to-all-done.recv = f32[16,72,128]{2,1,0:T(8,128)S(1)} async-done(((f32[16,72,128]{2,1,0:T(8,128)}), f32[16,72,128]{2,1,0:T(8,128)S(1)}, u32[]{:S(2)}, u32[]{:S(2)}) %all-to-all-start) | async-done | bytes 589856 | tf_op jit(solution)/shard_map/all_to_all | solution.py:488
  26.5 0.8 faces.1
  27.3 0.1 collective-permute-start
  27.4 3.1 %collective-permute-start.1 = (f32[64,128]{1,0:T(8,128)S(1)}, f32[64,128]{1,0:T(8,128)S(1)}, u32[]{:S(2)}, u32[]{:S(2)}) collective-permute-start(f32[64,128]{1,0:T(8,128)S(1)} %get-tuple-element.42), channel_id=1, source_target_pairs={{0,30},{2,4},{4,2},{6,8},{8,6},{10,12},{12,10},{14,16},{16,14},{18... | collective-permute-start | bytes 98312 | tf_op jit(solution)/shard_map/ppermute | solution.py:511
  30.5 0.0 copy-done.1
  30.5 5.2 %interior.1 = (f32[1024,128]{1,0:T(8,128)S(1)}, bf16[1024,2304]{1,0:T(8,128)(2,1)S(1)}, f32[256,128]{1,0:T(8,128)S(1)}, f32[64,128]{1,0:T(8,128)S(1)}, bf16[3,2304,256]{2,1,0:T(8,128)(2,1)S(1)}) custom-call(s32[2,27]{1,0:T(2,128)S(1)} %bitcast.14, f32[16,72,128]{2,1,0:T(8,128)S(1)} %all-to-all-done.recv, f32[27,128,128]{2,1,0:T(8,128)S(1)} %copy-done.1), custom_call_target="tpu_custom_call" | custom-call | flops 5000000000 | tf_op jit(solution)/shard_map/interior/pallas_call | solution.py:512
  35.7 0.0 collective-permute-done.from_core
  35.8 0.0 collective-permute-done.1.from_far
  35.8 2.0 %finish.1 = (f32[1024,128]{1,0:T(8,128)}, bf16[1024,256]{1,0:T(8,128)(2,1)S(1)}, bf16[2,128,2304]{2,1,0:T(8,128)(2,1)S(1)}, f32[64,128]{1,0:T(8,128)S(1)}, f32[64,128]{1,0:T(8,128)S(1)}) custom-call(s32[2,27]{1,0:T(2,128)S(1)} %bitcast.15, s32[1]{0:T(128)} %bitcast.1.me_ref.me, f32[1024,128]{1,0:T(8,128)S(1)} %get-tuple-element.39.before, ...), custom_call_target="tpu_custom_call" | custom-call | flops 2800000000 | tf_op jit(solution)/shard_map/finish/pallas_call | solution.py:533
  37.8 0.0 copy-start.4
  37.8 0.0 copy-start.5
  37.8 4.7 %weight_grad.1 = (f32[896,128]{1,0:T(8,128)S(1)}, f32[896,128]{1,0:T(8,128)}, f32[832,128]{1,0:T(8,128)S(1)}, f32[832,128]{1,0:T(8,128)}) custom-call(s32[1]{0:T(128)} %bitcast.1.me_ref.me, bf16[1024,2304]{1,0:T(8,128)(2,1)S(1)} %get-tuple-element.46.columns, bf16[2,128,2304]{2,1,0:T(8,128)(2,1)S(1)} %get-tuple-element.47.outer, ...), custom_call_target="tpu_custom_call" | custom-call | flops 4000000000 | tf_op jit(solution)/shard_map/weight_grad/pallas_call | solution.py:571
  42.5 0.1 collective-permute-start.3
  42.6 0.5 collective-permute-start.2
  43.1 0.1 collective-permute-start.6
  43.2 1.4 %collective-permute-start.7 = (f32[64,128]{1,0:T(8,128)}, f32[64,128]{1,0:T(8,128)S(1)}, u32[]{:S(2)}, u32[]{:S(2)}) collective-permute-start(f32[64,128]{1,0:T(8,128)} %copy-done.4), channel_id=1, source_target_pairs={{0,30},{2,4},{4,2},{6,8},{8,6},{10,12},{12,10},{14,16},{16,14},{18... | collective-permute-start | bytes 98312 | tf_op jit(solution)/shard_map/ppermute | solution.py:588
  44.6 0.1 collective-permute-done.3
  44.7 1.1 %dynamic-slice_add_fusion.2 = (f32[416,128]{1,0:T(8,128)S(1)}, f32[416,128]{1,0:T(8,128)S(1)}) fusion(f32[832,128]{1,0:T(8,128)} %collective-permute-done.3, s32[]{:T(128)S(6)} %select_n.37, f32[832,128]{1,0:T(8,128)S(1)} %get-tuple-element.51, s32[]{:T(128)S(6)} %select_n.35), kind=kLoop, calls=%fused_computation.3 | loop fusion | flops 106496 | bytes 1277960 | tf_op jit(solution)/shard_map/add | solution.py:374
  45.8 0.0 collective-permute-done.2
  45.8 1.2 %dynamic-slice_add_fusion.1 = (f32[448,128]{1,0:T(8,128)S(1)}, f32[448,128]{1,0:T(8,128)S(1)}) fusion(f32[896,128]{1,0:T(8,128)} %collective-permute-done.2, s32[]{:T(128)S(6)} %select_n.32, f32[896,128]{1,0:T(8,128)S(1)} %get-tuple-element.49, s32[]{:T(128)S(6)} %select_n.34), kind=kLoop, calls=%fused_computation.1 | loop fusion | flops 114688 | bytes 1376264 | tf_op jit(solution)/shard_map/add | solution.py:374
  47.0 0.6 collective-permute-start.4
  47.6 0.8 collective-permute-start.5
  48.4 0.0 collective-permute-done.6.halo_core
  48.4 1.0 %collective-permute-done.7.halo_far = f32[64,128]{1,0:T(8,128)S(1)} collective-permute-done((f32[64,128]{1,0:T(8,128)}, f32[64,128]{1,0:T(8,128)S(1)}, u32[]{:S(2)}, u32[]{:S(2)}) %collective-permute-start.7) | collective-permute-done | bytes 32800 | tf_op jit(solution)/shard_map/ppermute | solution.py:588
  49.4 6.2 %backward.1.grad_blocks = f32[1024,128]{1,0:T(8,128)S(1)} custom-call(s32[2,27]{1,0:T(2,128)S(1)} %bitcast.16, s32[2]{0:T(128)S(1)} %bitcast.18, s32[1]{0:T(128)} %bitcast.1.me_ref.me, bf16[1024,256]{1,0:T(8,128)(2,1)S(1)} %copy-done.9, bf16[1152,1152]{1,0:T(8,128)(2,1)S(1)} %weights.1.backward, f32[64,128]{1,0:T(8,128)S(1)} %collective-permute-done.6.halo_core, ...), custom_call_target="tpu_custom_call" | custom-call | flops 6499999744 | tf_op jit(solution)/shard_map/backward/pallas_call | solution.py:596
  55.6 0.9 %gather.1.rows = f32[1024,128]{1,0:T(8,128)S(1)} custom-call(f32[1024,128]{1,0:T(8,128)S(1)} %backward.1.grad_blocks, f32[64,128]{1,0:T(8,128)S(1)} %copy-done.11), custom_call_target="tpu_custom_call" | custom-call | flops 2200000000 | tf_op jit(solution)/shard_map/gather/pallas_call | solution.py:612
  56.5 0.0 collective-permute-done.5
  56.5 0.0 copy-start.15
  56.5 0.0 collective-permute-done.4
  56.5 0.4 collective-permute-start.8
  56.9 0.3 copy-done.15
  57.2 1.2 %collective-permute-start.9 = (f32[208,128]{1,0:T(8,128)S(1)}, f32[208,128]{1,0:T(8,128)S(1)}, u32[]{:S(2)}, u32[]{:S(2)}) collective-permute-start(f32[208,128]{1,0:T(8,128)S(1)} %dynamic-slice_add_fusion.5.two), channel_id=1, source_target_pairs={{0,4},{2,6},{4,0},{6,2},{8,12},{10,14},{12,8},{14,10},{16,20},{18,... | collective-permute-start | bytes 319496 | tf_op jit(solution)/shard_map/ppermute | solution.py:583
  58.5 3.7 %all-to-all-start.1 = ((f32[16,64,128]{2,1,0:T(8,128)}), f32[16,64,128]{2,1,0:T(8,128)S(1)}, u32[]{:S(2)}, u32[]{:S(2)}) async-start(f32[16,64,128]{2,1,0:T(8,128)} %bitcast.12), calls=%async_computation.1 | async-start | bytes 1048576 | tf_op jit(solution)/shard_map/all_to_all | solution.py:635
  62.2 0.0 collective-permute-done.9
  62.2 0.0 collective-permute-done.8
  62.3 1.6 %collective-permute-start.10 = (f32[432,128]{1,0:T(8,128)S(1)}, f32[432,128]{1,0:T(8,128)S(1)}, u32[]{:S(2)}, u32[]{:S(2)}) collective-permute-start(f32[432,128]{1,0:T(8,128)S(1)} %pad_maximum_fusion.kept), channel_id=1, source_target_pairs={{0,1},{1,0},{2,3},{3,2},{4,5},{5,4},{6,7},{7,6},{8,9},{9,8},{10,11... | collective-permute-start | bytes 663560 | tf_op jit(solution)/shard_map/ppermute | solution.py:583
  63.9 6.1 %collective-permute-done.10.arrived = f32[432,128]{1,0:T(8,128)S(1)} collective-permute-done((f32[432,128]{1,0:T(8,128)S(1)}, f32[432,128]{1,0:T(8,128)S(1)}, u32[]{:S(2)}, u32[]{:S(2)}) %collective-permute-start.10) | collective-permute-done | bytes 221216 | tf_op jit(solution)/shard_map/ppermute | solution.py:583
  70.0 2.7 %collective-permute-start.11 = (f32[216,128]{1,0:T(8,128)S(1)}, f32[216,128]{1,0:T(8,128)S(1)}, u32[]{:S(2)}, u32[]{:S(2)}) collective-permute-start(f32[216,128]{1,0:T(8,128)S(1)} %get-tuple-element.61), channel_id=1, source_target_pairs={{0,16},{2,18},{4,20},{6,22},{8,24},{10,26},{12,28},{14,30},{16,0},... | collective-permute-start | bytes 331784 | tf_op jit(solution)/shard_map/ppermute | solution.py:583
  72.7 4.4 %all-to-all-done.1 = f32[16,64,128]{2,1,0:T(8,128)S(1)} async-done(((f32[16,64,128]{2,1,0:T(8,128)}), f32[16,64,128]{2,1,0:T(8,128)S(1)}, u32[]{:S(2)}, u32[]{:S(2)}) %all-to-all-start.1) | async-done | bytes 524320 | tf_op jit(solution)/shard_map/all_to_all | solution.py:635
  77.1 1.7 %unpack.1 = f32[512,128]{1,0:T(8,128)} custom-call(f32[1024,128]{1,0:T(8,128)S(1)} %bitcast.11, s32[8,512]{1,0:T(8,128)S(1)} %copy-done.12), custom_call_target="tpu_custom_call" | custom-call | flops 1700000000 | tf_op jit(solution)/shard_map/unpack/pallas_call | solution.py:638
  78.8 3.3 %collective-permute-done.11 = f32[216,128]{1,0:T(8,128)S(1)} collective-permute-done((f32[216,128]{1,0:T(8,128)S(1)}, f32[216,128]{1,0:T(8,128)S(1)}, u32[]{:S(2)}, u32[]{:S(2)}) %collective-permute-start.11) | collective-permute-done | bytes 110624 | tf_op jit(solution)/shard_map/ppermute | solution.py:583
  82.1 0.7 add_multiply_fusion
  (37 shorter events, 0.2 us)
Async XLA Ops:
  3.6 22.9 %copy-start.7 = (s32[1,1,2,1]{2,3,1,0:T(1,128)S(1)}, s32[1,1,2,1]{2,3,1,0:T(1,128)}, u32[]{:S(2)}) copy-start(s32[1,1,2,1]{2,3,1,0:T(1,128)} %param.12) | copy-start | bytes 28
  3.6 22.9 %all-to-all-start = ((f32[16,72,128]{2,1,0:T(8,128)}), f32[16,72,128]{2,1,0:T(8,128)S(1)}, u32[]{:S(2)}, u32[]{:S(2)}) async-start(f32[16,72,128]{2,1,0:T(8,128)} %get-tuple-element.36), calls=%async_computation | async-start | bytes 1179648 | tf_op jit(solution)/shard_map/all_to_all | solution.py:488
  10.9 1.5 %copy-start = (f32[27,128,128]{2,1,0:T(8,128)S(1)}, f32[27,128,128]{2,1,0:T(8,128)}, u32[]{:S(2)}) copy-start(f32[27,128,128]{2,1,0:T(8,128)} %taps_in) | copy-start | bytes 5308420
  12.4 18.1 %copy-start.6 = (s32[1,2,27]{2,1,0:T(2,128)S(1)}, s32[1,2,27]{2,1,0:T(2,128)}, u32[]{:S(2)}) copy-start(s32[1,2,27]{2,1,0:T(2,128)} %param.13) | copy-start | bytes 652
  26.5 4.0 %copy-start.1 = (f32[27,128,128]{2,1,0:T(8,128)S(1)}, f32[27,128,128]{2,1,0:T(8,128)}, u32[]{:S(2)}) copy-start(f32[27,128,128]{2,1,0:T(8,128)} %taps_in) | copy-start | bytes 5308420
  27.3 8.5 %collective-permute-start = (f32[64,128]{1,0:T(8,128)S(1)}, f32[64,128]{1,0:T(8,128)S(1)}, u32[]{:S(2)}, u32[]{:S(2)}) collective-permute-start(f32[64,128]{1,0:T(8,128)S(1)} %get-tuple-element.41), channel_id=1, source_target_pairs={{0,2},{2,0},{4,6},{6,4},{8,10},{10,8},{12,14},{14,12},{16,18},{18,... | collective-permute-start | bytes 98312 | tf_op jit(solution)/shard_map/ppermute | solution.py:510
  27.4 8.4 %collective-permute-start.1 = (f32[64,128]{1,0:T(8,128)S(1)}, f32[64,128]{1,0:T(8,128)S(1)}, u32[]{:S(2)}, u32[]{:S(2)}) collective-permute-start(f32[64,128]{1,0:T(8,128)S(1)} %get-tuple-element.42), channel_id=1, source_target_pairs={{0,30},{2,4},{4,2},{6,8},{8,6},{10,12},{12,10},{14,16},{16,14},{18... | collective-permute-start | bytes 98312 | tf_op jit(solution)/shard_map/ppermute | solution.py:511
  30.5 5.2 %copy-start.3 = (f32[1,1024,128]{2,1,0:T(8,128)S(1)}, f32[1,1024,128]{2,1,0:T(8,128)}, u32[]{:S(2)}) copy-start(f32[1,1024,128]{2,1,0:T(8,128)} %param.15) | copy-start | bytes 1572868
  35.7 2.0 %copy-start.10 = (f32[64,128]{1,0:T(8,128)}, f32[64,128]{1,0:T(8,128)S(1)}, u32[]{:S(2)}) copy-start(f32[64,128]{1,0:T(8,128)S(1)} %get-tuple-element.58.codes) | copy-start | bytes 98308
  37.8 4.8 %copy-start.4 = (f32[64,128]{1,0:T(8,128)}, f32[64,128]{1,0:T(8,128)S(1)}, u32[]{:S(2)}) copy-start(f32[64,128]{1,0:T(8,128)S(1)} %get-tuple-element.57) | copy-start | bytes 98308
  37.8 4.7 %copy-start.5 = (f32[64,128]{1,0:T(8,128)}, f32[64,128]{1,0:T(8,128)S(1)}, u32[]{:S(2)}) copy-start(f32[64,128]{1,0:T(8,128)S(1)} %get-tuple-element.56) | copy-start | bytes 98308
  37.8 4.7 %copy-start.8 = (bf16[1024,256]{1,0:T(8,128)(2,1)}, bf16[1024,256]{1,0:T(8,128)(2,1)S(1)}, u32[]{:S(2)}) copy-start(bf16[1024,256]{1,0:T(8,128)(2,1)S(1)} %get-tuple-element.55.grads) | copy-start | bytes 1572868
  42.5 2.2 %collective-permute-start.3 = (f32[832,128]{1,0:T(8,128)}, f32[832,128]{1,0:T(8,128)}, u32[]{:S(2)}, u32[]{:S(2)}) collective-permute-start(f32[832,128]{1,0:T(8,128)} %get-tuple-element.52), channel_id=1, source_target_pairs={{0,2},{2,0},{4,6},{6,4},{8,10},{10,8},{12,14},{14,12},{16,18},{18,... | collective-permute-start | bytes 1277960 | tf_op jit(solution)/shard_map/ppermute | solution.py:583
  42.6 3.2 %collective-permute-start.2 = (f32[896,128]{1,0:T(8,128)}, f32[896,128]{1,0:T(8,128)}, u32[]{:S(2)}, u32[]{:S(2)}) collective-permute-start(f32[896,128]{1,0:T(8,128)} %get-tuple-element.50), channel_id=1, source_target_pairs={{0,2},{2,0},{4,6},{6,4},{8,10},{10,8},{12,14},{14,12},{16,18},{18,... | collective-permute-start | bytes 1376264 | tf_op jit(solution)/shard_map/ppermute | solution.py:583
  43.1 6.3 %copy-start.9 = (bf16[1024,256]{1,0:T(8,128)(2,1)S(1)}, bf16[1024,256]{1,0:T(8,128)(2,1)}, u32[]{:S(2)}) copy-start(bf16[1024,256]{1,0:T(8,128)(2,1)} %copy-done.8) | copy-start | bytes 1572868
  43.1 5.3 %collective-permute-start.6 = (f32[64,128]{1,0:T(8,128)}, f32[64,128]{1,0:T(8,128)S(1)}, u32[]{:S(2)}, u32[]{:S(2)}) collective-permute-start(f32[64,128]{1,0:T(8,128)} %copy-done.5), channel_id=1, source_target_pairs={{0,2},{2,0},{4,6},{6,4},{8,10},{10,8},{12,14},{14,12},{16,18},{18,... | collective-permute-start | bytes 98312 | tf_op jit(solution)/shard_map/ppermute | solution.py:589
  43.2 6.2 %collective-permute-start.7 = (f32[64,128]{1,0:T(8,128)}, f32[64,128]{1,0:T(8,128)S(1)}, u32[]{:S(2)}, u32[]{:S(2)}) collective-permute-start(f32[64,128]{1,0:T(8,128)} %copy-done.4), channel_id=1, source_target_pairs={{0,30},{2,4},{4,2},{6,8},{8,6},{10,12},{12,10},{14,16},{16,14},{18... | collective-permute-start | bytes 98312 | tf_op jit(solution)/shard_map/ppermute | solution.py:588
  45.8 11.1 %copy-start.13 = (f32[416,128]{1,0:T(8,128)}, f32[416,128]{1,0:T(8,128)S(1)}, u32[]{:S(2)}) copy-start(f32[416,128]{1,0:T(8,128)S(1)} %get-tuple-element.69) | copy-start | bytes 638980
  47.0 8.6 %copy-start.11 = (f32[64,128]{1,0:T(8,128)S(1)}, f32[64,128]{1,0:T(8,128)}, u32[]{:S(2)}) copy-start(f32[64,128]{1,0:T(8,128)} %copy-done.10) | copy-start | bytes 98308
  47.0 9.5 %collective-permute-start.4 = (f32[448,128]{1,0:T(8,128)S(1)}, f32[448,128]{1,0:T(8,128)S(1)}, u32[]{:S(2)}, u32[]{:S(2)}) collective-permute-start(f32[448,128]{1,0:T(8,128)S(1)} %get-tuple-element.53), channel_id=1, source_target_pairs={{0,4},{2,6},{4,0},{6,2},{8,12},{10,14},{12,8},{14,10},{16,20},{18,... | collective-permute-start | bytes 688136 | tf_op jit(solution)/shard_map/ppermute | solution.py:583
  47.6 8.8 %collective-permute-start.5 = (f32[416,128]{1,0:T(8,128)S(1)}, f32[416,128]{1,0:T(8,128)S(1)}, u32[]{:S(2)}, u32[]{:S(2)}) collective-permute-start(f32[416,128]{1,0:T(8,128)S(1)} %get-tuple-element.54), channel_id=1, source_target_pairs={{0,8},{2,10},{4,12},{6,14},{8,0},{10,2},{12,4},{14,6},{16,24},{18,... | collective-permute-start | bytes 638984 | tf_op jit(solution)/shard_map/ppermute | solution.py:583
  56.5 2.0 %copy-start.2 = (f32[1024,128]{1,0:T(8,128)}, f32[1024,128]{1,0:T(8,128)S(1)}, u32[]{:S(2)}) copy-start(f32[1024,128]{1,0:T(8,128)S(1)} %gather.1.rows) | copy-start | bytes 1572868
  56.5 0.7 copy-start.15
  56.5 1.9 %copy-start.17 = (f32[224,128]{1,0:T(8,128)}, f32[224,128]{1,0:T(8,128)S(1)}, u32[]{:S(2)}) copy-start(f32[224,128]{1,0:T(8,128)S(1)} %dynamic-slice_add_fusion.4.one) | copy-start | bytes 344068
  56.5 5.7 %collective-permute-start.8 = (f32[224,128]{1,0:T(8,128)S(1)}, f32[224,128]{1,0:T(8,128)S(1)}, u32[]{:S(2)}, u32[]{:S(2)}) collective-permute-start(f32[224,128]{1,0:T(8,128)S(1)} %dynamic-slice_add_fusion.4.one), channel_id=1, source_target_pairs={{0,8},{2,10},{4,12},{6,14},{8,0},{10,2},{12,4},{14,6},{16,24},{18,... | collective-permute-start | bytes 344072 | tf_op jit(solution)/shard_map/ppermute | solution.py:583
  57.2 1.2 %copy-start.18 = (f32[208,128]{1,0:T(8,128)}, f32[208,128]{1,0:T(8,128)S(1)}, u32[]{:S(2)}) copy-start(f32[208,128]{1,0:T(8,128)S(1)} %dynamic-slice_add_fusion.5.two) | copy-start | bytes 319492
  57.2 5.0 %copy-start.14 = (f32[416,128]{1,0:T(8,128)S(1)}, f32[416,128]{1,0:T(8,128)}, u32[]{:S(2)}) copy-start(f32[416,128]{1,0:T(8,128)} %copy-done.13) | copy-start | bytes 638980
  57.2 5.0 %collective-permute-start.9 = (f32[208,128]{1,0:T(8,128)S(1)}, f32[208,128]{1,0:T(8,128)S(1)}, u32[]{:S(2)}, u32[]{:S(2)}) collective-permute-start(f32[208,128]{1,0:T(8,128)S(1)} %dynamic-slice_add_fusion.5.two), channel_id=1, source_target_pairs={{0,4},{2,6},{4,0},{6,2},{8,12},{10,14},{12,8},{14,10},{16,20},{18,... | collective-permute-start | bytes 319496 | tf_op jit(solution)/shard_map/ppermute | solution.py:583
  58.4 3.8 %copy-start.16 = (f32[416,128]{1,0:T(8,128)S(1)}, f32[416,128]{1,0:T(8,128)}, u32[]{:S(2)}) copy-start(f32[416,128]{1,0:T(8,128)} %copy-done.15) | copy-start | bytes 638980
  58.5 18.6 %all-to-all-start.1 = ((f32[16,64,128]{2,1,0:T(8,128)}), f32[16,64,128]{2,1,0:T(8,128)S(1)}, u32[]{:S(2)}, u32[]{:S(2)}) async-start(f32[16,64,128]{2,1,0:T(8,128)} %bitcast.12), calls=%async_computation.1 | async-start | bytes 1048576 | tf_op jit(solution)/shard_map/all_to_all | solution.py:635
  62.3 7.7 %collective-permute-start.10 = (f32[432,128]{1,0:T(8,128)S(1)}, f32[432,128]{1,0:T(8,128)S(1)}, u32[]{:S(2)}, u32[]{:S(2)}) collective-permute-start(f32[432,128]{1,0:T(8,128)S(1)} %pad_maximum_fusion.kept), channel_id=1, source_target_pairs={{0,1},{1,0},{2,3},{3,2},{4,5},{5,4},{6,7},{7,6},{8,9},{9,8},{10,11... | collective-permute-start | bytes 663560 | tf_op jit(solution)/shard_map/ppermute | solution.py:583
  70.0 7.1 %copy-start.12 = (s32[8,512]{1,0:T(8,128)S(1)}, s32[8,512]{1,0:T(8,128)}, u32[]{:S(2)}) copy-start(s32[8,512]{1,0:T(8,128)} %get-tuple-element.63.dest) | copy-start | bytes 49156
  70.0 12.1 %collective-permute-start.11 = (f32[216,128]{1,0:T(8,128)S(1)}, f32[216,128]{1,0:T(8,128)S(1)}, u32[]{:S(2)}, u32[]{:S(2)}) collective-permute-start(f32[216,128]{1,0:T(8,128)S(1)} %get-tuple-element.61), channel_id=1, source_target_pairs={{0,16},{2,18},{4,20},{6,22},{8,24},{10,26},{12,28},{14,30},{16,0},... | collective-permute-start | bytes 331784 | tf_op jit(solution)/shard_map/ppermute | solution.py:583

commit v5 on v4

--- a/solution.py
+++ b/solution.py
@@ -43,13 +43,6 @@
 def split(value):
     high = value.astype(bf16)
     return high, (value - high.astype(f32)).astype(bf16)
-
-
-def split3(value):
-    high = value.astype(bf16)
-    rest = value - high.astype(f32)
-    middle = rest.astype(bf16)
-    return high, middle, (rest - middle.astype(f32)).astype(bf16)
 
 
 def iota(shape, dim):
@@ -81,9 +74,9 @@
     dest_out[...] = jnp.broadcast_to(target * capacity + rank, dest_out.shape)
     chosen = jnp.where(iota((slabs * block, points), 0) == place, 1.0, 0.0).astype(bf16)
     copies[3].wait()
-    parts = jnp.concatenate(split3(feats[...]), axis=1)
+    parts = jnp.concatenate(split(feats[...]), axis=1)
     rows = mm(chosen, parts)
-    rows = rows[:, :C] + rows[:, C : 2 * C] + rows[:, 2 * C :]
+    rows = rows[:, :C] + rows[:, C:]
     out[...] = rows.reshape(slabs, block, C)
     code = slot[...] * VOX + vox[...] + 1
     upper = lax.shift_right_logical(code, 5)
@@ -447,8 +440,8 @@
     places = dest[...].astype(f32).T[:, :1]
     points, slots = out.shape[0], came_back.shape[0]
     chosen = jnp.where(iota((points, slots), 1).astype(f32) == places, 1.0, 0.0).astype(bf16)
-    rows = mm(chosen, jnp.concatenate(split3(came_back[...]), axis=1))
-    out[...] = rows[:, :C] + rows[:, C : 2 * C] + rows[:, 2 * C :]
+    rows = mm(chosen, jnp.concatenate(split(came_back[...]), axis=1))
+    out[...] = rows[:, :C] + rows[:, C:]
 
 
 def place(slab, order):

time: 83.2 us -> 83 us (level)
  transfers between devices with their start and end apart: 14 -> 14, of which waited for: 6 -> 6; matrix products, arithmetic and copies ran while one was open for 3% -> 3% of each run, Pallas kernels for 18% -> 17%
where the time goes in v5:
time: 83 us; the launch traced here: 82.5 us
  waiting for transfers between devices  28.7 us (35%)
  Pallas kernels  24.3 us (29%)
  starting transfers between devices  23.4 us (28%)
  other arithmetic  3.08 us (4%)
  local copies, waits for them, and re-layouts  1.97 us (2%)
  between operations  0.96 us (1%)
    all_to_all x1, waiting for transfers between devices, per_device(): recv = lax.all_to_all(send, 'slab', split_axis=0, concat_axis=0, tiled=True)  13.5 us
    ppermute x8, waiting for transfers between devices, swapped(): return lax.ppermute(part, axis, [(i, i ^ 1 << bit) for i in range(size)])  9.83 us
    ppermute x8, starting transfers between devices, swapped(): return lax.ppermute(part, axis, [(i, i ^ 1 << bit) for i in range(size)])  7.67 us
    all_to_all x1, starting transfers between devices, per_device(): recv = lax.all_to_all(send, 'slab', split_axis=0, concat_axis=0, tiled=True)  7.37 us
    pallas_call x1, Pallas kernels, per_device(): pl.pallas_call(backward_kernel, out_shape=struct(voxels, C), in_specs=[AN...  6.18 us
    pallas_call x1, Pallas kernels, per_device(): pl.pallas_call(functools.partial(interior_kernel, capacity), out_shape=(s...  5.21 us
    pallas_call x1, Pallas kernels, per_device(): pl.pallas_call(functools.partial(weight_grad_kernel, chunk, pieces), out_...  4.72 us
    all_to_all x1, waiting for transfers between devices, per_device(): lax.all_to_all(back_points.reshape(slabs, capacity, C), 'slab', split_axi...  4.36 us
  transfers between devices with their start and end apart: 14, of which 6 were waited for; matrix products, arithmetic and copies ran while one was open for 3% of the time, Pallas kernels for 17%

profile of v5, /device:TPU:0, one launch (start us, length us, event | category | flops | bytes accessed | tf_op | source)
XLA Modules:
  0.0 82.5 jit_solution(9198863835598675575)
XLA Ops:
  0.6 2.6 %pack.1 = (f32[16,72,128]{2,1,0:T(8,128)}, s32[8,512]{1,0:T(8,128)}) custom-call(s32[1]{0:T(128)} %bitcast.1.me_ref.me, f32[512,128]{1,0:T(8,128)} %bitcast.19, s32[1,512]{1,0:T(1,128)} %bitcast.20, s32[1,512]{1,0:T(1,128)} %slot_in.1, s32[1,512]{1,0:T(1,128)} %vox_in.1), custom_call_target="tpu_custom_call" | custom-call | flops 2000000000 | tf_op jit(solution)/shard_map/pack/pallas_call | solution.py:468
  3.3 0.0 copy-start.7
  3.3 7.4 %all-to-all-start = ((f32[16,72,128]{2,1,0:T(8,128)}), f32[16,72,128]{2,1,0:T(8,128)S(1)}, u32[]{:S(2)}, u32[]{:S(2)}) async-start(f32[16,72,128]{2,1,0:T(8,128)} %get-tuple-element.36), calls=%async_computation | async-start | bytes 1179648 | tf_op jit(solution)/shard_map/all_to_all | solution.py:481
  10.7 0.0 copy-start
  10.7 1.5 %copy-done = f32[27,128,128]{2,1,0:T(8,128)S(1)} copy-done((f32[27,128,128]{2,1,0:T(8,128)S(1)}, f32[27,128,128]{2,1,0:T(8,128)}, u32[]{:S(2)}) %copy-start) | copy-done | bytes 1769496
  12.1 0.5 weights.1.backward
  12.7 13.5 %all-to-all-done.recv = f32[16,72,128]{2,1,0:T(8,128)S(1)} async-done(((f32[16,72,128]{2,1,0:T(8,128)}), f32[16,72,128]{2,1,0:T(8,128)S(1)}, u32[]{:S(2)}, u32[]{:S(2)}) %all-to-all-start) | async-done | bytes 589856 | tf_op jit(solution)/shard_map/all_to_all | solution.py:481
  26.2 0.0 copy-done.7
  26.2 0.8 faces.1
  27.0 0.1 collective-permute-start
  27.1 3.1 %collective-permute-start.1 = (f32[64,128]{1,0:T(8,128)S(1)}, f32[64,128]{1,0:T(8,128)S(1)}, u32[]{:S(2)}, u32[]{:S(2)}) collective-permute-start(f32[64,128]{1,0:T(8,128)S(1)} %get-tuple-element.42), channel_id=1, source_target_pairs={{0,30},{2,4},{4,2},{6,8},{8,6},{10,12},{12,10},{14,16},{16,14},{18... | collective-permute-start | bytes 98312 | tf_op jit(solution)/shard_map/ppermute | solution.py:504
  30.2 5.2 %interior.1 = (f32[1024,128]{1,0:T(8,128)S(1)}, bf16[1024,2304]{1,0:T(8,128)(2,1)S(1)}, f32[256,128]{1,0:T(8,128)S(1)}, f32[64,128]{1,0:T(8,128)S(1)}, bf16[3,2304,256]{2,1,0:T(8,128)(2,1)S(1)}) custom-call(s32[2,27]{1,0:T(2,128)S(1)} %bitcast.14, f32[16,72,128]{2,1,0:T(8,128)S(1)} %all-to-all-done.recv, f32[27,128,128]{2,1,0:T(8,128)S(1)} %copy-done.1), custom_call_target="tpu_custom_call" | custom-call | flops 5000000000 | tf_op jit(solution)/shard_map/interior/pallas_call | solution.py:505
  35.4 0.0 collective-permute-done.from_core
  35.5 0.0 collective-permute-done.1.from_far
  35.5 2.0 %finish.1 = (f32[1024,128]{1,0:T(8,128)}, bf16[1024,256]{1,0:T(8,128)(2,1)S(1)}, bf16[2,128,2304]{2,1,0:T(8,128)(2,1)S(1)}, f32[64,128]{1,0:T(8,128)S(1)}, f32[64,128]{1,0:T(8,128)S(1)}) custom-call(s32[2,27]{1,0:T(2,128)S(1)} %bitcast.15, s32[1]{0:T(128)} %bitcast.1.me_ref.me, f32[1024,128]{1,0:T(8,128)S(1)} %get-tuple-element.39.before, ...), custom_call_target="tpu_custom_call" | custom-call | flops 2800000000 | tf_op jit(solution)/shard_map/finish/pallas_call | solution.py:526
  37.5 0.0 copy-start.4
  37.5 0.0 copy-start.5
  37.5 4.7 %weight_grad.1 = (f32[896,128]{1,0:T(8,128)S(1)}, f32[896,128]{1,0:T(8,128)}, f32[832,128]{1,0:T(8,128)S(1)}, f32[832,128]{1,0:T(8,128)}) custom-call(s32[1]{0:T(128)} %bitcast.1.me_ref.me, bf16[1024,2304]{1,0:T(8,128)(2,1)S(1)} %get-tuple-element.46.columns, bf16[2,128,2304]{2,1,0:T(8,128)(2,1)S(1)} %get-tuple-element.47.outer, ...), custom_call_target="tpu_custom_call" | custom-call | flops 4000000000 | tf_op jit(solution)/shard_map/weight_grad/pallas_call | solution.py:564
  42.2 0.1 collective-permute-start.3
  42.3 0.5 collective-permute-start.2
  42.8 0.1 collective-permute-start.6
  42.9 1.4 %collective-permute-start.7 = (f32[64,128]{1,0:T(8,128)}, f32[64,128]{1,0:T(8,128)S(1)}, u32[]{:S(2)}, u32[]{:S(2)}) collective-permute-start(f32[64,128]{1,0:T(8,128)} %copy-done.4), channel_id=1, source_target_pairs={{0,30},{2,4},{4,2},{6,8},{8,6},{10,12},{12,10},{14,16},{16,14},{18... | collective-permute-start | bytes 98312 | tf_op jit(solution)/shard_map/ppermute | solution.py:581
  44.2 0.2 collective-permute-done.3
  44.4 1.1 %dynamic-slice_add_fusion.2 = (f32[416,128]{1,0:T(8,128)S(1)}, f32[416,128]{1,0:T(8,128)S(1)}) fusion(f32[832,128]{1,0:T(8,128)} %collective-permute-done.3, s32[]{:T(128)S(6)} %select_n.37, f32[832,128]{1,0:T(8,128)S(1)} %get-tuple-element.51, s32[]{:T(128)S(6)} %select_n.35), kind=kLoop, calls=%fused_computation.3 | loop fusion | flops 106496 | bytes 1277960 | tf_op jit(solution)/shard_map/add | solution.py:367
  45.5 0.0 collective-permute-done.2
  45.5 1.2 %dynamic-slice_add_fusion.1 = (f32[448,128]{1,0:T(8,128)S(1)}, f32[448,128]{1,0:T(8,128)S(1)}) fusion(f32[896,128]{1,0:T(8,128)} %collective-permute-done.2, s32[]{:T(128)S(6)} %select_n.32, f32[896,128]{1,0:T(8,128)S(1)} %get-tuple-element.49, s32[]{:T(128)S(6)} %select_n.34), kind=kLoop, calls=%fused_computation.1 | loop fusion | flops 114688 | bytes 1376264 | tf_op jit(solution)/shard_map/add | solution.py:367
  46.7 0.6 collective-permute-start.4
  47.3 0.8 collective-permute-start.5
  48.1 0.0 collective-permute-done.6.halo_core
  48.1 1.0 %collective-permute-done.7.halo_far = f32[64,128]{1,0:T(8,128)S(1)} collective-permute-done((f32[64,128]{1,0:T(8,128)}, f32[64,128]{1,0:T(8,128)S(1)}, u32[]{:S(2)}, u32[]{:S(2)}) %collective-permute-start.7) | collective-permute-done | bytes 32800 | tf_op jit(solution)/shard_map/ppermute | solution.py:581
  49.1 6.2 %backward.1.grad_blocks = f32[1024,128]{1,0:T(8,128)S(1)} custom-call(s32[2,27]{1,0:T(2,128)S(1)} %bitcast.16, s32[2]{0:T(128)S(1)} %bitcast.18, s32[1]{0:T(128)} %bitcast.1.me_ref.me, bf16[1024,256]{1,0:T(8,128)(2,1)S(1)} %copy-done.9, bf16[1152,1152]{1,0:T(8,128)(2,1)S(1)} %weights.1.backward, f32[64,128]{1,0:T(8,128)S(1)} %collective-permute-done.6.halo_core, ...), custom_call_target="tpu_custom_call" | custom-call | flops 6499999744 | tf_op jit(solution)/shard_map/backward/pallas_call | solution.py:589
  55.3 0.9 %gather.1.rows = f32[1024,128]{1,0:T(8,128)S(1)} custom-call(f32[1024,128]{1,0:T(8,128)S(1)} %backward.1.grad_blocks, f32[64,128]{1,0:T(8,128)S(1)} %copy-done.11), custom_call_target="tpu_custom_call" | custom-call | flops 2200000000 | tf_op jit(solution)/shard_map/gather/pallas_call | solution.py:605
  56.2 0.0 collective-permute-done.5
  56.2 0.0 copy-start.15
  56.2 0.0 collective-permute-done.4
  56.3 0.3 collective-permute-start.8
  56.6 0.4 copy-done.15
  57.0 1.1 %collective-permute-start.9 = (f32[208,128]{1,0:T(8,128)S(1)}, f32[208,128]{1,0:T(8,128)S(1)}, u32[]{:S(2)}, u32[]{:S(2)}) collective-permute-start(f32[208,128]{1,0:T(8,128)S(1)} %dynamic-slice_add_fusion.5.two), channel_id=1, source_target_pairs={{0,4},{2,6},{4,0},{6,2},{8,12},{10,14},{12,8},{14,10},{16,20},{18,... | collective-permute-start | bytes 319496 | tf_op jit(solution)/shard_map/ppermute | solution.py:576
  58.2 3.7 %all-to-all-start.1 = ((f32[16,64,128]{2,1,0:T(8,128)}), f32[16,64,128]{2,1,0:T(8,128)S(1)}, u32[]{:S(2)}, u32[]{:S(2)}) async-start(f32[16,64,128]{2,1,0:T(8,128)} %bitcast.12), calls=%async_computation.1 | async-start | bytes 1048576 | tf_op jit(solution)/shard_map/all_to_all | solution.py:628
  61.9 0.0 collective-permute-done.9
  61.9 0.0 collective-permute-done.8
  62.0 1.6 %collective-permute-start.10 = (f32[432,128]{1,0:T(8,128)S(1)}, f32[432,128]{1,0:T(8,128)S(1)}, u32[]{:S(2)}, u32[]{:S(2)}) collective-permute-start(f32[432,128]{1,0:T(8,128)S(1)} %pad_maximum_fusion.kept), channel_id=1, source_target_pairs={{0,1},{1,0},{2,3},{3,2},{4,5},{5,4},{6,7},{7,6},{8,9},{9,8},{10,11... | collective-permute-start | bytes 663560 | tf_op jit(solution)/shard_map/ppermute | solution.py:576
  63.7 6.0 %collective-permute-done.10.arrived = f32[432,128]{1,0:T(8,128)S(1)} collective-permute-done((f32[432,128]{1,0:T(8,128)S(1)}, f32[432,128]{1,0:T(8,128)S(1)}, u32[]{:S(2)}, u32[]{:S(2)}) %collective-permute-start.10) | collective-permute-done | bytes 221216 | tf_op jit(solution)/shard_map/ppermute | solution.py:576
  69.7 2.7 %collective-permute-start.11 = (f32[216,128]{1,0:T(8,128)S(1)}, f32[216,128]{1,0:T(8,128)S(1)}, u32[]{:S(2)}, u32[]{:S(2)}) collective-permute-start(f32[216,128]{1,0:T(8,128)S(1)} %get-tuple-element.61), channel_id=1, source_target_pairs={{0,16},{2,18},{4,20},{6,22},{8,24},{10,26},{12,28},{14,30},{16,0},... | collective-permute-start | bytes 331784 | tf_op jit(solution)/shard_map/ppermute | solution.py:576
  72.4 4.4 %all-to-all-done.1 = f32[16,64,128]{2,1,0:T(8,128)S(1)} async-done(((f32[16,64,128]{2,1,0:T(8,128)}), f32[16,64,128]{2,1,0:T(8,128)S(1)}, u32[]{:S(2)}, u32[]{:S(2)}) %all-to-all-start.1) | async-done | bytes 524320 | tf_op jit(solution)/shard_map/all_to_all | solution.py:628
  76.8 1.4 %unpack.1 = f32[512,128]{1,0:T(8,128)} custom-call(f32[1024,128]{1,0:T(8,128)S(1)} %bitcast.11, s32[8,512]{1,0:T(8,128)S(1)} %copy-done.12), custom_call_target="tpu_custom_call" | custom-call | flops 1700000000 | tf_op jit(solution)/shard_map/unpack/pallas_call | solution.py:631
  78.2 3.6 %collective-permute-done.11 = f32[216,128]{1,0:T(8,128)S(1)} collective-permute-done((f32[216,128]{1,0:T(8,128)S(1)}, f32[216,128]{1,0:T(8,128)S(1)}, u32[]{:S(2)}, u32[]{:S(2)}) %collective-permute-start.11) | collective-permute-done | bytes 110624 | tf_op jit(solution)/shard_map/ppermute | solution.py:576
  81.8 0.7 add_multiply_fusion
  (37 shorter events, 0.2 us)
Async XLA Ops:
  3.3 22.9 %copy-start.7 = (s32[1,1,2,1]{2,3,1,0:T(1,128)S(1)}, s32[1,1,2,1]{2,3,1,0:T(1,128)}, u32[]{:S(2)}) copy-start(s32[1,1,2,1]{2,3,1,0:T(1,128)} %param.12) | copy-start | bytes 28
  3.3 22.9 %all-to-all-start = ((f32[16,72,128]{2,1,0:T(8,128)}), f32[16,72,128]{2,1,0:T(8,128)S(1)}, u32[]{:S(2)}, u32[]{:S(2)}) async-start(f32[16,72,128]{2,1,0:T(8,128)} %get-tuple-element.36), calls=%async_computation | async-start | bytes 1179648 | tf_op jit(solution)/shard_map/all_to_all | solution.py:481
  10.7 1.5 %copy-start = (f32[27,128,128]{2,1,0:T(8,128)S(1)}, f32[27,128,128]{2,1,0:T(8,128)}, u32[]{:S(2)}) copy-start(f32[27,128,128]{2,1,0:T(8,128)} %taps_in) | copy-start | bytes 5308420
  12.1 18.1 %copy-start.6 = (s32[1,2,27]{2,1,0:T(2,128)S(1)}, s32[1,2,27]{2,1,0:T(2,128)}, u32[]{:S(2)}) copy-start(s32[1,2,27]{2,1,0:T(2,128)} %param.13) | copy-start | bytes 652
  26.2 4.0 %copy-start.1 = (f32[27,128,128]{2,1,0:T(8,128)S(1)}, f32[27,128,128]{2,1,0:T(8,128)}, u32[]{:S(2)}) copy-start(f32[27,128,128]{2,1,0:T(8,128)} %taps_in) | copy-start | bytes 5308420
  27.0 8.5 %collective-permute-start = (f32[64,128]{1,0:T(8,128)S(1)}, f32[64,128]{1,0:T(8,128)S(1)}, u32[]{:S(2)}, u32[]{:S(2)}) collective-permute-start(f32[64,128]{1,0:T(8,128)S(1)} %get-tuple-element.41), channel_id=1, source_target_pairs={{0,2},{2,0},{4,6},{6,4},{8,10},{10,8},{12,14},{14,12},{16,18},{18,... | collective-permute-start | bytes 98312 | tf_op jit(solution)/shard_map/ppermute | solution.py:503
  27.1 8.4 %collective-permute-start.1 = (f32[64,128]{1,0:T(8,128)S(1)}, f32[64,128]{1,0:T(8,128)S(1)}, u32[]{:S(2)}, u32[]{:S(2)}) collective-permute-start(f32[64,128]{1,0:T(8,128)S(1)} %get-tuple-element.42), channel_id=1, source_target_pairs={{0,30},{2,4},{4,2},{6,8},{8,6},{10,12},{12,10},{14,16},{16,14},{18... | collective-permute-start | bytes 98312 | tf_op jit(solution)/shard_map/ppermute | solution.py:504
  30.2 5.2 %copy-start.3 = (f32[1,1024,128]{2,1,0:T(8,128)S(1)}, f32[1,1024,128]{2,1,0:T(8,128)}, u32[]{:S(2)}) copy-start(f32[1,1024,128]{2,1,0:T(8,128)} %param.15) | copy-start | bytes 1572868
  35.4 2.0 %copy-start.10 = (f32[64,128]{1,0:T(8,128)}, f32[64,128]{1,0:T(8,128)S(1)}, u32[]{:S(2)}) copy-start(f32[64,128]{1,0:T(8,128)S(1)} %get-tuple-element.58.codes) | copy-start | bytes 98308
  37.5 4.8 %copy-start.4 = (f32[64,128]{1,0:T(8,128)}, f32[64,128]{1,0:T(8,128)S(1)}, u32[]{:S(2)}) copy-start(f32[64,128]{1,0:T(8,128)S(1)} %get-tuple-element.57) | copy-start | bytes 98308
  37.5 4.7 %copy-start.5 = (f32[64,128]{1,0:T(8,128)}, f32[64,128]{1,0:T(8,128)S(1)}, u32[]{:S(2)}) copy-start(f32[64,128]{1,0:T(8,128)S(1)} %get-tuple-element.56) | copy-start | bytes 98308
  37.5 4.7 %copy-start.8 = (bf16[1024,256]{1,0:T(8,128)(2,1)}, bf16[1024,256]{1,0:T(8,128)(2,1)S(1)}, u32[]{:S(2)}) copy-start(bf16[1024,256]{1,0:T(8,128)(2,1)S(1)} %get-tuple-element.55.grads) | copy-start | bytes 1572868
  42.2 2.2 %collective-permute-start.3 = (f32[832,128]{1,0:T(8,128)}, f32[832,128]{1,0:T(8,128)}, u32[]{:S(2)}, u32[]{:S(2)}) collective-permute-start(f32[832,128]{1,0:T(8,128)} %get-tuple-element.52), channel_id=1, source_target_pairs={{0,2},{2,0},{4,6},{6,4},{8,10},{10,8},{12,14},{14,12},{16,18},{18,... | collective-permute-start | bytes 1277960 | tf_op jit(solution)/shard_map/ppermute | solution.py:576
  42.3 3.2 %collective-permute-start.2 = (f32[896,128]{1,0:T(8,128)}, f32[896,128]{1,0:T(8,128)}, u32[]{:S(2)}, u32[]{:S(2)}) collective-permute-start(f32[896,128]{1,0:T(8,128)} %get-tuple-element.50), channel_id=1, source_target_pairs={{0,2},{2,0},{4,6},{6,4},{8,10},{10,8},{12,14},{14,12},{16,18},{18,... | collective-permute-start | bytes 1376264 | tf_op jit(solution)/shard_map/ppermute | solution.py:576
  42.8 6.3 %copy-start.9 = (bf16[1024,256]{1,0:T(8,128)(2,1)S(1)}, bf16[1024,256]{1,0:T(8,128)(2,1)}, u32[]{:S(2)}) copy-start(bf16[1024,256]{1,0:T(8,128)(2,1)} %copy-done.8) | copy-start | bytes 1572868
  42.8 5.3 %collective-permute-start.6 = (f32[64,128]{1,0:T(8,128)}, f32[64,128]{1,0:T(8,128)S(1)}, u32[]{:S(2)}, u32[]{:S(2)}) collective-permute-start(f32[64,128]{1,0:T(8,128)} %copy-done.5), channel_id=1, source_target_pairs={{0,2},{2,0},{4,6},{6,4},{8,10},{10,8},{12,14},{14,12},{16,18},{18,... | collective-permute-start | bytes 98312 | tf_op jit(solution)/shard_map/ppermute | solution.py:582
  42.9 6.2 %collective-permute-start.7 = (f32[64,128]{1,0:T(8,128)}, f32[64,128]{1,0:T(8,128)S(1)}, u32[]{:S(2)}, u32[]{:S(2)}) collective-permute-start(f32[64,128]{1,0:T(8,128)} %copy-done.4), channel_id=1, source_target_pairs={{0,30},{2,4},{4,2},{6,8},{8,6},{10,12},{12,10},{14,16},{16,14},{18... | collective-permute-start | bytes 98312 | tf_op jit(solution)/shard_map/ppermute | solution.py:581
  45.5 11.1 %copy-start.13 = (f32[416,128]{1,0:T(8,128)}, f32[416,128]{1,0:T(8,128)S(1)}, u32[]{:S(2)}) copy-start(f32[416,128]{1,0:T(8,128)S(1)} %get-tuple-element.69) | copy-start | bytes 638980
  46.7 8.6 %copy-start.11 = (f32[64,128]{1,0:T(8,128)S(1)}, f32[64,128]{1,0:T(8,128)}, u32[]{:S(2)}) copy-start(f32[64,128]{1,0:T(8,128)} %copy-done.10) | copy-start | bytes 98308
  46.7 9.5 %collective-permute-start.4 = (f32[448,128]{1,0:T(8,128)S(1)}, f32[448,128]{1,0:T(8,128)S(1)}, u32[]{:S(2)}, u32[]{:S(2)}) collective-permute-start(f32[448,128]{1,0:T(8,128)S(1)} %get-tuple-element.53), channel_id=1, source_target_pairs={{0,4},{2,6},{4,0},{6,2},{8,12},{10,14},{12,8},{14,10},{16,20},{18,... | collective-permute-start | bytes 688136 | tf_op jit(solution)/shard_map/ppermute | solution.py:576
  47.3 8.9 %collective-permute-start.5 = (f32[416,128]{1,0:T(8,128)S(1)}, f32[416,128]{1,0:T(8,128)S(1)}, u32[]{:S(2)}, u32[]{:S(2)}) collective-permute-start(f32[416,128]{1,0:T(8,128)S(1)} %get-tuple-element.54), channel_id=1, source_target_pairs={{0,8},{2,10},{4,12},{6,14},{8,0},{10,2},{12,4},{14,6},{16,24},{18,... | collective-permute-start | bytes 638984 | tf_op jit(solution)/shard_map/ppermute | solution.py:576
  56.2 1.9 %copy-start.2 = (f32[1024,128]{1,0:T(8,128)}, f32[1024,128]{1,0:T(8,128)S(1)}, u32[]{:S(2)}) copy-start(f32[1024,128]{1,0:T(8,128)S(1)} %gather.1.rows) | copy-start | bytes 1572868
  56.2 0.8 copy-start.15
  56.3 1.9 %copy-start.17 = (f32[224,128]{1,0:T(8,128)}, f32[224,128]{1,0:T(8,128)S(1)}, u32[]{:S(2)}) copy-start(f32[224,128]{1,0:T(8,128)S(1)} %dynamic-slice_add_fusion.4.one) | copy-start | bytes 344068
  56.3 5.7 %collective-permute-start.8 = (f32[224,128]{1,0:T(8,128)S(1)}, f32[224,128]{1,0:T(8,128)S(1)}, u32[]{:S(2)}, u32[]{:S(2)}) collective-permute-start(f32[224,128]{1,0:T(8,128)S(1)} %dynamic-slice_add_fusion.4.one), channel_id=1, source_target_pairs={{0,8},{2,10},{4,12},{6,14},{8,0},{10,2},{12,4},{14,6},{16,24},{18,... | collective-permute-start | bytes 344072 | tf_op jit(solution)/shard_map/ppermute | solution.py:576
  57.0 1.1 %copy-start.18 = (f32[208,128]{1,0:T(8,128)}, f32[208,128]{1,0:T(8,128)S(1)}, u32[]{:S(2)}) copy-start(f32[208,128]{1,0:T(8,128)S(1)} %dynamic-slice_add_fusion.5.two) | copy-start | bytes 319492
  57.0 4.9 %copy-start.14 = (f32[416,128]{1,0:T(8,128)S(1)}, f32[416,128]{1,0:T(8,128)}, u32[]{:S(2)}) copy-start(f32[416,128]{1,0:T(8,128)} %copy-done.13) | copy-start | bytes 638980
  57.0 4.9 %collective-permute-start.9 = (f32[208,128]{1,0:T(8,128)S(1)}, f32[208,128]{1,0:T(8,128)S(1)}, u32[]{:S(2)}, u32[]{:S(2)}) collective-permute-start(f32[208,128]{1,0:T(8,128)S(1)} %dynamic-slice_add_fusion.5.two), channel_id=1, source_target_pairs={{0,4},{2,6},{4,0},{6,2},{8,12},{10,14},{12,8},{14,10},{16,20},{18,... | collective-permute-start | bytes 319496 | tf_op jit(solution)/shard_map/ppermute | solution.py:576
  58.1 3.8 %copy-start.16 = (f32[416,128]{1,0:T(8,128)S(1)}, f32[416,128]{1,0:T(8,128)}, u32[]{:S(2)}) copy-start(f32[416,128]{1,0:T(8,128)} %copy-done.15) | copy-start | bytes 638980
  58.2 18.6 %all-to-all-start.1 = ((f32[16,64,128]{2,1,0:T(8,128)}), f32[16,64,128]{2,1,0:T(8,128)S(1)}, u32[]{:S(2)}, u32[]{:S(2)}) async-start(f32[16,64,128]{2,1,0:T(8,128)} %bitcast.12), calls=%async_computation.1 | async-start | bytes 1048576 | tf_op jit(solution)/shard_map/all_to_all | solution.py:628
  62.0 7.7 %collective-permute-start.10 = (f32[432,128]{1,0:T(8,128)S(1)}, f32[432,128]{1,0:T(8,128)S(1)}, u32[]{:S(2)}, u32[]{:S(2)}) collective-permute-start(f32[432,128]{1,0:T(8,128)S(1)} %pad_maximum_fusion.kept), channel_id=1, source_target_pairs={{0,1},{1,0},{2,3},{3,2},{4,5},{5,4},{6,7},{7,6},{8,9},{9,8},{10,11... | collective-permute-start | bytes 663560 | tf_op jit(solution)/shard_map/ppermute | solution.py:576
  69.7 7.1 %copy-start.12 = (s32[8,512]{1,0:T(8,128)S(1)}, s32[8,512]{1,0:T(8,128)}, u32[]{:S(2)}) copy-start(s32[8,512]{1,0:T(8,128)} %get-tuple-element.63.dest) | copy-start | bytes 49156
  69.7 12.1 %collective-permute-start.11 = (f32[216,128]{1,0:T(8,128)S(1)}, f32[216,128]{1,0:T(8,128)S(1)}, u32[]{:S(2)}, u32[]{:S(2)}) collective-permute-start(f32[216,128]{1,0:T(8,128)S(1)} %get-tuple-element.61), channel_id=1, source_target_pairs={{0,16},{2,18},{4,20},{6,22},{8,24},{10,26},{12,28},{14,30},{16,0},... | collective-permute-start | bytes 331784 | tf_op jit(solution)/shard_map/ppermute | solution.py:576
